TPU v7x, 32 devices: a whole 2x2x4 slice. The times are simulated.
32 devices in a mesh: expert: 8 (over z, y), wshard: 4 (over x, core).
Axes of the slice: x: 2, y: 2, z: 4, core: 2. Of those that a mesh axis runs over, the one named last changes fastest.
Arguments:
- tokens: bfloat16 [4096, 768], P(('expert', 'wshard')), may hold values from -6 to 6
- segments: int32 [8, 512], P('expert'), may hold values from 0 to 2, as said below
- routes: int32 [4096, 2], P(('expert', 'wshard')), may hold values from 0 to 7, all different within a row; in each aligned block of 128 rows (0 to 127, 128 to 255, ...) at most 96 rows name the same one
- blocks: int32 [8], P('expert'), may hold values from 1 to 2, as said below
- attention_gain: bfloat16 [768], P('wshard'), may hold values from 0.099609375 to 1.8984375
- query_weight: bfloat16 [768, 768], P('wshard'), may hold values from -0.21875 to 0.21875
- key_weight: bfloat16 [768, 768], P('wshard'), may hold values from -0.21875 to 0.21875
- value_weight: bfloat16 [768, 768], P('wshard'), may hold values from -0.21875 to 0.21875
- output_weight: bfloat16 [768, 768], P('wshard'), may hold values from -0.875 to 0.875
- position_bias: bfloat16 [32, 12], P('wshard'), may hold values from -4 to 4
- feed_gain: bfloat16 [768], P('wshard'), may hold values from 0.099609375 to 1.8984375
- router_weight: bfloat16 [768, 8], P('wshard'), may hold values from -0.15625 to 0.15625
- expert_in: bfloat16 [8, 3072, 768], P('expert', 'wshard'), may hold values from -0.21875 to 0.21875
- expert_out: bfloat16 [8, 3072, 768], P('expert', 'wshard'), may hold values from -0.15625 to 0.15625
- cotangent: bfloat16 [4096, 768], P(('expert', 'wshard')), may hold values from -6 to 6
Outputs:
- layer_out: bfloat16 [4096, 768], P(('expert', 'wshard'))
- tokens_grad: float32 [4096, 768], P(('expert', 'wshard'))
- attention_gain_grad: float32 [768], P('wshard')
- query_projection_gradient: float32 [768, 768], P('wshard')
- key_weight_grad: float32 [768, 768], P('wshard')
- value_weight_grad: float32 [768, 768], P('wshard')
- output_weight_grad: float32 [768, 768], P('wshard')
- position_bias_grad: float32 [32, 12], P('wshard')
- feed_gain_grad: float32 [768], P('wshard')
- router_weight_grad: float32 [768, 8], P('wshard')
- expert_in_grad: float32 [8, 3072, 768], P('expert', 'wshard')
- expert_out_grad: float32 [8, 3072, 768], P('expert', 'wshard')
Inputs may be any that keep to these rules, and one draw needn't show every extreme that they name: `segments`: along each sequence the numbers 0, 1, 2 never fall; document 1 begins within the first 128 positions and ends within the last 128. `routes`: the two experts of a row differ; in each aligned block of 128 rows (the rows of one device) no expert is named by more than 96 rows, a bound that some block reaches. `blocks`: blocks of 128 rows that an expert takes from each quarter of the tokens; some expert has 2.
All inputs are finite; a program needn't handle non-finite values.
Results may differ from a plain program's by a relative error of at most 0.013.
Values may be sent and summed in bfloat16 or wider, within the bound.
No kernel may reach another device: no remote copies, remote signals or barrier semaphores. Data moves between devices by JAX's collectives and lax.ppermute only.
A program may use at most 128 MiB of HBM per device.

v0:
```python
import math

import jax
import jax.numpy as jnp
from jax import lax
from jax.experimental import pallas as pl
from jax.experimental.pallas import tpu as pltpu
from jax.sharding import PartitionSpec as P

HEADS = 12
HEAD_DIM = 64
BUCKETS = 32
BLOCK = 128
MOST_BLOCKS = 2
SHARDS = 4
LANES = 128
CAP = MOST_BLOCKS * BLOCK
W = "wshard"
E = "expert"

epsilon = 1e-06
thresholds = tuple((math.ceil(16 * 2 ** (3 * order / 16)) for order in range(1, 16)))
low = jnp.bfloat16
wide = jnp.float32
FULL = 60 << 20


def bucket_of(distance):
    passed = jnp.zeros_like(distance)
    for edge in thresholds:
        passed = passed + (distance >= edge).astype(jnp.int32)
    return jnp.where(distance < 16, distance, 16 + passed)


def along_last(left, right):
    return lax.dot_general(left, right, (((1,), (1,)), ((), ())), preferred_element_type=wide)


def along_first(left, right):
    return lax.dot_general(left, right, (((0,), (0,)), ((), ())), preferred_element_type=wide)


def matmul(left, right):
    return jnp.dot(left, right, preferred_element_type=wide)


def swap(value, axis, step):
    count = lax.axis_size(axis)
    return lax.ppermute(value, axis, [(i, i ^ step) for i in range(count)])


def gather_w(value):
    far = swap(value, W, 2)
    near = swap(value, W, 1)
    return [value, near, far, swap(far, W, 1)]


def sum_w(parts):
    a3 = swap(parts[3], W, 1)
    a1 = swap(parts[1], W, 1)
    across = (parts[2].astype(wide) + a3.astype(wide)).astype(low)
    return [parts[0], a1, swap(across, W, 2)]


def exchange_w(parts):
    return [parts[0]] + [swap(parts[s], W, s) for s in (1, 2, 3)]


def place(parts, me):
    out = jnp.zeros((len(parts),) + parts[0].shape, parts[0].dtype)
    for s, part in enumerate(parts):
        out = lax.dynamic_update_index_in_dim(out, part, me ^ s, 0)
    return out


def gather_e(value):
    count = lax.axis_size(E)
    if count > 8:
        whole = lax.all_gather(value, E, axis=0)
        me = lax.axis_index(E)
        order = me ^ jnp.arange(count, dtype=jnp.int32)
        whole = whole[order]
        return [whole[s] for s in range(count)]
    out = {0: value}
    for s in (4, 6, 2):
        out[s] = swap(value, E, s)
    for s in (0, 4, 6, 2):
        out[s ^ 1] = swap(out[s], E, 1)
    return [out[s] for s in range(8)]


def sum_e_late(parts, pairs):
    got = [swap(pair, E, 1) for pair in pairs]
    terms = []
    for s, other in ((4, got[0][0]), (6, got[0][1]), (2, got[1][0])):
        terms.append(swap((parts[s].astype(wide) + other.astype(wide)).astype(low), E, s))
    return [parts[0], got[1][1]] + terms


def sum_e(parts):
    count = lax.axis_size(E)
    if count > 8:
        me = lax.axis_index(E)
        whole = jnp.stack(parts)[me ^ jnp.arange(count, dtype=jnp.int32)]
        return [lax.psum_scatter(whole, E, scatter_dimension=0)], whole
    got = {s: swap(parts[s ^ 1], E, 1) for s in (4, 6, 2, 0)}
    terms = [parts[0], got[0]]
    for s in (4, 6, 2):
        part = (parts[s].astype(wide) + got[s].astype(wide)).astype(low)
        terms.append(swap(part, E, s))
    return terms, part


def experts_of(small_rows):
    return {32: 8, 80: 64}[small_rows]


def total_of(refs):
    out = refs[0][...].astype(wide)
    for ref in refs[1:]:
        out = out + ref[...].astype(wide)
    return out


def call(kernel, outs, scratch, cost, scalars, *args, after=(), room=None):
    outs, scratch, after = tuple(outs), tuple(scratch), tuple(after)
    smem = pl.BlockSpec(memory_space=pltpu.SMEM)
    block = pl.BlockSpec()
    apart = pl.BlockSpec(memory_space=pl.ANY)
    size = sum(a.size * a.dtype.itemsize for a in args)
    size = size + sum(math.prod(s) * jnp.dtype(d).itemsize for s, d in outs + scratch)
    skip = len(after)
    return pl.pallas_call(
        lambda *refs: kernel(*refs[skip:]),
        out_shape=tuple(jax.ShapeDtypeStruct(s, d) for s, d in outs),
        in_specs=[apart] * skip + [smem] + [block] * len(args),
        out_specs=tuple(block for _ in outs),
        scratch_shapes=[pltpu.VMEM(s, d) for s, d in scratch],
        compiler_params=pltpu.CompilerParams(vmem_limit_bytes=room or (10 << 20) + size),
        cost_estimate=pl.CostEstimate(flops=cost[0], bytes_accessed=cost[1], transcendentals=cost[2]),
    )(*after, scalars, *args)


def start_kernel(me_ref, q_ref, k_ref, v_ref, router_ref, one_ref, two_ref, table_ref, up_ref, routes_ref, *rest):
    outs, sent_ref, held = rest[:SHARDS], rest[SHARDS], rest[SHARDS + 1]
    shard = q_ref.shape[0]
    rows = up_ref.shape[0]
    for w in range(SHARDS):
        here = slice(w * shard, (w + 1) * shard)
        held[w] = jnp.concatenate([q_ref[:, here], k_ref[:, here], v_ref[:, here]], axis=1)
    i = lax.broadcasted_iota(jnp.int32, (shard, shard), 0)
    j = lax.broadcasted_iota(jnp.int32, (shard, shard), 1)
    eye = (i == j).astype(low)
    small = [
        router_ref[...],
        one_ref[...].reshape(1, shard),
        two_ref[...].reshape(1, shard),
        along_first(table_ref[...], eye[: table_ref.shape[0]]).astype(low),
    ]
    used = sum(piece.shape[0] for piece in small)
    small = jnp.concatenate(small + [jnp.zeros((outs[0].shape[0] - shard - used, shard), low)], axis=0)
    small = jnp.concatenate([small, jnp.zeros((small.shape[0], 2 * shard), low)], axis=1)
    for s in range(SHARDS):
        outs[s][:shard, :] = held[me_ref[0] ^ s]
        outs[s][shard:, :] = small
    sent_ref[:rows, :] = up_ref[...]
    named = jnp.concatenate([routes_ref[...].astype(low), jnp.zeros((14, rows), low)], axis=0)
    sent_ref[rows:, :] = jnp.concatenate([named, jnp.zeros((16, up_ref.shape[1] - rows), low)], axis=1)


def attend_kernel(me_ref, *refs):
    tokens, weights = refs[:SHARDS], refs[SHARDS : 2 * SHARDS]
    row_ref, column_ref, out_ref = refs[2 * SHARDS : 2 * SHARDS + 3]
    rest = refs[2 * SHARDS + 3 :]
    tokens_ref, first_ref, qkv_ref, probs_ref, att_ref, weight_ref, small_ref, router_ref = rest[:8]
    branches, held_w, held_b = rest[8 : 8 + SHARDS], rest[8 + SHARDS], rest[9 + SHARDS]
    me = me_ref[0]
    shard = out_ref.shape[0]
    chunk, width = tokens[0].shape
    length = chunk * SHARDS
    heads = probs_ref.shape[0]
    span = heads * HEAD_DIM
    for s in range(SHARDS):
        tokens_ref[me ^ s] = tokens[s][...]
        held_w[me ^ s] = weights[s][...]
    for w in range(SHARDS):
        weight_ref[w * shard : (w + 1) * shard, :] = held_w[w, :shard, :]
    small = jnp.concatenate([held_w[w, shard:, :shard] for w in range(SHARDS)], axis=1)
    small_ref[...] = small
    experts = experts_of(small_ref.shape[0])
    router_ref[...] = jnp.zeros_like(router_ref)
    router_ref[:experts, :] = small[:experts]
    gain_one = small[experts : experts + 1].astype(wide)

    shift = lax.broadcasted_iota(jnp.int32, (length, width), 0)
    lane = lax.broadcasted_iota(jnp.int32, (length, width), 1)
    bucket = bucket_of(jnp.where(shift > 0, length - shift, 0))
    per = BUCKETS // SHARDS
    hits = (lane == (bucket // per) * shard + bucket % per).astype(low)
    vectors = along_last(small[experts + 2 : experts + 2 + HEADS], hits)
    i = lax.broadcasted_iota(jnp.int32, (length, length), 0)
    j = lax.broadcasted_iota(jnp.int32, (length, length), 1)
    allowed = (j <= i) & (row_ref[...] == column_ref[...])
    which = lax.broadcasted_iota(jnp.int32, vectors.shape, 0)

    rows = tokens_ref[...].reshape(length, width).astype(wide)
    scale = lax.rsqrt(jnp.mean(rows * rows, axis=-1, keepdims=True) + epsilon)
    first = (rows * scale * gain_one).astype(low)
    first_ref[...] = first
    qkv = matmul(first, weight_ref[...]).astype(low)
    qkv_ref[...] = qkv
    columns = []
    for h in range(heads):
        vector = jnp.sum(jnp.where(which == me * heads + h, vectors, 0.0), axis=0, keepdims=True)
        bias = pltpu.roll(jnp.broadcast_to(vector, (length, length)), 0, 1, stride=1, stride_axis=0)
        bias = jnp.where(allowed, bias, -1e30)
        q = qkv[:, h * HEAD_DIM : (h + 1) * HEAD_DIM] * (HEAD_DIM**-0.5)
        k = qkv[:, span + h * HEAD_DIM : span + (h + 1) * HEAD_DIM]
        v = qkv[:, 2 * span + h * HEAD_DIM : 2 * span + (h + 1) * HEAD_DIM]
        pieces = []
        for b in range(SHARDS):
            end = (b + 1) * chunk
            here = slice(b * chunk, end)
            scores = along_last(q[here], k[:end]) + bias[here, :end]
            largest = jnp.max(scores, axis=-1, keepdims=True)
            grown = jnp.exp(scores - largest)
            total = jnp.sum(grown, axis=-1, keepdims=True)
            probs = (grown / total).astype(low)
            probs_ref[h, here, :end] = probs
            if end < length:
                probs_ref[h, here, end:] = jnp.zeros((chunk, length - end), low)
            pieces.append(matmul(probs, v[:end]))
        columns.append(jnp.concatenate(pieces, axis=0))
    attended = jnp.concatenate(columns, axis=1).astype(low)
    att_ref[...] = attended
    branch = matmul(attended, out_ref[...]).astype(low)
    for w in range(SHARDS):
        held_b[w] = branch[w * chunk : (w + 1) * chunk]
    for s in range(SHARDS):
        branches[s][...] = held_b[me ^ s]


def second_kernel(me_ref, tokens_ref, small_ref, *refs):
    terms, (resid_ref, second_ref) = refs[:-2], refs[-2:]
    experts = experts_of(small_ref.shape[0])
    gain = small_ref[experts + 1 : experts + 2, :].astype(wide)
    resid = tokens_ref[...].astype(wide) + total_of(terms)
    resid_ref[...] = resid
    scale = lax.rsqrt(jnp.mean(resid * resid, axis=-1, keepdims=True) + epsilon)
    second_ref[...] = (resid * scale * gain).astype(low)


def route_kernel(me_ref, *refs):
    me, limit = me_ref[1], me_ref[2].astype(wide)
    mine = me.astype(wide)
    sent, (dispatch_ref, rows_ref) = refs[:-2], refs[-2:]
    count = len(sent)
    tall = sent[0].shape[0] - 16
    hits, others = [], []
    for s in range(count):
        named = sent[s][tall:, :tall].astype(wide)
        r0, r1 = named[0:1], named[1:2]
        hits.append(((r0 == mine) | (r1 == mine)).astype(wide))
        others.append(jnp.where(r0 == mine, r1, r0))
    hits = jnp.concatenate(hits, axis=0)
    i = lax.broadcasted_iota(jnp.int32, (tall, tall), 0)
    j = lax.broadcasted_iota(jnp.int32, (tall, tall), 1)
    within = matmul(hits.astype(low), (i < j).astype(low))
    counts = jnp.sum(hits, axis=1, keepdims=True)
    index = me ^ lax.broadcasted_iota(jnp.int32, (count, 1), 0)
    slots = lax.broadcasted_iota(jnp.int32, (CAP, tall), 0).astype(wide)
    packed = jnp.zeros((CAP, rows_ref.shape[1]), wide)
    other = jnp.zeros((16, CAP), wide)
    for s in range(count):
        base = jnp.sum(jnp.where(index < (me ^ s), counts, 0.0), axis=0, keepdims=True)
        rank = within[s : s + 1] + base
        slot = jnp.where((hits[s : s + 1] > 0) & (rank < limit), rank, -1.0)
        one_hot = (slots == slot).astype(low)
        dispatch_ref[:, s * tall : (s + 1) * tall] = one_hot
        packed = packed + matmul(one_hot, sent[s][:tall, :])
        other = other + along_last(jnp.broadcast_to(others[s], (16, tall)).astype(low), one_hot)
    rows_ref[:CAP, :] = packed.astype(low)
    tail = jnp.zeros((16, rows_ref.shape[1] - CAP), low)
    rows_ref[CAP:, :] = jnp.concatenate([other.astype(low), tail], axis=1)


def upstream_kernel(me_ref, weight_ref, *refs):
    rows, backs, choices = refs[:SHARDS], refs[SHARDS : 2 * SHARDS], refs[2 * SHARDS :]
    mine = me_ref[1].astype(wide)
    i = lax.broadcasted_iota(jnp.int32, (CAP, CAP), 0)
    j = lax.broadcasted_iota(jnp.int32, (CAP, CAP), 1)
    lane = lax.broadcasted_iota(jnp.int32, (CAP, LANES), 1).astype(wide)
    for k in range(SHARDS):
        backs[k][...] = along_last(rows[k][:CAP, :], weight_ref[...])
        across = rows[k][CAP:, :CAP].astype(wide)[0:1]
        other = jnp.sum(jnp.where(i == j, across, 0.0), axis=1, keepdims=True)
        choices[k][...] = (lane == mine).astype(wide) - (lane == other).astype(wide)


def pack_kernel(me_ref, dispatch_ref, *refs):
    rows, out_ref = refs[:-1], refs[-1]
    tall = rows[0].shape[0]
    total = jnp.zeros(out_ref.shape, wide)
    for s, ref in enumerate(rows):
        total = total + matmul(dispatch_ref[:, s * tall : (s + 1) * tall], ref[...])
    out_ref[...] = total.astype(low)


def expert_kernel(me_ref, back_a, back_b, choice_a, choice_b, weight_ref, router_ref, *refs):
    rows, outs, (act_ref, back_pre_ref, logits_ref) = refs[:2], refs[2:4], refs[4:]
    for k in range(2):
        here = slice(k * CAP, (k + 1) * CAP)
        block = rows[k][...]
        choice = (choice_a, choice_b)[k][...]
        back = (back_a, back_b)[k][...]
        chosen = jnp.sum(along_last(block, router_ref[...]) * choice, axis=1, keepdims=True)
        gate = jax.nn.sigmoid(chosen)
        pre = along_last(block, weight_ref[...])
        square = pre * pre
        slope = math.sqrt(2 / math.pi)
        bent = jnp.tanh(slope * pre * (1.0 + 0.044715 * square))
        half = 0.5 * (1.0 + bent)
        act = pre * half
        steep = half + 0.5 * pre * (1.0 - bent * bent) * (slope * (1.0 + 3 * 0.044715 * square))
        act_ref[here, :] = (act * gate).astype(low)
        back_pre = (steep * (back * gate)).astype(low)
        back_pre_ref[here, :] = back_pre
        back_gate = jnp.sum(act * back, axis=1, keepdims=True)
        logits = (gate * jax.nn.sigmoid(-chosen) * back_gate * choice).astype(low)
        logits_ref[here, :] = logits
        outs[k][...] = (matmul(back_pre, weight_ref[...]) + matmul(logits, router_ref[...])).astype(low)


def result_kernel(order, me_ref, weight_ref, act_a, act_b, logits_a, logits_b, *refs):
    rows, outs, router_ref = refs[:SHARDS], refs[SHARDS:-1], refs[-1]
    router = jnp.zeros(router_ref.shape, wide)
    for k, s in enumerate(order):
        here = slice((k % 2) * CAP, (k % 2 + 1) * CAP)
        outs[s][...] = matmul((act_a, act_b)[k // 2][here, :], weight_ref[...]).astype(low)
        router = router + along_first(rows[s][...], (logits_a, logits_b)[k // 2][here, :])
    router_ref[...] = router


def unpack_late_kernel(me_ref, dispatch_ref, *refs):
    terms, outs, pairs = refs[:3], refs[3:-2], refs[-2:]
    block = total_of(terms).astype(low)
    tall = outs[0].shape[0]
    for k, s in enumerate((4, 6, 2, 0)):
        outs[s // 2][...] = along_first(dispatch_ref[:, s * tall : (s + 1) * tall], block).astype(low)
        other = dispatch_ref[:, (s + 1) * tall : (s + 2) * tall]
        pairs[k // 2][k % 2] = along_first(other, block).astype(low)


def layer_kernel(me_ref, resid_ref, *refs):
    refs[-1][...] = (resid_ref[...] + total_of(refs[:-1])).astype(low)


def grads_kernel(order, me_ref, *refs):
    acts, pres = refs[0:2], refs[2:4]
    rows, ups = refs[4 : 4 + SHARDS], refs[4 + SHARDS : 4 + 2 * SHARDS]
    first_ref, second_ref = refs[4 + 2 * SHARDS :]
    acts = jnp.concatenate([ref[...] for ref in acts], axis=0)
    pres = jnp.concatenate([ref[...] for ref in pres], axis=0)
    block = jnp.concatenate([rows[s][...] for s in order], axis=0)
    first_ref[0] = along_first(pres, block)
    ups = jnp.concatenate([ups[s][:CAP, :] for s in order], axis=0)
    second_ref[0] = along_first(acts, ups)


def unpack_kernel(me_ref, dispatch_ref, *refs):
    terms, outs = refs[:3], refs[3:]
    block = total_of(terms).astype(low)
    tall = outs[0].shape[0]
    for s, ref in enumerate(outs):
        ref[...] = along_first(dispatch_ref[:, s * tall : (s + 1) * tall], block).astype(low)


def resid_back_kernel(me_ref, resid_ref, small_ref, cotangent_ref, *refs):
    terms, (back_ref, branch_ref, gain_ref) = refs[:-3], refs[-3:]
    experts = experts_of(small_ref.shape[0])
    gain = small_ref[experts + 1 : experts + 2, :].astype(wide)
    resid = resid_ref[...]
    upstream = total_of(terms)
    r = lax.rsqrt(jnp.mean(resid * resid, axis=-1, keepdims=True) + epsilon)
    gain_ref[...] = jnp.sum(upstream * (resid * r), axis=0, keepdims=True)
    m = upstream * gain
    back = r * m - (r * r * r) * resid * jnp.mean(m * resid, axis=-1, keepdims=True)
    back = back + cotangent_ref[...].astype(wide)
    back_ref[...] = back
    branch_ref[...] = back.astype(low)


def attend_back_kernel(
    experts,
    table_rows,
    me_ref,
    out_ref,
    qkv_ref,
    probs_ref,
    weight_ref,
    tokens_ref,
    first_ref,
    att_ref,
    gain_two_ref,
    router_ref,
    *refs,
):
    ups, backs = refs[:SHARDS], refs[SHARDS : 2 * SHARDS]
    parts, (held, table) = refs[2 * SHARDS : -2], refs[-2:]
    me = me_ref[0]
    shard = out_ref.shape[0]
    chunk, width = ups[0].shape
    length = chunk * SHARDS
    heads = probs_ref.shape[0]
    span = heads * HEAD_DIM
    scale = HEAD_DIM**-0.5
    for s in range(SHARDS):
        held[me ^ s] = ups[s][...]
    up = held[...].reshape(length, width)
    back = along_last(up, out_ref[...]).astype(low)
    qkv = qkv_ref[...]
    dq, dk, dv = [], [], []
    i = lax.broadcasted_iota(jnp.int32, (chunk, chunk), 0)
    j = lax.broadcasted_iota(jnp.int32, (chunk, chunk), 1)
    reverse = (i + j == chunk - 1).astype(low)
    diagonals = []
    for h in range(heads):
        q = qkv[:, h * HEAD_DIM : (h + 1) * HEAD_DIM]
        k = qkv[:, span + h * HEAD_DIM : span + (h + 1) * HEAD_DIM]
        v = qkv[:, 2 * span + h * HEAD_DIM : 2 * span + (h + 1) * HEAD_DIM]
        d = back[:, h * HEAD_DIM : (h + 1) * HEAD_DIM]
        probs_low = probs_ref[h]
        probs = probs_low.astype(wide)
        back_probs = along_last(d, v)
        inner = jnp.sum(back_probs * probs, axis=-1, keepdims=True)
        scores = (probs * (back_probs - inner)).astype(low)
        diagonal = jnp.zeros((1, length), wide)
        for b in range(SHARDS):
            turned = matmul(reverse, scores[b * chunk : (b + 1) * chunk])
            start = (1 - (b + 1) * chunk) % length
            turned = pltpu.roll(turned, start, 1, stride=1, stride_axis=0)
            diagonal = diagonal + jnp.sum(turned, axis=0, keepdims=True)
        diagonals.append(diagonal)
        dq.append((matmul(scores, k) * scale).astype(low))
        dk.append((along_first(scores, q) * scale).astype(low))
        dv.append(along_first(probs_low, d).astype(low))
    dqkv = jnp.concatenate(dq + dk + dv, axis=1)
    back_first = along_last(dqkv, weight_ref[...])
    rows = tokens_ref[...].reshape(length, width).astype(wide)
    rows = rows * lax.rsqrt(jnp.mean(rows * rows, axis=-1, keepdims=True) + epsilon)
    for w in range(SHARDS):
        held[w] = back_first[w * chunk : (w + 1) * chunk].astype(low)
    for s in range(SHARDS):
        backs[s][...] = held[me ^ s]

    gains = [jnp.sum(back_first * rows, axis=0, keepdims=True), gain_two_ref[...]]
    gains = jnp.concatenate(gains + [jnp.zeros((14, width), wide)], axis=0).astype(low)
    i = lax.broadcasted_iota(jnp.int32, (LANES, LANES), 0)
    j = lax.broadcasted_iota(jnp.int32, (LANES, LANES), 1)
    extra = along_first(gains, (i[:16] == j[:16]).astype(low))
    extra = extra + matmul(router_ref[...].astype(low), (i + 2 == j).astype(low))
    above = jnp.zeros((2 + experts, length), wide)
    below = jnp.zeros((LANES - 2 - experts - heads, length), wide)
    spread = jnp.concatenate([above] + diagonals + [below], axis=0)
    shift = lax.broadcasted_iota(jnp.int32, (length, width), 0)
    lane = lax.broadcasted_iota(jnp.int32, (length, width), 1)
    bucket = bucket_of(jnp.where(shift > 0, length - shift, 0))
    hits = (lane == (bucket // table_rows) * shard + bucket % table_rows).astype(low)
    spread_low = spread.astype(low)
    rest = (spread - spread_low.astype(wide)).astype(low)
    turn = (((0,), (1,)), ((), ()))
    extra = extra + lax.dot_general(hits, spread_low, turn, preferred_element_type=wide)
    extra = extra + lax.dot_general(hits, rest, turn, preferred_element_type=wide)
    output = along_first(att_ref[...], up)
    output = jnp.concatenate([output[:, w * shard : (w + 1) * shard] for w in range(SHARDS)], axis=0)
    grads = jnp.concatenate([along_first(first_ref[...], dqkv), extra, output], axis=1)
    if len(parts) == 1:
        parts[0][...] = grads.astype(low)
    else:
        table[...] = grads
        piece = parts[0].shape[1]
        for s, ref in enumerate(parts):
            for w in range(SHARDS):
                start = pl.multiple_of(w * shard + (me_ref[1] ^ s) * piece, 8)
                ref[w] = table[pl.ds(start, piece), :].astype(low)


def join_kernel(me_ref, *refs):
    terms, outs, output_ref, held = refs[:5], refs[5 : 5 + SHARDS], refs[5 + SHARDS], refs[6 + SHARDS]
    total = total_of(terms)
    columns = outs[0].shape[1]
    held[...] = total[:, :, :columns]
    for s in range(SHARDS):
        outs[s][...] = held[me_ref[0] ^ s].astype(low)
    output_ref[...] = jnp.concatenate([total[w][:, columns:] for w in range(SHARDS)], axis=1).astype(low)


def order_kernel(experts, me_ref, *refs):
    parts, output_ref, out_ref, held = refs[:SHARDS], refs[SHARDS], refs[SHARDS + 1], refs[SHARDS + 2]
    for s in range(SHARDS):
        held[me_ref[0] ^ s] = parts[s][...].astype(wide)
    own = HEADS // SHARDS
    span = own * HEAD_DIM
    blocks = [held[w] for w in range(SHARDS)]
    pieces = [blocks[w][:, k * span : (k + 1) * span] for k in range(3) for w in range(SHARDS)]
    lane = lax.broadcasted_iota(jnp.int32, (parts[0].shape[0], LANES), 1)
    extra = jnp.zeros((parts[0].shape[0], LANES), wide)
    for w in range(SHARDS):
        small = blocks[w][:, 3 * span :]
        heads = jnp.where((lane >= 2 + experts) & (lane < 2 + experts + own), small, 0.0)
        extra = extra + jnp.where(lane < 2 + experts, small, 0.0) + pltpu.roll(heads, own * w, 1)
    pieces = pieces + [output_ref[...].astype(wide), extra]
    out_ref[...] = jnp.concatenate(pieces, axis=1).astype(low)


def final_kernel(me_ref, *refs):
    parts, outs = refs[:-9], refs[-9:-1]
    held = refs[-1]
    piece = parts[0].shape[0]
    width = outs[0].shape[1]
    experts = outs[6].shape[1]
    for s, ref in enumerate(parts):
        here = pl.ds(pl.multiple_of((me_ref[1] ^ s) * piece, 8), piece)
        block = ref[...].astype(wide)
        for k in range(4):
            outs[k][here, :] = block[:, k * width : (k + 1) * width]
        held[here, :] = block[:, 4 * width :]
    extra = held[...]
    shard = extra.shape[0]
    i = lax.broadcasted_iota(jnp.int32, (shard, shard), 0)
    j = lax.broadcasted_iota(jnp.int32, (shard, shard), 1)
    turned = along_first(extra.astype(low), (i == j).astype(low))
    outs[4][...] = turned[0:1]
    outs[5][...] = turned[1:2]
    outs[6][...] = extra[:, 2 : 2 + experts]
    outs[7][...] = extra[: outs[7].shape[0], 2 + experts : 2 + experts + HEADS]


def tokens_back_kernel(me_ref, tokens_ref, small_ref, resid_ref, *refs):
    terms, out_ref = refs[:-1], refs[-1]
    experts = experts_of(small_ref.shape[0])
    gain = small_ref[experts : experts + 1, :].astype(wide)
    rows = tokens_ref[...].astype(wide)
    r = lax.rsqrt(jnp.mean(rows * rows, axis=-1, keepdims=True) + epsilon)
    m = total_of(terms) * gain
    back = r * m - (r * r * r) * rows * jnp.mean(m * rows, axis=-1, keepdims=True)
    out_ref[...] = resid_ref[...] + back


def local(
    tokens,
    segments,
    routes,
    blocks,
    attention_gain,
    query_weight,
    key_weight,
    value_weight,
    output_weight,
    position_bias,
    feed_gain,
    router_weight,
    expert_in,
    expert_out,
    cotangent,
):
    rows, width = tokens.shape
    length = rows * SHARDS
    experts = lax.axis_size(E)
    me_w = lax.axis_index(W)
    me_e = lax.axis_index(E)
    me = jnp.stack([me_w, me_e, blocks[0] * BLOCK]).astype(jnp.int32)
    shard = query_weight.shape[0]
    own_heads = HEADS // SHARDS
    table_rows = position_bias.shape[0]
    first_local, second_local = expert_in[0], expert_out[0]
    row = (rows, width)
    packed_row = (CAP, width)

    quick = experts == 8
    small_rows = -(-(experts + 2 + HEADS) // 16) * 16
    tokens_rel = gather_w(tokens)
    *weight_parts, sent = call(
        start_kernel,
        [((shard + small_rows, 3 * shard), low)] * SHARDS + [((rows + 16, width), low)],
        [((SHARDS, shard, 3 * shard), low)],
        (0, 4 * shard * width * 3, 0),
        me,
        query_weight,
        key_weight,
        value_weight,
        router_weight.T,
        attention_gain,
        feed_gain,
        position_bias,
        cotangent,
        routes.T,
        room=FULL,
    )
    weight_rel = exchange_w(weight_parts)
    sent = gather_e(sent)

    square = (own_heads, length, length)
    outs = call(
        attend_kernel,
        [
            ((SHARDS, rows, width), low),
            ((length, width), low),
            ((length, 3 * shard), low),
            (square, low),
            ((length, shard), low),
            ((width, 3 * shard), low),
            ((small_rows, width), low),
            ((LANES, width), low),
        ]
        + [(row, low)] * SHARDS,
        [((SHARDS, shard + small_rows, 3 * shard), low), ((SHARDS, rows, width), low)],
        (2 * length * width * 4 * shard, 8 * length * length * own_heads, own_heads * length * length),
        me,
        *tokens_rel,
        *weight_rel,
        segments,
        segments.reshape(length, 1),
        output_weight,
        room=FULL,
    )
    tokens_all, first, qkv, probs, attended, weight, small, router = outs[:8]
    resid, second = call(
        second_kernel,
        [(row, wide), (row, low)],
        [],
        (0, 8 * rows * width, 0),
        me,
        tokens,
        small,
        *sum_w(outs[8:]),
    )

    dispatch, upstream_rows = call(
        route_kernel,
        [((CAP, experts * rows), low), ((CAP + 16, width), low)],
        [],
        (2 * CAP * experts * rows * width, 4 * experts * rows * width, 0),
        me,
        *sent,
    )
    upstream_rel = gather_w(upstream_rows)
    order = (3, 2, 1, 0)
    outs = call(
        upstream_kernel,
        [(packed_row, wide)] * SHARDS + [((CAP, LANES), wide)] * SHARDS,
        [],
        (2 * SHARDS * CAP * width * width, 4 * SHARDS * CAP * width, 0),
        me,
        second_local,
        *[upstream_rel[s] for s in order],
    )
    back_act, choice = outs[:SHARDS], outs[SHARDS:]

    (packed,) = call(
        pack_kernel,
        [(packed_row, low)],
        [],
        (2 * CAP * experts * rows * width, 4 * experts * rows * width, 0),
        me,
        dispatch,
        *gather_e(second),
        after=(back_act[0],),
    )
    rows_rel = gather_w(packed)
    half = (2 * CAP, width)

    def expert_half(k, after):
        return call(
            expert_kernel,
            [(packed_row, low)] * 2 + [(half, low), (half, low), ((2 * CAP, LANES), low)],
            [],
            (8 * CAP * width * width, 8 * CAP * width, 2 * CAP * width),
            me,
            back_act[2 * k],
            back_act[2 * k + 1],
            choice[2 * k],
            choice[2 * k + 1],
            first_local,
            router,
            rows_rel[order[2 * k]],
            rows_rel[order[2 * k + 1]],
            after=after,
        )

    halves = [expert_half(0, ())]
    near = swap(halves[0][0], W, 1)
    across = (halves[0][1].astype(wide) + near.astype(wide)).astype(low)
    halves.append(expert_half(1, (across,)))
    far = swap(across, W, 2)
    back_parts = call(
        unpack_kernel,
        [(row, low)] * experts,
        [],
        (2 * CAP * experts * rows * width, 4 * experts * rows * width, 0),
        me,
        dispatch,
        halves[1][1],
        swap(halves[1][0], W, 1),
        far,
    )
    back_terms, tie = sum_e(back_parts)

    *results, router_grad = call(
        lambda *refs: result_kernel(order, *refs),
        [(packed_row, low)] * SHARDS + [((width, LANES), wide)],
        [],
        (8 * CAP * width * width, 8 * CAP * width, 0),
        me,
        second_local,
        halves[0][2],
        halves[1][2],
        halves[0][4],
        halves[1][4],
        *rows_rel,
        after=(back_parts[0],),
    )
    result_terms = sum_w(results)

    back_resid, back_branch, gain_two_grad = call(
        resid_back_kernel,
        [(row, wide), (row, low), ((1, width), wide)],
        [],
        (0, 16 * rows * width, 0),
        me,
        resid,
        small,
        cotangent,
        *back_terms,
    )
    back_rel = gather_w(back_branch)
    if quick:
        outs = call(
            unpack_late_kernel,
            [(row, low)] * 4 + [((2,) + row, low)] * 2,
            [],
            (2 * CAP * experts * rows * width, 4 * experts * rows * width, 0),
            me,
            dispatch,
            *result_terms,
            after=(tie,),
        )
        mixed_terms = sum_e_late(dict(zip((0, 2, 4, 6), outs[:4])), outs[4:])
    else:
        mixed_parts = call(
            unpack_kernel,
            [(row, low)] * experts,
            [],
            (2 * CAP * experts * rows * width, 4 * experts * rows * width, 0),
            me,
            dispatch,
            *result_terms,
        )
        mixed_terms, _ = sum_e(mixed_parts)
    (layer_out,) = call(
        layer_kernel, [(row, low)], [], (0, 16 * rows * width, 0), me, resid, *mixed_terms
    )
    columns = 3 * shard + LANES
    piece = shard // experts
    part = (SHARDS, piece, columns + shard)
    outs = call(
        lambda *refs: attend_back_kernel(experts, table_rows, *refs),
        [(row, low)] * SHARDS + ([(part, low)] * experts if quick else [((width, columns + shard), low)]),
        [((SHARDS, rows, width), low), ((width, columns + shard), wide)],
        (2 * length * width * 9 * shard, 8 * length * length * own_heads, 0),
        me,
        output_weight,
        qkv,
        probs,
        weight,
        tokens_all,
        first,
        attended,
        gain_two_grad,
        router_grad,
        *back_rel,
        after=(mixed_terms[0],),
    )
    grads = outs[SHARDS:]
    (tokens_grad,) = call(
        tokens_back_kernel,
        [(row, wide)],
        [],
        (0, 16 * rows * width, 0),
        me,
        tokens,
        small,
        back_resid,
        *sum_w(outs[:SHARDS]),
    )

    first_grad, second_grad = call(
        lambda *refs: grads_kernel(order, *refs),
        [((1,) + first_local.shape, wide), ((1,) + second_local.shape, wide)],
        [],
        (16 * CAP * width * width, 24 * CAP * width, 0),
        me,
        halves[0][2],
        halves[1][2],
        halves[0][3],
        halves[1][3],
        *rows_rel,
        *upstream_rel,
        after=(grads[0],),
    )

    if quick:
        terms, _ = sum_e(grads)
        *grads, output_grad = call(
            join_kernel,
            [((piece, columns), low)] * SHARDS + [((piece, width), low)],
            [((SHARDS, piece, columns), wide)],
            (0, 8 * width * columns, 0),
            me,
            *terms,
        )
        (grads,) = call(
            lambda *refs: order_kernel(experts, *refs),
            [((piece, 4 * width + LANES), low)],
            [((SHARDS, piece, columns), wide)],
            (0, 8 * width * columns, 0),
            me,
            *exchange_w(grads),
            output_grad,
        )
        shape = (shard, width)
        outs = call(
            final_kernel,
            [(shape, wide)] * 4
            + [((1, shard), wide)] * 2
            + [((shard, experts), wide), ((table_rows, HEADS), wide)],
            [((shard, LANES), wide)],
            (0, 16 * shard * width, 0),
            me,
            *gather_e(grads),
        )
        query_grad, key_grad, value_grad, output_grad = outs[:4]
        gain_one_grad, gain_two_grad = outs[4].reshape(shard), outs[5].reshape(shard)
        router_grad, table_grad = outs[6], outs[7]
    else:
        grads = lax.psum(grads[0], E).astype(wide).reshape(SHARDS, shard, columns + shard)
        output_grad = grads[:, :, columns:].transpose(1, 0, 2).reshape(shard, width)
        grads = grads[:, :, :columns].astype(low)
        grads = place(
            exchange_w([lax.dynamic_index_in_dim(grads, me_w ^ s, 0, False) for s in range(SHARDS)]), me_w
        ).astype(wide)
        main = grads[:, :, : 3 * shard].reshape(SHARDS, shard, 3, shard).transpose(2, 1, 0, 3)
        query_grad, key_grad, value_grad = main.reshape(3, shard, width)
        extra = grads[:, :, 3 * shard :]
        summed = jnp.sum(extra[:, :, : 2 + experts], axis=0)
        gain_one_grad, gain_two_grad, router_grad = summed[:, 0], summed[:, 1], summed[:, 2:]
        table_grad = extra[:, :table_rows, 2 + experts : 2 + experts + own_heads]
        table_grad = table_grad.transpose(1, 0, 2).reshape(table_rows, HEADS)
    return (
        layer_out,
        tokens_grad,
        gain_one_grad,
        query_grad,
        key_grad,
        value_grad,
        output_grad,
        table_grad,
        gain_two_grad,
        router_grad,
        first_grad,
        second_grad,
    )


def solution(mesh):
    in_specs = (
        P(("expert", "wshard"), None),
        P("expert", None),
        P(("expert", "wshard"), None),
        P("expert"),
        P("wshard"),
        P("wshard", None),
        P("wshard", None),
        P("wshard", None),
        P("wshard", None),
        P("wshard", None),
        P("wshard"),
        P("wshard", None),
        P("expert", "wshard", None),
        P("expert", "wshard", None),
        P(("expert", "wshard"), None),
    )
    out_specs = (
        P(("expert", "wshard"), None),
        P(("expert", "wshard"), None),
        P("wshard"),
        P("wshard", None),
        P("wshard", None),
        P("wshard", None),
        P("wshard", None),
        P("wshard", None),
        P("wshard"),
        P("wshard", None),
        P("expert", "wshard", None),
        P("expert", "wshard", None),
    )
    return jax.shard_map(local, mesh=mesh, in_specs=in_specs, out_specs=out_specs, check_vma=False)
```

profile of v0, /device:TPU:0, one launch (start us, length us, event | category | flops | bytes accessed | tf_op | source)
XLA Modules:
  0.0 267.7 jit_solution(16552034739020990298)
XLA Ops:
  1.2 2.6 collective-permute-start.1
  5.0 2.6 shard_map.238
  7.6 1.6 collective-permute-start.10
  9.2 2.6 collective-permute-start.12
  13.7 6.3 %collective-permute-done.10.refs_3_ = bf16[144,768]{1,0:T(8,128)(2,1)S(1)} collective-permute-done((bf16[144,768]{1,0:T(8,128)(2,1)}, bf16[144,768]{1,0:T(8,128)(2,1)S(1)}, u32[]{:S(2)}, u32[]{:S(2)}) %collective-permute-start.10) | collective-permute-done | bytes 221216 | tf_op jit(solution)/shard_map/ppermute | solution.py:49
  20.0 2.5 collective-permute-start.14
  22.5 6.3 %collective-permute-done.14.refs_7_ = bf16[144,768]{1,0:T(8,128)(2,1)S(1)} collective-permute-done((bf16[144,768]{1,0:T(8,128)(2,1)}, bf16[144,768]{1,0:T(8,128)(2,1)S(1)}, u32[]{:S(2)}, u32[]{:S(2)}) %collective-permute-start.14) | collective-permute-done | bytes 221216 | tf_op jit(solution)/shard_map/ppermute | solution.py:49
  28.7 1.5 collective-permute-start.9
  30.8 1.5 collective-permute-start.13
  32.8 1.5 copy.28.refs_10_
  35.0 8.2 %shard_map.239 = (bf16[4,128,768]{2,1,0:T(8,128)(2,1)}, bf16[512,768]{1,0:T(8,128)(2,1)}, bf16[512,576]{1,0:T(8,128)(2,1)}, bf16[3,512,512]{2,1,0:T(8,128)(2,1)}...) custom-call(s32[3]{0:T(128)} %pad_add_fusion.refs_0_.refs_1_, ...), custom_call_target="tpu_custom_call" | custom-call | flops 603979776 | bytes 6291456 | tf_op jit(solution)/shard_map/pallas_call | solution.py:133
  43.4 3.1 %collective-permute-done.13.refs_6_ = bf16[144,768]{1,0:T(8,128)(2,1)S(1)} collective-permute-done((bf16[144,768]{1,0:T(8,128)(2,1)S(1)}, bf16[144,768]{1,0:T(8,128)(2,1)S(1)}, u32[]{:S(2)}, u32[]{:S(2)}) %collective-permute-start.13) | collective-permute-done | bytes 221216 | tf_op jit(solution)/shard_map/ppermute | solution.py:49
  46.5 2.4 collective-permute-done.15.refs_8_
  48.9 1.8 shard_map.241
  53.4 8.5 %collective-permute-done.16.refs_3_.refs_12_ = bf16[272,768]{1,0:T(8,128)(2,1)S(1)} collective-permute-done((bf16[272,768]{1,0:T(8,128)(2,1)S(1)}, bf16[272,768]{1,0:T(8,128)(2,1)S(1)}, u32[]{:S(2)}, u32[]{:S(2)}) %collective-permute-start.16) | collective-permute-done | bytes 417824 | tf_op jit(solution)/shard_map/ppermute | solution.py:49
  61.9 2.1 collective-permute-done.8.refs_5_
  64.8 6.1 %collective-permute-start.20 = (bf16[128,768]{1,0:T(8,128)(2,1)S(1)}, bf16[128,768]{1,0:T(8,128)(2,1)S(1)}, u32[]{:S(2)}, u32[]{:S(2)}) collective-permute-start(bf16[128,768]{1,0:T(8,128)(2,1)S(1)} %get-tuple-element.118.refs_3_), channel_id=1, source_target_pairs={{0,8},{4,12},{8,0},{12,4},{16,24},{20,28},{24,16},{28,20},{1,9},{5... | collective-permute-start | bytes 589832 | tf_op jit(solution)/shard_map/ppermute | solution.py:49
  70.9 2.4 collective-permute-start.24
  73.3 1.5 collective-permute-start.19
  74.8 2.1 collective-permute-done.20.refs_5_
  76.9 1.5 collective-permute-start.21
  78.4 8.4 %collective-permute-done.22.refs_7_ = bf16[128,768]{1,0:T(8,128)(2,1)S(1)} collective-permute-done((bf16[128,768]{1,0:T(8,128)(2,1)S(1)}, bf16[128,768]{1,0:T(8,128)(2,1)S(1)}, u32[]{:S(2)}, u32[]{:S(2)}) %collective-permute-start.22) | collective-permute-done | bytes 196640 | tf_op jit(solution)/shard_map/ppermute | solution.py:49
  86.8 1.5 collective-permute-start.23
  88.8 2.0 shard_map.242
  90.8 1.6 collective-permute-done.23.refs_8_
  92.4 2.1 collective-permute-done.25.refs_10_
  97.4 6.5 %collective-permute-done.26.refs_8_.refs_9_ = bf16[256,768]{1,0:T(8,128)(2,1)S(1)} collective-permute-done((bf16[256,768]{1,0:T(8,128)(2,1)S(1)}, bf16[256,768]{1,0:T(8,128)(2,1)S(1)}, u32[]{:S(2)}, u32[]{:S(2)}) %collective-permute-start.26) | collective-permute-done | bytes 393248 | tf_op jit(solution)/shard_map/ppermute | solution.py:49
  103.9 1.7 collective-permute-done.27.refs_7_.refs_10_.refs_9_
  105.6 4.2 %shard_map.244 = (bf16[256,768]{1,0:T(8,128)(2,1)S(1)}, bf16[256,768]{1,0:T(8,128)(2,1)S(1)}, bf16[512,768]{1,0:T(8,128)(2,1)S(1)}, bf16[512,768]{1,0:T(8,128)(2,1)S(1)}, bf16[512,128]{1,0:T(8,128)(2,1)S(1)}) custom-call(s32[3]{0:T(128)S(1)} %copy-done.13, f32[256,768]{1,0:T(8,128)S(1)} %get-tuple-element.113.refs_0_.refs_1_, ...), custom_call_target="tpu_custom_call" | custom-call | flops 1207959552 | bytes 1572864 | tf_op jit(solution)/shard_map/pallas_call | solution.py:133
  112.1 4.0 %shard_map.245 = (bf16[256,768]{1,0:T(8,128)(2,1)S(1)}, bf16[256,768]{1,0:T(8,128)(2,1)S(1)}, bf16[512,768]{1,0:T(8,128)(2,1)S(1)}, bf16[512,768]{1,0:T(8,128)(2,1)S(1)}, bf16[512,128]{1,0:T(8,128)(2,1)S(1)}) custom-call(bf16[256,768]{1,0:T(8,128)(2,1)S(1)} %add_convert_fusion.1.refs_0_, s32[3]{0:T(128)S(1)} %copy-done.13, ...), custom_call_target="tpu_custom_call" | custom-call | flops 1207959552 | bytes 1572864 | tf_op jit(solution)/shard_map/pallas_call | solution.py:133
  117.9 9.8 %collective-permute-done.31.refs_4_ = bf16[256,768]{1,0:T(8,128)(2,1)S(1)} collective-permute-done((bf16[256,768]{1,0:T(8,128)(2,1)S(1)}, bf16[256,768]{1,0:T(8,128)(2,1)S(1)}, u32[]{:S(2)}, u32[]{:S(2)}) %collective-permute-start.31) | collective-permute-done | bytes 393248 | tf_op jit(solution)/shard_map/ppermute | solution.py:49
  129.0 1.6 collective-permute-start.42
  131.1 2.3 shard_map.247
  134.0 1.5 collective-permute-start.41
  136.9 1.5 collective-permute-start.44
  138.4 9.6 %collective-permute-done.44 = bf16[128,768]{1,0:T(8,128)(2,1)S(1)} collective-permute-done((bf16[128,768]{1,0:T(8,128)(2,1)S(1)}, bf16[128,768]{1,0:T(8,128)(2,1)S(1)}, u32[]{:S(2)}, u32[]{:S(2)}) %collective-permute-start.44) | collective-permute-done | bytes 196640 | tf_op jit(solution)/shard_map/ppermute | solution.py:49
  148.0 3.2 %collective-permute-start.43 = (bf16[128,768]{1,0:T(8,128)(2,1)S(1)}, bf16[128,768]{1,0:T(8,128)(2,1)S(1)}, u32[]{:S(2)}, u32[]{:S(2)}) collective-permute-start(bf16[128,768]{1,0:T(8,128)(2,1)S(1)} %add_convert_fusion.4), channel_id=1, source_target_pairs={{0,16},{4,20},{8,24},{12,28},{16,0},{20,4},{24,8},{28,12},{1,17},{... | collective-permute-start | bytes 589832 | tf_op jit(solution)/shard_map/ppermute | solution.py:49
  151.3 1.8 collective-permute-start.45
  153.8 11.2 %collective-permute-done.43.refs_6_ = bf16[128,768]{1,0:T(8,128)(2,1)S(1)} collective-permute-done((bf16[128,768]{1,0:T(8,128)(2,1)S(1)}, bf16[128,768]{1,0:T(8,128)(2,1)S(1)}, u32[]{:S(2)}, u32[]{:S(2)}) %collective-permute-start.43) | collective-permute-done | bytes 196640 | tf_op jit(solution)/shard_map/ppermute | solution.py:49
  166.9 4.8 %collective-permute-done.48.refs_13_ = bf16[128,768]{1,0:T(8,128)(2,1)S(1)} collective-permute-done((bf16[128,768]{1,0:T(8,128)(2,1)S(1)}, bf16[128,768]{1,0:T(8,128)(2,1)S(1)}, u32[]{:S(2)}, u32[]{:S(2)}) %collective-permute-start.48) | collective-permute-done | bytes 196640 | tf_op jit(solution)/shard_map/ppermute | solution.py:49
  173.2 6.6 %shard_map.251 = (bf16[128,768]{1,0:T(8,128)(2,1)S(1)}, bf16[128,768]{1,0:T(8,128)(2,1)S(1)}, bf16[128,768]{1,0:T(8,128)(2,1)S(1)}, bf16[128,768]{1,0:T(8,128)(2...) custom-call(bf16[128,768]{1,0:T(8,128)(2,1)S(1)} %get-tuple-element., ...), custom_call_target="tpu_custom_call" | custom-call | flops 1358954496 | bytes 6291456 | tf_op jit(solution)/shard_map/pallas_call | solution.py:133
  179.8 1.6 collective-permute-start.54
  181.9 1.5 collective-permute-start.53
  183.9 3.1 %collective-permute-done.54 = bf16[4,24,896]{2,1,0:T(8,128)(2,1)S(1)} collective-permute-done((bf16[4,24,896]{2,1,0:T(8,128)(2,1)S(1)}, bf16[4,24,896]{2,1,0:T(8,128)(2,1)S(1)}, u32[]{:S(2)}, u32[]{:S(2)}) %collective-permute-start.54) | collective-permute-done | bytes 172064 | tf_op jit(solution)/shard_map/ppermute | solution.py:49
  187.1 1.5 collective-permute-start.58
  188.7 14.2 %collective-permute-done.56 = bf16[4,24,896]{2,1,0:T(8,128)(2,1)S(1)} collective-permute-done((bf16[4,24,896]{2,1,0:T(8,128)(2,1)S(1)}, bf16[4,24,896]{2,1,0:T(8,128)(2,1)S(1)}, u32[]{:S(2)}, u32[]{:S(2)}) %collective-permute-start.56) | collective-permute-done | bytes 172064 | tf_op jit(solution)/shard_map/ppermute | solution.py:49
  202.9 3.4 %collective-permute-start.55 = (bf16[4,24,896]{2,1,0:T(8,128)(2,1)S(1)}, bf16[4,24,896]{2,1,0:T(8,128)(2,1)S(1)}, u32[]{:S(2)}, u32[]{:S(2)}) collective-permute-start(bf16[4,24,896]{2,1,0:T(8,128)(2,1)S(1)} %add_convert_fusion.9), channel_id=1, source_target_pairs={{0,16},{4,20},{8,24},{12,28},{16,0},{20,4},{24,8},{28,12},{1,17},{... | collective-permute-start | bytes 516104 | tf_op jit(solution)/shard_map/ppermute | solution.py:49
  206.4 2.1 collective-permute-start.57
  208.5 1.6 collective-permute-start.59
  210.1 4.9 %shard_map.256 = (f32[1,768,768]{2,1,0:T(8,128)}, f32[1,768,768]{2,1,0:T(8,128)}) custom-call(bf16[4,24,896]{2,1,0:T(8,128)(2,1)S(1)} %get-tuple-element.163.refs_1_.refs_0_, s32[3]{0:T(128)S(1)} %copy-done.13, bf16[512,768]{1,0:T(8,128)(2,1)S(1)} %get-tuple-element.130.refs_3_.refs_2_, bf16[512,768]{1,0:T(8,128)(2,1)S(1)} %get-tuple-element.131.refs_4_.refs_3_, ...), custom_call_target="tpu_custom_call" | custom-call | flops 2415919104 | bytes 4718592 | tf_op jit(solution)/shard_map/pallas_call | solution.py:133
  215.0 3.9 %collective-permute-done.55.refs_3_ = bf16[4,24,896]{2,1,0:T(8,128)(2,1)S(1)} collective-permute-done((bf16[4,24,896]{2,1,0:T(8,128)(2,1)S(1)}, bf16[4,24,896]{2,1,0:T(8,128)(2,1)S(1)}, u32[]{:S(2)}, u32[]{:S(2)}) %collective-permute-start.55) | collective-permute-done | bytes 172064 | tf_op jit(solution)/shard_map/ppermute | solution.py:49
  223.6 2.0 collective-permute-done.61.refs_3_
  227.4 2.1 collective-permute-start.66
  231.7 1.5 collective-permute-start.38
  233.2 1.5 shard_map.252
  234.7 1.8 collective-permute-start.39
  236.6 1.6 collective-permute-start.63
  238.2 11.7 %collective-permute-done.66.refs_5_ = bf16[24,3200]{1,0:T(8,128)(2,1)S(1)} collective-permute-done((bf16[24,3200]{1,0:T(8,128)(2,1)S(1)}, bf16[24,3200]{1,0:T(8,128)(2,1)S(1)}, u32[]{:S(2)}, u32[]{:S(2)}) %collective-permute-start.66) | collective-permute-done | bytes 153632 | tf_op jit(solution)/shard_map/ppermute | solution.py:49
  250.2 1.7 collective-permute-start.65
  251.9 5.7 %collective-permute-done.38.refs_4_ = bf16[128,768]{1,0:T(8,128)(2,1)S(1)} collective-permute-done((bf16[128,768]{1,0:T(8,128)(2,1)S(1)}, bf16[128,768]{1,0:T(8,128)(2,1)S(1)}, u32[]{:S(2)}, u32[]{:S(2)}) %collective-permute-start.38) | collective-permute-done | bytes 196640 | tf_op jit(solution)/shard_map/ppermute | solution.py:49
  257.7 1.8 collective-permute-start.67
  261.1 2.2 collective-permute-done.67.refs_6_
  263.3 1.6 collective-permute-done.69.refs_8_
  264.9 2.1 shard_map.255
  (159 shorter events, 35.8 us)
Async XLA Ops:
  0.6 11.2 %collective-permute-start = (bf16[128,768]{1,0:T(8,128)(2,1)}, bf16[128,768]{1,0:T(8,128)(2,1)S(1)}, u32[]{:S(2)}, u32[]{:S(2)}) collective-permute-start(bf16[128,768]{1,0:T(8,128)(2,1)} %refs_1_.7), channel_id=1, source_target_pairs={{0,1},{1,0},{2,3},{3,2},{4,5},{5,4},{6,7},{7,6},{8,9},{9,8},{10,11... | collective-permute-start | bytes 589832 | tf_op jit(solution)/shard_map/ppermute | solution.py:49
  1.2 11.3 %collective-permute-start.1 = (bf16[128,768]{1,0:T(8,128)(2,1)}, bf16[128,768]{1,0:T(8,128)(2,1)S(1)}, u32[]{:S(2)}, u32[]{:S(2)}) collective-permute-start(bf16[128,768]{1,0:T(8,128)(2,1)} %refs_1_.7), channel_id=1, source_target_pairs={{0,2},{1,3},{2,0},{3,1},{4,6},{5,7},{6,4},{7,5},{8,10},{9,11},{10,... | collective-permute-start | bytes 589832 | tf_op jit(solution)/shard_map/ppermute | solution.py:49
  7.6 12.4 %collective-permute-start.10 = (bf16[144,768]{1,0:T(8,128)(2,1)}, bf16[144,768]{1,0:T(8,128)(2,1)S(1)}, u32[]{:S(2)}, u32[]{:S(2)}) collective-permute-start(bf16[144,768]{1,0:T(8,128)(2,1)} %get-tuple-element.110.refs_1_), channel_id=1, source_target_pairs={{0,8},{4,12},{8,0},{12,4},{16,24},{20,28},{24,16},{28,20},{1,9},{5... | collective-permute-start | bytes 663560 | tf_op jit(solution)/shard_map/ppermute | solution.py:49
  9.2 13.2 %collective-permute-start.12 = (bf16[144,768]{1,0:T(8,128)(2,1)}, bf16[144,768]{1,0:T(8,128)(2,1)S(1)}, u32[]{:S(2)}, u32[]{:S(2)}) collective-permute-start(bf16[144,768]{1,0:T(8,128)(2,1)} %get-tuple-element.110.refs_1_), channel_id=1, source_target_pairs={{0,16},{4,20},{8,24},{12,28},{16,0},{20,4},{24,8},{28,12},{1,17},{... | collective-permute-start | bytes 663560 | tf_op jit(solution)/shard_map/ppermute | solution.py:49
  11.8 18.5 %collective-permute-start.3 = (bf16[224,576]{1,0:T(8,128)(2,1)}, bf16[224,576]{1,0:T(8,128)(2,1)S(1)}, u32[]{:S(2)}, u32[]{:S(2)}) collective-permute-start(bf16[224,576]{1,0:T(8,128)(2,1)} %get-tuple-element.101), channel_id=1, source_target_pairs={{0,1},{1,0},{2,3},{3,2},{4,5},{5,4},{6,7},{7,6},{8,9},{9,8},{10,11... | collective-permute-start | bytes 774152 | tf_op jit(solution)/shard_map/ppermute | solution.py:49
  11.8 19.0 %collective-permute-start.4 = (bf16[224,576]{1,0:T(8,128)(2,1)}, bf16[224,576]{1,0:T(8,128)(2,1)S(1)}, u32[]{:S(2)}, u32[]{:S(2)}) collective-permute-start(bf16[224,576]{1,0:T(8,128)(2,1)} %get-tuple-element.102), channel_id=1, source_target_pairs={{0,2},{1,3},{2,0},{3,1},{4,6},{5,7},{6,4},{7,5},{8,10},{9,11},{10,... | collective-permute-start | bytes 774152 | tf_op jit(solution)/shard_map/ppermute | solution.py:49
  12.4 19.9 %collective-permute-start.5 = (bf16[224,576]{1,0:T(8,128)(2,1)}, bf16[224,576]{1,0:T(8,128)(2,1)S(1)}, u32[]{:S(2)}, u32[]{:S(2)}) collective-permute-start(bf16[224,576]{1,0:T(8,128)(2,1)} %get-tuple-element.103), channel_id=1, source_target_pairs={{0,3},{1,2},{2,1},{3,0},{4,7},{5,6},{6,5},{7,4},{8,11},{9,10},{10,... | collective-permute-start | bytes 774152 | tf_op jit(solution)/shard_map/ppermute | solution.py:49
  20.0 8.8 %collective-permute-start.14 = (bf16[144,768]{1,0:T(8,128)(2,1)}, bf16[144,768]{1,0:T(8,128)(2,1)S(1)}, u32[]{:S(2)}, u32[]{:S(2)}) collective-permute-start(bf16[144,768]{1,0:T(8,128)(2,1)} %get-tuple-element.110.refs_1_), channel_id=1, source_target_pairs={{0,24},{4,28},{8,16},{12,20},{16,8},{20,12},{24,0},{28,4},{1,25},{... | collective-permute-start | bytes 663560 | tf_op jit(solution)/shard_map/ppermute | solution.py:49
  22.5 11.9 %collective-permute-start.2 = (bf16[128,768]{1,0:T(8,128)(2,1)S(1)}, bf16[128,768]{1,0:T(8,128)(2,1)S(1)}, u32[]{:S(2)}, u32[]{:S(2)}) collective-permute-start(bf16[128,768]{1,0:T(8,128)(2,1)S(1)} %collective-permute-done.1.refs_3_), channel_id=1, source_target_pairs={{0,1},{1,0},{2,3},{3,2},{4,5},{5,4},{6,7},{7,6},{8,9},{9,8},{10,11... | collective-permute-start | bytes 589832 | tf_op jit(solution)/shard_map/ppermute | solution.py:49
  28.7 14.7 %collective-permute-start.9 = (bf16[144,768]{1,0:T(8,128)(2,1)}, bf16[144,768]{1,0:T(8,128)(2,1)S(1)}, u32[]{:S(2)}, u32[]{:S(2)}) collective-permute-start(bf16[144,768]{1,0:T(8,128)(2,1)} %get-tuple-element.110.refs_1_), channel_id=1, source_target_pairs={{0,4},{4,0},{8,12},{12,8},{16,20},{20,16},{24,28},{28,24},{1,5},{5... | collective-permute-start | bytes 663560 | tf_op jit(solution)/shard_map/ppermute | solution.py:49
  30.3 13.1 %collective-permute-start.11 = (bf16[144,768]{1,0:T(8,128)(2,1)S(1)}, bf16[144,768]{1,0:T(8,128)(2,1)S(1)}, u32[]{:S(2)}, u32[]{:S(2)}) collective-permute-start(bf16[144,768]{1,0:T(8,128)(2,1)S(1)} %collective-permute-done.10.refs_3_), channel_id=1, source_target_pairs={{0,4},{4,0},{8,12},{12,8},{16,20},{20,16},{24,28},{28,24},{1,5},{5... | collective-permute-start | bytes 663560 | tf_op jit(solution)/shard_map/ppermute | solution.py:49
  30.8 15.8 %collective-permute-start.13 = (bf16[144,768]{1,0:T(8,128)(2,1)S(1)}, bf16[144,768]{1,0:T(8,128)(2,1)S(1)}, u32[]{:S(2)}, u32[]{:S(2)}) collective-permute-start(bf16[144,768]{1,0:T(8,128)(2,1)S(1)} %collective-permute-done.12.refs_5_), channel_id=1, source_target_pairs={{0,4},{4,0},{8,12},{12,8},{16,20},{20,16},{24,28},{28,24},{1,5},{5... | collective-permute-start | bytes 663560 | tf_op jit(solution)/shard_map/ppermute | solution.py:49
  32.3 16.6 %collective-permute-start.15 = (bf16[144,768]{1,0:T(8,128)(2,1)S(1)}, bf16[144,768]{1,0:T(8,128)(2,1)S(1)}, u32[]{:S(2)}, u32[]{:S(2)}) collective-permute-start(bf16[144,768]{1,0:T(8,128)(2,1)S(1)} %collective-permute-done.14.refs_7_), channel_id=1, source_target_pairs={{0,4},{4,0},{8,12},{12,8},{16,20},{20,16},{24,28},{28,24},{1,5},{5... | collective-permute-start | bytes 663560 | tf_op jit(solution)/shard_map/ppermute | solution.py:49
  43.3 9.0 %collective-permute-start.7 = (bf16[128,768]{1,0:T(8,128)(2,1)}, bf16[128,768]{1,0:T(8,128)(2,1)S(1)}, u32[]{:S(2)}, u32[]{:S(2)}) collective-permute-start(bf16[128,768]{1,0:T(8,128)(2,1)} %get-tuple-element.108), channel_id=1, source_target_pairs={{0,1},{1,0},{2,3},{3,2},{4,5},{5,4},{6,7},{7,6},{8,9},{9,8},{10,11... | collective-permute-start | bytes 589832 | tf_op jit(solution)/shard_map/ppermute | solution.py:49
  50.7 11.2 %collective-permute-start.16 = (bf16[272,768]{1,0:T(8,128)(2,1)S(1)}, bf16[272,768]{1,0:T(8,128)(2,1)S(1)}, u32[]{:S(2)}, u32[]{:S(2)}) collective-permute-start(bf16[272,768]{1,0:T(8,128)(2,1)S(1)} %get-tuple-element.112.refs_5_.refs_10_), channel_id=1, source_target_pairs={{0,2},{1,3},{2,0},{3,1},{4,6},{5,7},{6,4},{7,5},{8,10},{9,11},{10,... | collective-permute-start | bytes 1253384 | tf_op jit(solution)/shard_map/ppermute | solution.py:49
  51.8 10.1 %collective-permute-start.6 = (bf16[128,768]{1,0:T(8,128)(2,1)S(1)}, bf16[128,768]{1,0:T(8,128)(2,1)S(1)}, u32[]{:S(2)}, u32[]{:S(2)}) collective-permute-start(bf16[128,768]{1,0:T(8,128)(2,1)S(1)} %copy-done.23), channel_id=1, source_target_pairs={{0,1},{1,0},{2,3},{3,2},{4,5},{5,4},{6,7},{7,6},{8,9},{9,8},{10,11... | collective-permute-start | bytes 589832 | tf_op jit(solution)/shard_map/ppermute | solution.py:49
  51.8 21.5 %collective-permute-start.18 = (bf16[272,768]{1,0:T(8,128)(2,1)S(1)}, bf16[272,768]{1,0:T(8,128)(2,1)S(1)}, u32[]{:S(2)}, u32[]{:S(2)}) collective-permute-start(bf16[272,768]{1,0:T(8,128)(2,1)S(1)} %get-tuple-element.112.refs_5_.refs_10_), channel_id=1, source_target_pairs={{0,1},{1,0},{2,3},{3,2},{4,5},{5,4},{6,7},{7,6},{8,9},{9,8},{10,11... | collective-permute-start | bytes 1253384 | tf_op jit(solution)/shard_map/ppermute | solution.py:49
  52.4 11.6 %collective-permute-start.8 = (bf16[128,768]{1,0:T(8,128)(2,1)S(1)}, bf16[128,768]{1,0:T(8,128)(2,1)S(1)}, u32[]{:S(2)}, u32[]{:S(2)}) collective-permute-start(bf16[128,768]{1,0:T(8,128)(2,1)S(1)} %add_convert_fusion.6), channel_id=1, source_target_pairs={{0,2},{1,3},{2,0},{3,1},{4,6},{5,7},{6,4},{7,5},{8,10},{9,11},{10,... | collective-permute-start | bytes 589832 | tf_op jit(solution)/shard_map/ppermute | solution.py:49
  61.9 26.9 %collective-permute-start.17 = (bf16[272,768]{1,0:T(8,128)(2,1)S(1)}, bf16[272,768]{1,0:T(8,128)(2,1)S(1)}, u32[]{:S(2)}, u32[]{:S(2)}) collective-permute-start(bf16[272,768]{1,0:T(8,128)(2,1)S(1)} %collective-permute-done.16.refs_3_.refs_12_), channel_id=1, source_target_pairs={{0,1},{1,0},{2,3},{3,2},{4,5},{5,4},{6,7},{7,6},{8,9},{9,8},{10,11... | collective-permute-start | bytes 1253384 | tf_op jit(solution)/shard_map/ppermute | solution.py:49
  64.8 12.1 %collective-permute-start.20 = (bf16[128,768]{1,0:T(8,128)(2,1)S(1)}, bf16[128,768]{1,0:T(8,128)(2,1)S(1)}, u32[]{:S(2)}, u32[]{:S(2)}) collective-permute-start(bf16[128,768]{1,0:T(8,128)(2,1)S(1)} %get-tuple-element.118.refs_3_), channel_id=1, source_target_pairs={{0,8},{4,12},{8,0},{12,4},{16,24},{20,28},{24,16},{28,20},{1,9},{5... | collective-permute-start | bytes 589832 | tf_op jit(solution)/shard_map/ppermute | solution.py:49
  70.8 15.9 %collective-permute-start.22 = (bf16[128,768]{1,0:T(8,128)(2,1)S(1)}, bf16[128,768]{1,0:T(8,128)(2,1)S(1)}, u32[]{:S(2)}, u32[]{:S(2)}) collective-permute-start(bf16[128,768]{1,0:T(8,128)(2,1)S(1)} %get-tuple-element.118.refs_3_), channel_id=1, source_target_pairs={{0,16},{4,20},{8,24},{12,28},{16,0},{20,4},{24,8},{28,12},{1,17},{... | collective-permute-start | bytes 589832 | tf_op jit(solution)/shard_map/ppermute | solution.py:49
  70.9 17.4 %collective-permute-start.24 = (bf16[128,768]{1,0:T(8,128)(2,1)S(1)}, bf16[128,768]{1,0:T(8,128)(2,1)S(1)}, u32[]{:S(2)}, u32[]{:S(2)}) collective-permute-start(bf16[128,768]{1,0:T(8,128)(2,1)S(1)} %get-tuple-element.118.refs_3_), channel_id=1, source_target_pairs={{0,24},{4,28},{8,16},{12,20},{16,8},{20,12},{24,0},{28,4},{1,25},{... | collective-permute-start | bytes 589832 | tf_op jit(solution)/shard_map/ppermute | solution.py:49
  73.3 17.5 %collective-permute-start.19 = (bf16[128,768]{1,0:T(8,128)(2,1)S(1)}, bf16[128,768]{1,0:T(8,128)(2,1)S(1)}, u32[]{:S(2)}, u32[]{:S(2)}) collective-permute-start(bf16[128,768]{1,0:T(8,128)(2,1)S(1)} %get-tuple-element.118.refs_3_), channel_id=1, source_target_pairs={{0,4},{4,0},{8,12},{12,8},{16,20},{20,16},{24,28},{28,24},{1,5},{5... | collective-permute-start | bytes 589832 | tf_op jit(solution)/shard_map/ppermute | solution.py:49
  76.9 13.9 %collective-permute-start.21 = (bf16[128,768]{1,0:T(8,128)(2,1)S(1)}, bf16[128,768]{1,0:T(8,128)(2,1)S(1)}, u32[]{:S(2)}, u32[]{:S(2)}) collective-permute-start(bf16[128,768]{1,0:T(8,128)(2,1)S(1)} %collective-permute-done.20.refs_5_), channel_id=1, source_target_pairs={{0,4},{4,0},{8,12},{12,8},{16,20},{20,16},{24,28},{28,24},{1,5},{5... | collective-permute-start | bytes 589832 | tf_op jit(solution)/shard_map/ppermute | solution.py:49
  86.8 5.7 %collective-permute-start.23 = (bf16[128,768]{1,0:T(8,128)(2,1)S(1)}, bf16[128,768]{1,0:T(8,128)(2,1)S(1)}, u32[]{:S(2)}, u32[]{:S(2)}) collective-permute-start(bf16[128,768]{1,0:T(8,128)(2,1)S(1)} %collective-permute-done.22.refs_7_), channel_id=1, source_target_pairs={{0,4},{4,0},{8,12},{12,8},{16,20},{20,16},{24,28},{28,24},{1,5},{5... | collective-permute-start | bytes 589832 | tf_op jit(solution)/shard_map/ppermute | solution.py:49
  88.3 6.3 %collective-permute-start.25 = (bf16[128,768]{1,0:T(8,128)(2,1)S(1)}, bf16[128,768]{1,0:T(8,128)(2,1)S(1)}, u32[]{:S(2)}, u32[]{:S(2)}) collective-permute-start(bf16[128,768]{1,0:T(8,128)(2,1)S(1)} %collective-permute-done.24.refs_9_), channel_id=1, source_target_pairs={{0,4},{4,0},{8,12},{12,8},{16,20},{20,16},{24,28},{28,24},{1,5},{5... | collective-permute-start | bytes 589832 | tf_op jit(solution)/shard_map/ppermute | solution.py:49
  96.1 7.8 %collective-permute-start.26 = (bf16[256,768]{1,0:T(8,128)(2,1)S(1)}, bf16[256,768]{1,0:T(8,128)(2,1)S(1)}, u32[]{:S(2)}, u32[]{:S(2)}) collective-permute-start(bf16[256,768]{1,0:T(8,128)(2,1)S(1)} %shard_map.243.refs_9_.refs_7_.refs_6_), channel_id=1, source_target_pairs={{0,2},{1,3},{2,0},{3,1},{4,6},{5,7},{6,4},{7,5},{8,10},{9,11},{10,... | collective-permute-start | bytes 1179656 | tf_op jit(solution)/shard_map/ppermute | solution.py:49
  116.3 11.4 %collective-permute-start.31 = (bf16[256,768]{1,0:T(8,128)(2,1)S(1)}, bf16[256,768]{1,0:T(8,128)(2,1)S(1)}, u32[]{:S(2)}, u32[]{:S(2)}) collective-permute-start(bf16[256,768]{1,0:T(8,128)(2,1)S(1)} %add_convert_fusion.1.refs_0_), channel_id=1, source_target_pairs={{0,2},{1,3},{2,0},{3,1},{4,6},{5,7},{6,4},{7,5},{8,10},{9,11},{10,... | collective-permute-start | bytes 1179656 | tf_op jit(solution)/shard_map/ppermute | solution.py:49
  129.0 7.9 %collective-permute-start.42 = (bf16[128,768]{1,0:T(8,128)(2,1)S(1)}, bf16[128,768]{1,0:T(8,128)(2,1)S(1)}, u32[]{:S(2)}, u32[]{:S(2)}) collective-permute-start(bf16[128,768]{1,0:T(8,128)(2,1)S(1)} %get-tuple-element.146), channel_id=1, source_target_pairs={{0,4},{4,0},{8,12},{12,8},{16,20},{20,16},{24,28},{28,24},{1,5},{5... | collective-permute-start | bytes 589832 | tf_op jit(solution)/shard_map/ppermute | solution.py:49
  130.6 20.7 %collective-permute-start.32 = (bf16[128,768]{1,0:T(8,128)(2,1)S(1)}, bf16[128,768]{1,0:T(8,128)(2,1)S(1)}, u32[]{:S(2)}, u32[]{:S(2)}) collective-permute-start(bf16[128,768]{1,0:T(8,128)(2,1)S(1)} %get-tuple-element.128), channel_id=1, source_target_pairs={{0,4},{4,0},{8,12},{12,8},{16,20},{20,16},{24,28},{28,24},{1,5},{5... | collective-permute-start | bytes 589832 | tf_op jit(solution)/shard_map/ppermute | solution.py:49
  133.4 38.3 %collective-permute-start.33 = (bf16[256,768]{1,0:T(8,128)(2,1)S(1)}, bf16[256,768]{1,0:T(8,128)(2,1)S(1)}, u32[]{:S(2)}, u32[]{:S(2)}) collective-permute-start(bf16[256,768]{1,0:T(8,128)(2,1)S(1)} %get-tuple-element.135), channel_id=1, source_target_pairs={{0,1},{1,0},{2,3},{3,2},{4,5},{5,4},{6,7},{7,6},{8,9},{9,8},{10,11... | collective-permute-start | bytes 1179656 | tf_op jit(solution)/shard_map/ppermute | solution.py:49
  133.5 19.7 %collective-permute-start.34 = (bf16[256,768]{1,0:T(8,128)(2,1)S(1)}, bf16[256,768]{1,0:T(8,128)(2,1)S(1)}, u32[]{:S(2)}, u32[]{:S(2)}) collective-permute-start(bf16[256,768]{1,0:T(8,128)(2,1)S(1)} %get-tuple-element.137), channel_id=1, source_target_pairs={{0,1},{1,0},{2,3},{3,2},{4,5},{5,4},{6,7},{7,6},{8,9},{9,8},{10,11... | collective-permute-start | bytes 1179656 | tf_op jit(solution)/shard_map/ppermute | solution.py:49
  134.0 19.4 %collective-permute-start.41 = (bf16[128,768]{1,0:T(8,128)(2,1)S(1)}, bf16[128,768]{1,0:T(8,128)(2,1)S(1)}, u32[]{:S(2)}, u32[]{:S(2)}) collective-permute-start(bf16[128,768]{1,0:T(8,128)(2,1)S(1)} %get-tuple-element.144), channel_id=1, source_target_pairs={{0,4},{4,0},{8,12},{12,8},{16,20},{20,16},{24,28},{28,24},{1,5},{5... | collective-permute-start | bytes 589832 | tf_op jit(solution)/shard_map/ppermute | solution.py:49
  136.9 11.2 %collective-permute-start.44 = (bf16[128,768]{1,0:T(8,128)(2,1)S(1)}, bf16[128,768]{1,0:T(8,128)(2,1)S(1)}, u32[]{:S(2)}, u32[]{:S(2)}) collective-permute-start(bf16[128,768]{1,0:T(8,128)(2,1)S(1)} %get-tuple-element.148), channel_id=1, source_target_pairs={{0,4},{4,0},{8,12},{12,8},{16,20},{20,16},{24,28},{28,24},{1,5},{5... | collective-permute-start | bytes 589832 | tf_op jit(solution)/shard_map/ppermute | solution.py:49
  148.0 17.0 %collective-permute-start.43 = (bf16[128,768]{1,0:T(8,128)(2,1)S(1)}, bf16[128,768]{1,0:T(8,128)(2,1)S(1)}, u32[]{:S(2)}, u32[]{:S(2)}) collective-permute-start(bf16[128,768]{1,0:T(8,128)(2,1)S(1)} %add_convert_fusion.4), channel_id=1, source_target_pairs={{0,16},{4,20},{8,24},{12,28},{16,0},{20,4},{24,8},{28,12},{1,17},{... | collective-permute-start | bytes 589832 | tf_op jit(solution)/shard_map/ppermute | solution.py:49
  151.3 13.7 %collective-permute-start.45 = (bf16[128,768]{1,0:T(8,128)(2,1)S(1)}, bf16[128,768]{1,0:T(8,128)(2,1)S(1)}, u32[]{:S(2)}, u32[]{:S(2)}) collective-permute-start(bf16[128,768]{1,0:T(8,128)(2,1)S(1)} %add_convert_fusion.3), channel_id=1, source_target_pairs={{0,24},{4,28},{8,16},{12,20},{16,8},{20,12},{24,0},{28,4},{1,25},{... | collective-permute-start | bytes 589832 | tf_op jit(solution)/shard_map/ppermute | solution.py:49
  153.2 11.8 %collective-permute-start.46 = (bf16[128,768]{1,0:T(8,128)(2,1)S(1)}, bf16[128,768]{1,0:T(8,128)(2,1)S(1)}, u32[]{:S(2)}, u32[]{:S(2)}) collective-permute-start(bf16[128,768]{1,0:T(8,128)(2,1)S(1)} %add_convert_fusion.5.refs_0_), channel_id=1, source_target_pairs={{0,8},{4,12},{8,0},{12,4},{16,24},{20,28},{24,16},{28,20},{1,9},{5... | collective-permute-start | bytes 589832 | tf_op jit(solution)/shard_map/ppermute | solution.py:49
  153.4 18.3 %collective-permute-start.35 = (bf16[256,768]{1,0:T(8,128)(2,1)S(1)}, bf16[256,768]{1,0:T(8,128)(2,1)S(1)}, u32[]{:S(2)}, u32[]{:S(2)}) collective-permute-start(bf16[256,768]{1,0:T(8,128)(2,1)S(1)} %add_convert_fusion), channel_id=1, source_target_pairs={{0,2},{1,3},{2,0},{3,1},{4,6},{5,7},{6,4},{7,5},{8,10},{9,11},{10,... | collective-permute-start | bytes 1179656 | tf_op jit(solution)/shard_map/ppermute | solution.py:49
  165.9 5.7 %collective-permute-start.48 = (bf16[128,768]{1,0:T(8,128)(2,1)S(1)}, bf16[128,768]{1,0:T(8,128)(2,1)S(1)}, u32[]{:S(2)}, u32[]{:S(2)}) collective-permute-start(bf16[128,768]{1,0:T(8,128)(2,1)S(1)} %get-tuple-element.158.refs_11_), channel_id=1, source_target_pairs={{0,2},{1,3},{2,0},{3,1},{4,6},{5,7},{6,4},{7,5},{8,10},{9,11},{10,... | collective-permute-start | bytes 589832 | tf_op jit(solution)/shard_map/ppermute | solution.py:49
  166.9 6.0 %collective-permute-start.47 = (bf16[128,768]{1,0:T(8,128)(2,1)S(1)}, bf16[128,768]{1,0:T(8,128)(2,1)S(1)}, u32[]{:S(2)}, u32[]{:S(2)}) collective-permute-start(bf16[128,768]{1,0:T(8,128)(2,1)S(1)} %get-tuple-element.158.refs_11_), channel_id=1, source_target_pairs={{0,1},{1,0},{2,3},{3,2},{4,5},{5,4},{6,7},{7,6},{8,9},{9,8},{10,11... | collective-permute-start | bytes 589832 | tf_op jit(solution)/shard_map/ppermute | solution.py:49
  179.8 7.3 %collective-permute-start.54 = (bf16[4,24,896]{2,1,0:T(8,128)(2,1)S(1)}, bf16[4,24,896]{2,1,0:T(8,128)(2,1)S(1)}, u32[]{:S(2)}, u32[]{:S(2)}) collective-permute-start(bf16[4,24,896]{2,1,0:T(8,128)(2,1)S(1)} %get-tuple-element.166), channel_id=1, source_target_pairs={{0,4},{4,0},{8,12},{12,8},{16,20},{20,16},{24,28},{28,24},{1,5},{5... | collective-permute-start | bytes 516104 | tf_op jit(solution)/shard_map/ppermute | solution.py:49
  181.4 45.9 %collective-permute-start.37 = (bf16[2,128,768]{2,1,0:T(8,128)(2,1)S(1)}, bf16[2,128,768]{2,1,0:T(8,128)(2,1)S(1)}, u32[]{:S(2)}, u32[]{:S(2)}) collective-permute-start(bf16[2,128,768]{2,1,0:T(8,128)(2,1)S(1)} %get-tuple-element.141), channel_id=1, source_target_pairs={{0,4},{4,0},{8,12},{12,8},{16,20},{20,16},{24,28},{28,24},{1,5},{5... | collective-permute-start | bytes 1179656 | tf_op jit(solution)/shard_map/ppermute | solution.py:49
  181.9 39.9 %collective-permute-start.51 = (bf16[128,768]{1,0:T(8,128)(2,1)S(1)}, bf16[128,768]{1,0:T(8,128)(2,1)S(1)}, u32[]{:S(2)}, u32[]{:S(2)}) collective-permute-start(bf16[128,768]{1,0:T(8,128)(2,1)S(1)} %get-tuple-element.162), channel_id=1, source_target_pairs={{0,1},{1,0},{2,3},{3,2},{4,5},{5,4},{6,7},{7,6},{8,9},{9,8},{10,11... | collective-permute-start | bytes 589832 | tf_op jit(solution)/shard_map/ppermute | solution.py:49
  181.9 26.6 %collective-permute-start.53 = (bf16[4,24,896]{2,1,0:T(8,128)(2,1)S(1)}, bf16[4,24,896]{2,1,0:T(8,128)(2,1)S(1)}, u32[]{:S(2)}, u32[]{:S(2)}) collective-permute-start(bf16[4,24,896]{2,1,0:T(8,128)(2,1)S(1)} %get-tuple-element.164), channel_id=1, source_target_pairs={{0,4},{4,0},{8,12},{12,8},{16,20},{20,16},{24,28},{28,24},{1,5},{5... | collective-permute-start | bytes 516104 | tf_op jit(solution)/shard_map/ppermute | solution.py:49
  183.4 19.4 %collective-permute-start.56 = (bf16[4,24,896]{2,1,0:T(8,128)(2,1)S(1)}, bf16[4,24,896]{2,1,0:T(8,128)(2,1)S(1)}, u32[]{:S(2)}, u32[]{:S(2)}) collective-permute-start(bf16[4,24,896]{2,1,0:T(8,128)(2,1)S(1)} %get-tuple-element.168), channel_id=1, source_target_pairs={{0,4},{4,0},{8,12},{12,8},{16,20},{20,16},{24,28},{28,24},{1,5},{5... | collective-permute-start | bytes 516104 | tf_op jit(solution)/shard_map/ppermute | solution.py:49
  187.1 19.3 %collective-permute-start.58 = (bf16[4,24,896]{2,1,0:T(8,128)(2,1)S(1)}, bf16[4,24,896]{2,1,0:T(8,128)(2,1)S(1)}, u32[]{:S(2)}, u32[]{:S(2)}) collective-permute-start(bf16[4,24,896]{2,1,0:T(8,128)(2,1)S(1)} %get-tuple-element.170), channel_id=1, source_target_pairs={{0,4},{4,0},{8,12},{12,8},{16,20},{20,16},{24,28},{28,24},{1,5},{5... | collective-permute-start | bytes 516104 | tf_op jit(solution)/shard_map/ppermute | solution.py:49
  202.9 16.1 %collective-permute-start.55 = (bf16[4,24,896]{2,1,0:T(8,128)(2,1)S(1)}, bf16[4,24,896]{2,1,0:T(8,128)(2,1)S(1)}, u32[]{:S(2)}, u32[]{:S(2)}) collective-permute-start(bf16[4,24,896]{2,1,0:T(8,128)(2,1)S(1)} %add_convert_fusion.9), channel_id=1, source_target_pairs={{0,16},{4,20},{8,24},{12,28},{16,0},{20,4},{24,8},{28,12},{1,17},{... | collective-permute-start | bytes 516104 | tf_op jit(solution)/shard_map/ppermute | solution.py:49
  206.4 14.1 %collective-permute-start.57 = (bf16[4,24,896]{2,1,0:T(8,128)(2,1)S(1)}, bf16[4,24,896]{2,1,0:T(8,128)(2,1)S(1)}, u32[]{:S(2)}, u32[]{:S(2)}) collective-permute-start(bf16[4,24,896]{2,1,0:T(8,128)(2,1)S(1)} %add_convert_fusion.8), channel_id=1, source_target_pairs={{0,24},{4,28},{8,16},{12,20},{16,8},{20,12},{24,0},{28,4},{1,25},{... | collective-permute-start | bytes 516104 | tf_op jit(solution)/shard_map/ppermute | solution.py:49
  208.5 11.9 %collective-permute-start.59 = (bf16[4,24,896]{2,1,0:T(8,128)(2,1)S(1)}, bf16[4,24,896]{2,1,0:T(8,128)(2,1)S(1)}, u32[]{:S(2)}, u32[]{:S(2)}) collective-permute-start(bf16[4,24,896]{2,1,0:T(8,128)(2,1)S(1)} %add_convert_fusion.7), channel_id=1, source_target_pairs={{0,8},{4,12},{8,0},{12,4},{16,24},{20,28},{24,16},{28,20},{1,9},{5... | collective-permute-start | bytes 516104 | tf_op jit(solution)/shard_map/ppermute | solution.py:49
  219.0 15.8 %collective-permute-start.36 = (bf16[2,128,768]{2,1,0:T(8,128)(2,1)S(1)}, bf16[2,128,768]{2,1,0:T(8,128)(2,1)S(1)}, u32[]{:S(2)}, u32[]{:S(2)}) collective-permute-start(bf16[2,128,768]{2,1,0:T(8,128)(2,1)S(1)} %get-tuple-element.139), channel_id=1, source_target_pairs={{0,4},{4,0},{8,12},{12,8},{16,20},{20,16},{24,28},{28,24},{1,5},{5... | collective-permute-start | bytes 1179656 | tf_op jit(solution)/shard_map/ppermute | solution.py:49
  221.3 4.3 %collective-permute-start.61 = (bf16[24,704]{1,0:T(8,128)(2,1)S(1)}, bf16[24,704]{1,0:T(8,128)(2,1)S(1)}, u32[]{:S(2)}, u32[]{:S(2)}) collective-permute-start(bf16[24,704]{1,0:T(8,128)(2,1)S(1)} %get-tuple-element.173), channel_id=1, source_target_pairs={{0,2},{1,3},{2,0},{3,1},{4,6},{5,7},{6,4},{7,5},{8,10},{9,11},{10,... | collective-permute-start | bytes 101384 | tf_op jit(solution)/shard_map/ppermute | solution.py:49
  221.8 4.0 %collective-permute-start.62 = (bf16[24,704]{1,0:T(8,128)(2,1)S(1)}, bf16[24,704]{1,0:T(8,128)(2,1)S(1)}, u32[]{:S(2)}, u32[]{:S(2)}) collective-permute-start(bf16[24,704]{1,0:T(8,128)(2,1)S(1)} %get-tuple-element.174), channel_id=1, source_target_pairs={{0,3},{1,2},{2,1},{3,0},{4,7},{5,6},{6,5},{7,4},{8,11},{9,10},{10,... | collective-permute-start | bytes 101384 | tf_op jit(solution)/shard_map/ppermute | solution.py:49
  223.2 6.4 %collective-permute-start.50 = (bf16[128,768]{1,0:T(8,128)(2,1)S(1)}, bf16[128,768]{1,0:T(8,128)(2,1)S(1)}, u32[]{:S(2)}, u32[]{:S(2)}) collective-permute-start(bf16[128,768]{1,0:T(8,128)(2,1)S(1)} %get-tuple-element.160), channel_id=1, source_target_pairs={{0,1},{1,0},{2,3},{3,2},{4,5},{5,4},{6,7},{7,6},{8,9},{9,8},{10,11... | collective-permute-start | bytes 589832 | tf_op jit(solution)/shard_map/ppermute | solution.py:49
  225.6 6.1 %collective-permute-start.52 = (bf16[128,768]{1,0:T(8,128)(2,1)S(1)}, bf16[128,768]{1,0:T(8,128)(2,1)S(1)}, u32[]{:S(2)}, u32[]{:S(2)}) collective-permute-start(bf16[128,768]{1,0:T(8,128)(2,1)S(1)} %add_convert_fusion.2), channel_id=1, source_target_pairs={{0,2},{1,3},{2,0},{3,1},{4,6},{5,7},{6,4},{7,5},{8,10},{9,11},{10,... | collective-permute-start | bytes 589832 | tf_op jit(solution)/shard_map/ppermute | solution.py:49
  226.5 10.1 %collective-permute-start.64 = (bf16[24,3200]{1,0:T(8,128)(2,1)S(1)}, bf16[24,3200]{1,0:T(8,128)(2,1)S(1)}, u32[]{:S(2)}, u32[]{:S(2)}) collective-permute-start(bf16[24,3200]{1,0:T(8,128)(2,1)S(1)} %shard_map.254.refs_1_), channel_id=1, source_target_pairs={{0,8},{4,12},{8,0},{12,4},{16,24},{20,28},{24,16},{28,20},{1,9},{5... | collective-permute-start | bytes 460808 | tf_op jit(solution)/shard_map/ppermute | solution.py:49
  227.4 22.5 %collective-permute-start.66 = (bf16[24,3200]{1,0:T(8,128)(2,1)S(1)}, bf16[24,3200]{1,0:T(8,128)(2,1)S(1)}, u32[]{:S(2)}, u32[]{:S(2)}) collective-permute-start(bf16[24,3200]{1,0:T(8,128)(2,1)S(1)} %shard_map.254.refs_1_), channel_id=1, source_target_pairs={{0,16},{4,20},{8,24},{12,28},{16,0},{20,4},{24,8},{28,12},{1,17},{... | collective-permute-start | bytes 460808 | tf_op jit(solution)/shard_map/ppermute | solution.py:49
  229.6 20.6 %collective-permute-start.68 = (bf16[24,3200]{1,0:T(8,128)(2,1)S(1)}, bf16[24,3200]{1,0:T(8,128)(2,1)S(1)}, u32[]{:S(2)}, u32[]{:S(2)}) collective-permute-start(bf16[24,3200]{1,0:T(8,128)(2,1)S(1)} %shard_map.254.refs_1_), channel_id=1, source_target_pairs={{0,24},{4,28},{8,16},{12,20},{16,8},{20,12},{24,0},{28,4},{1,25},{... | collective-permute-start | bytes 460808 | tf_op jit(solution)/shard_map/ppermute | solution.py:49
  231.7 26.0 %collective-permute-start.38 = (bf16[128,768]{1,0:T(8,128)(2,1)S(1)}, bf16[128,768]{1,0:T(8,128)(2,1)S(1)}, u32[]{:S(2)}, u32[]{:S(2)}) collective-permute-start(bf16[128,768]{1,0:T(8,128)(2,1)S(1)} %get-tuple-element.213), channel_id=1, source_target_pairs={{0,16},{4,20},{8,24},{12,28},{16,0},{20,4},{24,8},{28,12},{1,17},{... | collective-permute-start | bytes 589832 | tf_op jit(solution)/shard_map/ppermute | solution.py:49
  234.7 24.7 %collective-permute-start.39 = (bf16[128,768]{1,0:T(8,128)(2,1)S(1)}, bf16[128,768]{1,0:T(8,128)(2,1)S(1)}, u32[]{:S(2)}, u32[]{:S(2)}) collective-permute-start(bf16[128,768]{1,0:T(8,128)(2,1)S(1)} %get-tuple-element.212), channel_id=1, source_target_pairs={{0,24},{4,28},{8,16},{12,20},{16,8},{20,12},{24,0},{28,4},{1,25},{... | collective-permute-start | bytes 589832 | tf_op jit(solution)/shard_map/ppermute | solution.py:49
  236.6 24.5 %collective-permute-start.63 = (bf16[24,3200]{1,0:T(8,128)(2,1)S(1)}, bf16[24,3200]{1,0:T(8,128)(2,1)S(1)}, u32[]{:S(2)}, u32[]{:S(2)}) collective-permute-start(bf16[24,3200]{1,0:T(8,128)(2,1)S(1)} %shard_map.254.refs_1_), channel_id=1, source_target_pairs={{0,4},{4,0},{8,12},{12,8},{16,20},{20,16},{24,28},{28,24},{1,5},{5... | collective-permute-start | bytes 460808 | tf_op jit(solution)/shard_map/ppermute | solution.py:49
  249.9 9.8 %collective-permute-start.40 = (bf16[128,768]{1,0:T(8,128)(2,1)S(1)}, bf16[128,768]{1,0:T(8,128)(2,1)S(1)}, u32[]{:S(2)}, u32[]{:S(2)}) collective-permute-start(bf16[128,768]{1,0:T(8,128)(2,1)S(1)} %fusion), channel_id=1, source_target_pairs={{0,8},{4,12},{8,0},{12,4},{16,24},{20,28},{24,16},{28,20},{1,9},{5... | collective-permute-start | bytes 589832 | tf_op jit(solution)/shard_map/ppermute | solution.py:49
  250.2 10.9 %collective-permute-start.65 = (bf16[24,3200]{1,0:T(8,128)(2,1)S(1)}, bf16[24,3200]{1,0:T(8,128)(2,1)S(1)}, u32[]{:S(2)}, u32[]{:S(2)}) collective-permute-start(bf16[24,3200]{1,0:T(8,128)(2,1)S(1)} %collective-permute-done.64.refs_3_), channel_id=1, source_target_pairs={{0,4},{4,0},{8,12},{12,8},{16,20},{20,16},{24,28},{28,24},{1,5},{5... | collective-permute-start | bytes 460808 | tf_op jit(solution)/shard_map/ppermute | solution.py:49
  257.7 5.6 %collective-permute-start.67 = (bf16[24,3200]{1,0:T(8,128)(2,1)S(1)}, bf16[24,3200]{1,0:T(8,128)(2,1)S(1)}, u32[]{:S(2)}, u32[]{:S(2)}) collective-permute-start(bf16[24,3200]{1,0:T(8,128)(2,1)S(1)} %collective-permute-done.66.refs_5_), channel_id=1, source_target_pairs={{0,4},{4,0},{8,12},{12,8},{16,20},{20,16},{24,28},{28,24},{1,5},{5... | collective-permute-start | bytes 460808 | tf_op jit(solution)/shard_map/ppermute | solution.py:49
  259.4 5.5 %collective-permute-start.69 = (bf16[24,3200]{1,0:T(8,128)(2,1)S(1)}, bf16[24,3200]{1,0:T(8,128)(2,1)S(1)}, u32[]{:S(2)}, u32[]{:S(2)}) collective-permute-start(bf16[24,3200]{1,0:T(8,128)(2,1)S(1)} %collective-permute-done.68.refs_7_), channel_id=1, source_target_pairs={{0,4},{4,0},{8,12},{12,8},{16,20},{20,16},{24,28},{28,24},{1,5},{5... | collective-permute-start | bytes 460808 | tf_op jit(solution)/shard_map/ppermute | solution.py:49
  (30 other events, 433.5 us)
where the time goes:
time: 268 us
  waiting for transfers between devices  135 us (50%)
  starting transfers between devices  77.9 us (29%)
  Pallas kernels  48.6 us (18%)
  local copies, waits for them, and re-layouts  2.95 us (1%)
    ppermute x70, waiting for transfers between devices, swap(): return lax.ppermute(value, axis, [(i, i ^ step) for i in range(count)])  135 us
    ppermute x70, starting transfers between devices, swap(): return lax.ppermute(value, axis, [(i, i ^ step) for i in range(count)])  77.9 us
    pallas_call x19, Pallas kernels, call(): pl.pallas_call(lambda *refs: kernel(*refs[skip:]), out_shape=tuple((jax.S...  48.6 us
  transfers between devices with their start and end apart: 70, of which 30 were waited for; matrix products, arithmetic and copies ran while one was open for 1% of the time, Pallas kernels for 11%

commit v1 on v0

--- a/solution.py
+++ b/solution.py
@@ -55,11 +55,10 @@
     return [value, near, far, swap(far, W, 1)]
 
 
-def sum_w(parts):
-    a3 = swap(parts[3], W, 1)
-    a1 = swap(parts[1], W, 1)
-    across = (parts[2].astype(wide) + a3.astype(wide)).astype(low)
-    return [parts[0], a1, swap(across, W, 2)]
+def sum_w(own, across, pair):
+    got = swap(pair, W, 1)
+    across = (across.astype(wide) + got[0].astype(wide)).astype(low)
+    return [own, got, swap(across, W, 2)], across
 
 
 def exchange_w(parts):
@@ -89,26 +88,18 @@
     return [out[s] for s in range(8)]
 
 
-def sum_e_late(parts, pairs):
-    got = [swap(pair, E, 1) for pair in pairs]
-    terms = []
-    for s, other in ((4, got[0][0]), (6, got[0][1]), (2, got[1][0])):
-        terms.append(swap((parts[s].astype(wide) + other.astype(wide)).astype(low), E, s))
-    return [parts[0], got[1][1]] + terms
-
-
 def sum_e(parts):
     count = lax.axis_size(E)
     if count > 8:
         me = lax.axis_index(E)
         whole = jnp.stack(parts)[me ^ jnp.arange(count, dtype=jnp.int32)]
-        return [lax.psum_scatter(whole, E, scatter_dimension=0)], whole
+        return [lax.psum_scatter(whole, E, scatter_dimension=0)]
     got = {s: swap(parts[s ^ 1], E, 1) for s in (4, 6, 2, 0)}
     terms = [parts[0], got[0]]
     for s in (4, 6, 2):
         part = (parts[s].astype(wide) + got[s].astype(wide)).astype(low)
         terms.append(swap(part, E, s))
-    return terms, part
+    return terms
 
 
 def experts_of(small_rows):
@@ -116,13 +107,21 @@
 
 
 def total_of(refs):
+    rank = len(refs[0].shape)
     out = refs[0][...].astype(wide)
     for ref in refs[1:]:
-        out = out + ref[...].astype(wide)
+        out = out + (ref[...] if len(ref.shape) == rank else ref[1]).astype(wide)
     return out
 
 
-def call(kernel, outs, scratch, cost, scalars, *args, after=(), room=None):
+def store_w(outs, held, me):
+    outs[0][...] = held[me]
+    outs[1][...] = held[me ^ 2]
+    outs[2][0] = held[me ^ 3]
+    outs[2][1] = held[me ^ 1]
+
+
+def call(kernel, outs, scratch, scalars, *args, after=(), room=None, cover=0):
     outs, scratch, after = tuple(outs), tuple(scratch), tuple(after)
     smem = pl.BlockSpec(memory_space=pltpu.SMEM)
     block = pl.BlockSpec()
@@ -137,25 +136,36 @@
         out_specs=tuple(block for _ in outs),
         scratch_shapes=[pltpu.VMEM(s, d) for s, d in scratch],
         compiler_params=pltpu.CompilerParams(vmem_limit_bytes=room or (10 << 20) + size),
-        cost_estimate=pl.CostEstimate(flops=cost[0], bytes_accessed=cost[1], transcendentals=cost[2]),
+        cost_estimate=pl.CostEstimate(flops=1 + cover * 10**9, bytes_accessed=1, transcendentals=0),
     )(*after, scalars, *args)
 
 
-def start_kernel(me_ref, q_ref, k_ref, v_ref, router_ref, one_ref, two_ref, table_ref, up_ref, routes_ref, *rest):
-    outs, sent_ref, held = rest[:SHARDS], rest[SHARDS], rest[SHARDS + 1]
+def tie(value, *after):
+    apart = pl.BlockSpec(memory_space=pl.ANY)
+    return pl.pallas_call(
+        lambda *refs: None,
+        out_shape=jax.ShapeDtypeStruct(value.shape, value.dtype),
+        in_specs=[apart] * (1 + len(after)),
+        out_specs=apart,
+        input_output_aliases={0: 0},
+        compiler_params=pltpu.CompilerParams(vmem_limit_bytes=1 << 20),
+        cost_estimate=pl.CostEstimate(flops=1, bytes_accessed=1, transcendentals=0),
+    )(value, *after)
+
+
+def start_kernel(me_ref, q_ref, k_ref, v_ref, router_ref, one_ref, two_ref, table_ref, *rest):
+    outs, held = rest[:SHARDS], rest[SHARDS]
     shard = q_ref.shape[0]
-    rows = up_ref.shape[0]
     for w in range(SHARDS):
         here = slice(w * shard, (w + 1) * shard)
         held[w] = jnp.concatenate([q_ref[:, here], k_ref[:, here], v_ref[:, here]], axis=1)
-    i = lax.broadcasted_iota(jnp.int32, (shard, shard), 0)
-    j = lax.broadcasted_iota(jnp.int32, (shard, shard), 1)
-    eye = (i == j).astype(low)
+    i = lax.broadcasted_iota(jnp.int32, (table_ref.shape[0], shard), 0)
+    j = lax.broadcasted_iota(jnp.int32, (table_ref.shape[0], shard), 1)
     small = [
         router_ref[...],
         one_ref[...].reshape(1, shard),
         two_ref[...].reshape(1, shard),
-        along_first(table_ref[...], eye[: table_ref.shape[0]]).astype(low),
+        along_first(table_ref[...], (i == j).astype(low)).astype(low),
     ]
     used = sum(piece.shape[0] for piece in small)
     small = jnp.concatenate(small + [jnp.zeros((outs[0].shape[0] - shard - used, shard), low)], axis=0)
@@ -163,19 +173,22 @@
     for s in range(SHARDS):
         outs[s][:shard, :] = held[me_ref[0] ^ s]
         outs[s][shard:, :] = small
+
+
+def sent_kernel(me_ref, up_ref, routes_ref, sent_ref):
+    rows, width = up_ref.shape
     sent_ref[:rows, :] = up_ref[...]
-    named = jnp.concatenate([routes_ref[...].astype(low), jnp.zeros((14, rows), low)], axis=0)
-    sent_ref[rows:, :] = jnp.concatenate([named, jnp.zeros((16, up_ref.shape[1] - rows), low)], axis=1)
+    blocks = jnp.full((1, rows), me_ref[2].astype(wide) / BLOCK).astype(low)
+    named = jnp.concatenate([routes_ref[...].astype(low), blocks, jnp.zeros((13, rows), low)], axis=0)
+    sent_ref[rows:, :] = jnp.concatenate([named, jnp.zeros((16, width - rows), low)], axis=1)
 
 
 def attend_kernel(me_ref, *refs):
     tokens, weights = refs[:SHARDS], refs[SHARDS : 2 * SHARDS]
-    row_ref, column_ref, out_ref = refs[2 * SHARDS : 2 * SHARDS + 3]
-    rest = refs[2 * SHARDS + 3 :]
-    tokens_ref, first_ref, qkv_ref, probs_ref, att_ref, weight_ref, small_ref, router_ref = rest[:8]
-    branches, held_w, held_b = rest[8 : 8 + SHARDS], rest[8 + SHARDS], rest[9 + SHARDS]
+    row_ref, *rest = refs[2 * SHARDS :]
+    tokens_ref, first_ref, qkv_ref, probs_ref, att_ref, weight_ref, small_ref, router_ref, held_w = rest
     me = me_ref[0]
-    shard = out_ref.shape[0]
+    shard = att_ref.shape[1]
     chunk, width = tokens[0].shape
     length = chunk * SHARDS
     heads = probs_ref.shape[0]
@@ -200,7 +213,9 @@
     vectors = along_last(small[experts + 2 : experts + 2 + HEADS], hits)
     i = lax.broadcasted_iota(jnp.int32, (length, length), 0)
     j = lax.broadcasted_iota(jnp.int32, (length, length), 1)
-    allowed = (j <= i) & (row_ref[...] == column_ref[...])
+    marks = jnp.broadcast_to(row_ref[...], (length, length))
+    column = jnp.sum(jnp.where(i == j, marks, 0), axis=1, keepdims=True)
+    allowed = (j <= i) & (marks == column)
     which = lax.broadcasted_iota(jnp.int32, vectors.shape, 0)
 
     rows = tokens_ref[...].reshape(length, width).astype(wide)
@@ -231,13 +246,18 @@
                 probs_ref[h, here, end:] = jnp.zeros((chunk, length - end), low)
             pieces.append(matmul(probs, v[:end]))
         columns.append(jnp.concatenate(pieces, axis=0))
-    attended = jnp.concatenate(columns, axis=1).astype(low)
-    att_ref[...] = attended
-    branch = matmul(attended, out_ref[...]).astype(low)
+    att_ref[...] = jnp.concatenate(columns, axis=1).astype(low)
+
+
+def branch_kernel(me_ref, att_ref, out_ref, *refs):
+    sent, branches, held = refs[:-5], refs[-5:-2], refs[-1]
+    chunk = held.shape[1]
+    for k, ref in enumerate(sent):
+        refs[-2][k] = ref[...]
+    branch = matmul(att_ref[...], out_ref[...]).astype(low)
     for w in range(SHARDS):
-        held_b[w] = branch[w * chunk : (w + 1) * chunk]
-    for s in range(SHARDS):
-        branches[s][...] = held_b[me ^ s]
+        held[w] = branch[w * chunk : (w + 1) * chunk]
+    store_w(branches, held, me_ref[0])
 
 
 def second_kernel(me_ref, tokens_ref, small_ref, *refs):
@@ -253,46 +273,57 @@
 def route_kernel(me_ref, *refs):
     me, limit = me_ref[1], me_ref[2].astype(wide)
     mine = me.astype(wide)
-    sent, (dispatch_ref, rows_ref) = refs[:-2], refs[-2:]
+    sent, (dispatch_ref, partner_ref, rows_ref, last_ref) = refs[:-4], refs[-4:]
+    if len(sent[-1].shape) == 3:
+        sent = [sent[s // 2] if s % 2 == 0 else sent[-1].at[s // 2] for s in range(8)]
     count = len(sent)
     tall = sent[0].shape[0] - 16
-    hits, others = [], []
-    for s in range(count):
-        named = sent[s][tall:, :tall].astype(wide)
-        r0, r1 = named[0:1], named[1:2]
-        hits.append(((r0 == mine) | (r1 == mine)).astype(wide))
-        others.append(jnp.where(r0 == mine, r1, r0))
-    hits = jnp.concatenate(hits, axis=0)
     i = lax.broadcasted_iota(jnp.int32, (tall, tall), 0)
     j = lax.broadcasted_iota(jnp.int32, (tall, tall), 1)
-    within = matmul(hits.astype(low), (i < j).astype(low))
-    counts = jnp.sum(hits, axis=1, keepdims=True)
-    index = me ^ lax.broadcasted_iota(jnp.int32, (count, 1), 0)
+    before = (i < j).astype(low)
     slots = lax.broadcasted_iota(jnp.int32, (CAP, tall), 0).astype(wide)
+    named = [sent[s][tall:, :tall].astype(wide) for s in range(count)]
+
+    def one_hots(expert, limit, wanted):
+        mine = expert.astype(wide)
+        hits = jnp.concatenate([((r[0:1] == mine) | (r[1:2] == mine)).astype(wide) for r in named], axis=0)
+        within = matmul(hits.astype(low), before)
+        counts = jnp.sum(hits, axis=1, keepdims=True)
+        index = me ^ lax.broadcasted_iota(jnp.int32, (count, 1), 0)
+        for s in wanted:
+            base = jnp.sum(jnp.where(index < (me ^ s), counts, 0.0), axis=0, keepdims=True)
+            rank = within[s : s + 1] + base
+            slot = jnp.where((hits[s : s + 1] > 0) & (rank < limit), rank, -1.0)
+            yield s, (slots == slot).astype(low)
+
     packed = jnp.zeros((CAP, rows_ref.shape[1]), wide)
     other = jnp.zeros((16, CAP), wide)
-    for s in range(count):
-        base = jnp.sum(jnp.where(index < (me ^ s), counts, 0.0), axis=0, keepdims=True)
-        rank = within[s : s + 1] + base
-        slot = jnp.where((hits[s : s + 1] > 0) & (rank < limit), rank, -1.0)
-        one_hot = (slots == slot).astype(low)
+    mine = me.astype(wide)
+    for s, one_hot in one_hots(me, limit, range(count)):
         dispatch_ref[:, s * tall : (s + 1) * tall] = one_hot
         packed = packed + matmul(one_hot, sent[s][:tall, :])
-        other = other + along_last(jnp.broadcast_to(others[s], (16, tall)).astype(low), one_hot)
-    rows_ref[:CAP, :] = packed.astype(low)
+        name = jnp.where(named[s][0:1] == mine, named[s][1:2], named[s][0:1])
+        other = other + along_last(jnp.broadcast_to(name, (16, tall)).astype(low), one_hot)
+    half = rows_ref.shape[0]
+    rows_ref[...] = packed[:half].astype(low)
+    last_ref[: CAP - half, :] = packed[half:].astype(low)
     tail = jnp.zeros((16, rows_ref.shape[1] - CAP), low)
-    rows_ref[CAP:, :] = jnp.concatenate([other.astype(low), tail], axis=1)
+    last_ref[CAP - half :, :] = jnp.concatenate([other.astype(low), tail], axis=1)
+    for s, one_hot in one_hots(me ^ 1, named[1][2:3] * BLOCK, range(0, count, 2)):
+        partner_ref[:, s // 2 * tall : (s // 2 + 1) * tall] = one_hot
 
 
 def upstream_kernel(me_ref, weight_ref, *refs):
-    rows, backs, choices = refs[:SHARDS], refs[SHARDS : 2 * SHARDS], refs[2 * SHARDS :]
+    rows, backs, choices = refs[: 2 * SHARDS], refs[2 * SHARDS : 3 * SHARDS], refs[3 * SHARDS :]
+    half = rows[0].shape[0]
     mine = me_ref[1].astype(wide)
     i = lax.broadcasted_iota(jnp.int32, (CAP, CAP), 0)
     j = lax.broadcasted_iota(jnp.int32, (CAP, CAP), 1)
     lane = lax.broadcasted_iota(jnp.int32, (CAP, LANES), 1).astype(wide)
     for k in range(SHARDS):
-        backs[k][...] = along_last(rows[k][:CAP, :], weight_ref[...])
-        across = rows[k][CAP:, :CAP].astype(wide)[0:1]
+        backs[k][:half, :] = along_last(rows[2 * k][...], weight_ref[...])
+        backs[k][half:, :] = along_last(rows[2 * k + 1][: CAP - half, :], weight_ref[...])
+        across = rows[2 * k + 1][CAP - half :, :CAP].astype(wide)[0:1]
         other = jnp.sum(jnp.where(i == j, across, 0.0), axis=1, keepdims=True)
         choices[k][...] = (lane == mine).astype(wide) - (lane == other).astype(wide)
 
@@ -332,38 +363,33 @@
 
 
 def result_kernel(order, me_ref, weight_ref, act_a, act_b, logits_a, logits_b, *refs):
-    rows, outs, router_ref = refs[:SHARDS], refs[SHARDS:-1], refs[-1]
+    rows, (own_ref, across_ref, pair_ref, router_ref) = refs[:SHARDS], refs[SHARDS:]
     router = jnp.zeros(router_ref.shape, wide)
     for k, s in enumerate(order):
         here = slice((k % 2) * CAP, (k % 2 + 1) * CAP)
-        outs[s][...] = matmul((act_a, act_b)[k // 2][here, :], weight_ref[...]).astype(low)
+        result = matmul((act_a, act_b)[k // 2][here, :], weight_ref[...]).astype(low)
+        if s % 2 == 0:
+            (own_ref, across_ref)[s // 2][...] = result
+        else:
+            pair_ref[(3 - s) // 2] = result
         router = router + along_first(rows[s][...], (logits_a, logits_b)[k // 2][here, :])
     router_ref[...] = router
 
 
-def unpack_late_kernel(me_ref, dispatch_ref, *refs):
-    terms, outs, pairs = refs[:3], refs[3:-2], refs[-2:]
-    block = total_of(terms).astype(low)
-    tall = outs[0].shape[0]
-    for k, s in enumerate((4, 6, 2, 0)):
-        outs[s // 2][...] = along_first(dispatch_ref[:, s * tall : (s + 1) * tall], block).astype(low)
-        other = dispatch_ref[:, (s + 1) * tall : (s + 2) * tall]
-        pairs[k // 2][k % 2] = along_first(other, block).astype(low)
-
-
 def layer_kernel(me_ref, resid_ref, *refs):
     refs[-1][...] = (resid_ref[...] + total_of(refs[:-1])).astype(low)
 
 
 def grads_kernel(order, me_ref, *refs):
     acts, pres = refs[0:2], refs[2:4]
-    rows, ups = refs[4 : 4 + SHARDS], refs[4 + SHARDS : 4 + 2 * SHARDS]
-    first_ref, second_ref = refs[4 + 2 * SHARDS :]
+    rows, ups = refs[4 : 4 + SHARDS], refs[4 + SHARDS : 4 + 3 * SHARDS]
+    first_ref, second_ref = refs[4 + 3 * SHARDS :]
     acts = jnp.concatenate([ref[...] for ref in acts], axis=0)
     pres = jnp.concatenate([ref[...] for ref in pres], axis=0)
     block = jnp.concatenate([rows[s][...] for s in order], axis=0)
     first_ref[0] = along_first(pres, block)
-    ups = jnp.concatenate([ups[s][:CAP, :] for s in order], axis=0)
+    half = CAP - ups[0].shape[0]
+    ups = jnp.concatenate([ref[...] for s in order for ref in (ups[2 * s], ups[2 * s + 1].at[:half])], axis=0)
     second_ref[0] = along_first(acts, ups)
 
 
@@ -373,6 +399,18 @@
     tall = outs[0].shape[0]
     for s, ref in enumerate(outs):
         ref[...] = along_first(dispatch_ref[:, s * tall : (s + 1) * tall], block).astype(low)
+
+
+def total_kernel(me_ref, *refs):
+    refs[-1][...] = total_of(refs[:-1]).astype(low)
+
+
+def unpack_both_kernel(me_ref, dispatch_ref, partner_ref, block_ref, other_ref, *outs):
+    tall = outs[0].shape[0]
+    for k, ref in enumerate(outs):
+        own = along_first(dispatch_ref[:, 2 * k * tall : (2 * k + 1) * tall], block_ref[...])
+        other = along_first(partner_ref[:, k * tall : (k + 1) * tall], other_ref[...])
+        ref[...] = (own + other).astype(low)
 
 
 def resid_back_kernel(me_ref, resid_ref, small_ref, cotangent_ref, *refs):
@@ -405,8 +443,8 @@
     router_ref,
     *refs,
 ):
-    ups, backs = refs[:SHARDS], refs[SHARDS : 2 * SHARDS]
-    parts, (held, table) = refs[2 * SHARDS : -2], refs[-2:]
+    ups, backs = refs[:SHARDS], refs[SHARDS : SHARDS + 3]
+    parts, (held, table) = refs[SHARDS + 3 : -2], refs[-2:]
     me = me_ref[0]
     shard = out_ref.shape[0]
     chunk, width = ups[0].shape
@@ -450,8 +488,7 @@
     rows = rows * lax.rsqrt(jnp.mean(rows * rows, axis=-1, keepdims=True) + epsilon)
     for w in range(SHARDS):
         held[w] = back_first[w * chunk : (w + 1) * chunk].astype(low)
-    for s in range(SHARDS):
-        backs[s][...] = held[me ^ s]
+    store_w(backs, held, me)
 
     gains = [jnp.sum(back_first * rows, axis=0, keepdims=True), gain_two_ref[...]]
     gains = jnp.concatenate(gains + [jnp.zeros((14, width), wide)], axis=0).astype(low)
@@ -576,29 +613,36 @@
     first_local, second_local = expert_in[0], expert_out[0]
     row = (rows, width)
     packed_row = (CAP, width)
+    three_rows = [(row, low), (row, low), ((2,) + row, low)]
 
     quick = experts == 8
     small_rows = -(-(experts + 2 + HEADS) // 16) * 16
     tokens_rel = gather_w(tokens)
-    *weight_parts, sent = call(
-        start_kernel,
-        [((shard + small_rows, 3 * shard), low)] * SHARDS + [((rows + 16, width), low)],
-        [((SHARDS, shard, 3 * shard), low)],
-        (0, 4 * shard * width * 3, 0),
-        me,
-        query_weight,
-        key_weight,
-        value_weight,
-        router_weight.T,
-        attention_gain,
-        feed_gain,
-        position_bias,
+    weight_rel = exchange_w(
+        call(
+            start_kernel,
+            [((shard + small_rows, 3 * shard), low)] * SHARDS,
+            [((SHARDS, shard, 3 * shard), low)],
+            me,
+            query_weight,
+            key_weight,
+            value_weight,
+            router_weight.T,
+            attention_gain,
+            feed_gain,
+            position_bias,
+            room=FULL,
+        )
+    )
+    (sent,) = call(
+        sent_kernel,
+        [((rows + 16, width), low)],
+        [],
+        me,
         cotangent,
         routes.T,
-        room=FULL,
-    )
-    weight_rel = exchange_w(weight_parts)
-    sent = gather_e(sent)
+    )
+    sent = [sent, swap(sent, E, 2), swap(sent, E, 4), swap(sent, E, 6)] if quick else gather_e(sent)
 
     square = (own_heads, length, length)
     outs = call(
@@ -612,48 +656,63 @@
             ((width, 3 * shard), low),
             ((small_rows, width), low),
             ((LANES, width), low),
-        ]
-        + [(row, low)] * SHARDS,
-        [((SHARDS, shard + small_rows, 3 * shard), low), ((SHARDS, rows, width), low)],
-        (2 * length * width * 4 * shard, 8 * length * length * own_heads, own_heads * length * length),
+        ],
+        [((SHARDS, shard + small_rows, 3 * shard), low)],
         me,
         *tokens_rel,
         *weight_rel,
         segments,
-        segments.reshape(length, 1),
+        room=FULL,
+        cover=20,
+    )
+    tokens_all, first, qkv, probs, attended, weight, small, router = outs
+    near_sent = sent if quick else sent[:4]
+    *branches, stacked = call(
+        branch_kernel,
+        three_rows + [((len(near_sent), rows + 16, width), low)],
+        [((SHARDS, rows, width), low)],
+        me,
+        attended,
         output_weight,
-        room=FULL,
-    )
-    tokens_all, first, qkv, probs, attended, weight, small, router = outs[:8]
+        *near_sent,
+    )
+    branch_terms, _ = sum_w(*branches)
     resid, second = call(
         second_kernel,
         [(row, wide), (row, low)],
         [],
-        (0, 8 * rows * width, 0),
         me,
         tokens,
         small,
-        *sum_w(outs[8:]),
-    )
-
-    dispatch, upstream_rows = call(
+        *branch_terms,
+    )
+
+    second_rel = gather_e(second)
+
+    if quick:
+        sent.append(swap(stacked, E, 1))
+    dispatch, partner, *upstream_rows = call(
         route_kernel,
-        [((CAP, experts * rows), low), ((CAP + 16, width), low)],
+        [
+            ((CAP, experts * rows), low),
+            ((CAP, experts * rows // 2), low),
+            ((CAP // 2, width), low),
+            ((CAP // 2 + 16, width), low),
+        ],
         [],
-        (2 * CAP * experts * rows * width, 4 * experts * rows * width, 0),
         me,
         *sent,
-    )
-    upstream_rel = gather_w(upstream_rows)
-    order = (3, 2, 1, 0)
+        after=(second,),
+    )
+    upstream_rel = list(zip(gather_w(upstream_rows[0]), gather_w(upstream_rows[1])))
+    order = (0, 1, 2, 3)
     outs = call(
         upstream_kernel,
         [(packed_row, wide)] * SHARDS + [((CAP, LANES), wide)] * SHARDS,
         [],
-        (2 * SHARDS * CAP * width * width, 4 * SHARDS * CAP * width, 0),
         me,
         second_local,
-        *[upstream_rel[s] for s in order],
+        *[piece for s in order for piece in upstream_rel[s]],
     )
     back_act, choice = outs[:SHARDS], outs[SHARDS:]
 
@@ -661,13 +720,11 @@
         pack_kernel,
         [(packed_row, low)],
         [],
-        (2 * CAP * experts * rows * width, 4 * experts * rows * width, 0),
         me,
         dispatch,
-        *gather_e(second),
-        after=(back_act[0],),
-    )
-    rows_rel = gather_w(packed)
+        *second_rel,
+        after=upstream_rel[2],
+    )
     half = (2 * CAP, width)
 
     def expert_half(k, after):
@@ -675,7 +732,6 @@
             expert_kernel,
             [(packed_row, low)] * 2 + [(half, low), (half, low), ((2 * CAP, LANES), low)],
             [],
-            (8 * CAP * width * width, 8 * CAP * width, 2 * CAP * width),
             me,
             back_act[2 * k],
             back_act[2 * k + 1],
@@ -688,29 +744,30 @@
             after=after,
         )
 
+    far = swap(packed, W, 2)
+    rows_rel = [packed, swap(packed, W, 1)]
     halves = [expert_half(0, ())]
-    near = swap(halves[0][0], W, 1)
-    across = (halves[0][1].astype(wide) + near.astype(wide)).astype(low)
-    halves.append(expert_half(1, (across,)))
-    far = swap(across, W, 2)
+    far = tie(far, halves[0][0])
+    rows_rel = rows_rel + [far, swap(far, W, 1)]
+    halves.append(expert_half(1, ()))
+    near = swap(halves[1][1], W, 1)
+    across = (halves[1][0].astype(wide) + near.astype(wide)).astype(low)
     back_parts = call(
         unpack_kernel,
         [(row, low)] * experts,
         [],
-        (2 * CAP * experts * rows * width, 4 * experts * rows * width, 0),
         me,
         dispatch,
-        halves[1][1],
-        swap(halves[1][0], W, 1),
-        far,
-    )
-    back_terms, tie = sum_e(back_parts)
+        halves[0][0],
+        swap(halves[0][1], W, 1),
+        swap(across, W, 2),
+    )
+    back_terms = sum_e(back_parts)
 
     *results, router_grad = call(
         lambda *refs: result_kernel(order, *refs),
-        [(packed_row, low)] * SHARDS + [((width, LANES), wide)],
+        [(packed_row, low), (packed_row, low), ((2,) + packed_row, low), ((width, LANES), wide)],
         [],
-        (8 * CAP * width * width, 8 * CAP * width, 0),
         me,
         second_local,
         halves[0][2],
@@ -718,56 +775,39 @@
         halves[0][4],
         halves[1][4],
         *rows_rel,
-        after=(back_parts[0],),
-    )
-    result_terms = sum_w(results)
+        after=(across,),
+    )
+    result_terms, _ = sum_w(*results)
+    if quick:
+        (mixed,) = call(total_kernel, [(packed_row, low)], [], me, *result_terms)
+        mixed_parts = call(
+            unpack_both_kernel, [(row, low)] * 4, [], me, dispatch, partner, mixed, swap(mixed, E, 1)
+        )
+        mixed_terms = [mixed_parts[0]] + [swap(mixed_parts[s // 2], E, s) for s in (4, 6, 2)]
+    else:
+        mixed_parts = call(unpack_kernel, [(row, low)] * experts, [], me, dispatch, *result_terms)
+        mixed_terms = sum_e(mixed_parts)
 
     back_resid, back_branch, gain_two_grad = call(
         resid_back_kernel,
         [(row, wide), (row, low), ((1, width), wide)],
         [],
-        (0, 16 * rows * width, 0),
         me,
         resid,
         small,
         cotangent,
         *back_terms,
+        after=(mixed_parts[0],),
     )
     back_rel = gather_w(back_branch)
-    if quick:
-        outs = call(
-            unpack_late_kernel,
-            [(row, low)] * 4 + [((2,) + row, low)] * 2,
-            [],
-            (2 * CAP * experts * rows * width, 4 * experts * rows * width, 0),
-            me,
-            dispatch,
-            *result_terms,
-            after=(tie,),
-        )
-        mixed_terms = sum_e_late(dict(zip((0, 2, 4, 6), outs[:4])), outs[4:])
-    else:
-        mixed_parts = call(
-            unpack_kernel,
-            [(row, low)] * experts,
-            [],
-            (2 * CAP * experts * rows * width, 4 * experts * rows * width, 0),
-            me,
-            dispatch,
-            *result_terms,
-        )
-        mixed_terms, _ = sum_e(mixed_parts)
-    (layer_out,) = call(
-        layer_kernel, [(row, low)], [], (0, 16 * rows * width, 0), me, resid, *mixed_terms
-    )
     columns = 3 * shard + LANES
     piece = shard // experts
     part = (SHARDS, piece, columns + shard)
     outs = call(
         lambda *refs: attend_back_kernel(experts, table_rows, *refs),
-        [(row, low)] * SHARDS + ([(part, low)] * experts if quick else [((width, columns + shard), low)]),
+        three_rows
+        + ([(part, low)] * experts if quick else [((width, columns + shard), low)]),
         [((SHARDS, rows, width), low), ((width, columns + shard), wide)],
-        (2 * length * width * 9 * shard, 8 * length * length * own_heads, 0),
         me,
         output_weight,
         qkv,
@@ -779,43 +819,44 @@
         gain_two_grad,
         router_grad,
         *back_rel,
-        after=(mixed_terms[0],),
-    )
-    grads = outs[SHARDS:]
+        cover=20,
+    )
+    grads = list(outs[3:])
+    (layer_out,) = call(layer_kernel, [(row, low)], [], me, resid, *mixed_terms, after=(grads[0],))
+    if quick:
+        grads[5] = tie(grads[5], layer_out)
+    back_terms, _ = sum_w(*outs[:3])
     (tokens_grad,) = call(
         tokens_back_kernel,
         [(row, wide)],
         [],
-        (0, 16 * rows * width, 0),
         me,
         tokens,
         small,
         back_resid,
-        *sum_w(outs[:SHARDS]),
+        *back_terms,
     )
 
     first_grad, second_grad = call(
         lambda *refs: grads_kernel(order, *refs),
         [((1,) + first_local.shape, wide), ((1,) + second_local.shape, wide)],
         [],
-        (16 * CAP * width * width, 24 * CAP * width, 0),
         me,
         halves[0][2],
         halves[1][2],
         halves[0][3],
         halves[1][3],
         *rows_rel,
-        *upstream_rel,
-        after=(grads[0],),
+        *[piece for pieces in upstream_rel for piece in pieces],
+        after=(grads[-1],),
     )
 
     if quick:
-        terms, _ = sum_e(grads)
+        terms = sum_e(grads)
         *grads, output_grad = call(
             join_kernel,
             [((piece, columns), low)] * SHARDS + [((piece, width), low)],
             [((SHARDS, piece, columns), wide)],
-            (0, 8 * width * columns, 0),
             me,
             *terms,
         )
@@ -823,7 +864,6 @@
             lambda *refs: order_kernel(experts, *refs),
             [((piece, 4 * width + LANES), low)],
             [((SHARDS, piece, columns), wide)],
-            (0, 8 * width * columns, 0),
             me,
             *exchange_w(grads),
             output_grad,
@@ -835,7 +875,6 @@
             + [((1, shard), wide)] * 2
             + [((shard, experts), wide), ((table_rows, HEADS), wide)],
             [((shard, LANES), wide)],
-            (0, 16 * shard * width, 0),
             me,
             *gather_e(grads),
         )

time: 268 us -> 232 us (0.87)
  waiting for transfers between devices: 135 us -> 103 us
  starting transfers between devices: 77.9 us -> 67.5 us
  Pallas kernels: 48.6 us -> 52.1 us
    ppermute x70 -> x66, waiting for transfers between devices: 135 us -> 103 us  [swap(): return lax.ppermute(value, axis, [(i, i ^ step) for i in range(count)])]
    ppermute x70 -> x66, starting transfers between devices: 77.9 us -> 67.5 us  [swap(): return lax.ppermute(value, axis, [(i, i ^ step) for i in range(count)])]
    unnamed x49 -> x51, local copies, waits for them, and re-layouts: 1.4 us -> 5.6 us
    pallas_call x19 -> x22, Pallas kernels: 48.6 us -> 52.1 us  [call(): pl.pallas_call(lambda *refs: kernel(*refs[skip:]), out_shape=tuple((jax.S...]
  transfers between devices with their start and end apart: 70 -> 66, of which waited for: 30 -> 33; matrix products, arithmetic and copies ran while one was open for 1% -> 0% of each run, Pallas kernels for 11% -> 17%
where the time goes in v1:
time: 232 us; the launch traced here: 231 us
  waiting for transfers between devices  103 us (44%)
  starting transfers between devices  67.5 us (29%)
  Pallas kernels  52.1 us (22%)
  local copies, waits for them, and re-layouts  5.6 us (2%)
    ppermute x66, waiting for transfers between devices, swap(): return lax.ppermute(value, axis, [(i, i ^ step) for i in range(count)])  103 us
    ppermute x66, starting transfers between devices, swap(): return lax.ppermute(value, axis, [(i, i ^ step) for i in range(count)])  67.5 us
    pallas_call x22, Pallas kernels, call(): pl.pallas_call(lambda *refs: kernel(*refs[skip:]), out_shape=tuple((jax.S...  52.1 us
    unnamed x51, local copies, waits for them, and re-layouts  5.6 us
  transfers between devices with their start and end apart: 66, of which 33 were waited for; matrix products, arithmetic and copies ran while one was open for 0% of the time, Pallas kernels for 17%

profile of v1, /device:TPU:0, one launch (start us, length us, event | category | flops | bytes accessed | tf_op | source)
XLA Modules:
  0.0 231.4 jit_solution(11008182310829638123)
XLA Ops:
  0.6 3.0 %collective-permute-start.1 = (bf16[128,768]{1,0:T(8,128)(2,1)}, bf16[128,768]{1,0:T(8,128)(2,1)S(1)}, u32[]{:S(2)}, u32[]{:S(2)}) collective-permute-start(bf16[128,768]{1,0:T(8,128)(2,1)} %refs_1_.11), channel_id=1, source_target_pairs={{0,2},{1,3},{2,0},{3,1},{4,6},{5,7},{6,4},{7,5},{8,10},{9,11},{10,... | collective-permute-start | bytes 589832 | tf_op jit(solution)/shard_map/ppermute | solution.py:49
  4.9 2.4 %shard_map.238 = (bf16[224,576]{1,0:T(8,128)(2,1)}, bf16[224,576]{1,0:T(8,128)(2,1)}, bf16[224,576]{1,0:T(8,128)(2,1)}, bf16[224,576]{1,0:T(8,128)(2,1)}) custom-call(s32[3]{0:T(128)} %pad_add_fusion.refs_0_.refs_1_.refs_2_, bf16[192,768]{1,0:T(8,128)(2,1)} %refs_1_.6, bf16[192,768]{1,0:T(8,128)(2,1)} %refs_2_.2, bf16[192,768]{1,0:T(8,128)(2,1)} %refs_3_.1, ...), custom_call_target="tpu_custom_call" | custom-call | flops 1 | bytes 1 | tf_op jit(solution)/shard_map/pallas_call | solution.py:132
  7.3 1.8 collective-permute-start.5
  12.6 3.7 %collective-permute-start.8 = (bf16[144,768]{1,0:T(8,128)(2,1)S(1)}, bf16[144,768]{1,0:T(8,128)(2,1)S(1)}, u32[]{:S(2)}, u32[]{:S(2)}) collective-permute-start(bf16[144,768]{1,0:T(8,128)(2,1)S(1)} %shard_map.240.refs_3_.refs_2_), channel_id=1, source_target_pairs={{0,24},{4,28},{8,16},{12,20},{16,8},{20,12},{24,0},{28,4},{1,25},{... | collective-permute-start | bytes 663560 | tf_op jit(solution)/shard_map/ppermute | solution.py:49
  17.2 1.6 collective-permute-start.6
  18.7 3.8 %collective-permute-done.5.refs_8_ = bf16[224,576]{1,0:T(8,128)(2,1)S(1)} collective-permute-done((bf16[224,576]{1,0:T(8,128)(2,1)}, bf16[224,576]{1,0:T(8,128)(2,1)S(1)}, u32[]{:S(2)}, u32[]{:S(2)}) %collective-permute-start.5) | collective-permute-done | bytes 258080 | tf_op jit(solution)/shard_map/ppermute | solution.py:49
  23.3 8.0 %shard_map.239 = (bf16[4,128,768]{2,1,0:T(8,128)(2,1)}, bf16[512,768]{1,0:T(8,128)(2,1)}, bf16[512,576]{1,0:T(8,128)(2,1)}, bf16[3,512,512]{2,1,0:T(8,128)(2,1)}...) custom-call(s32[3]{0:T(128)} %pad_add_fusion.refs_0_.refs_1_.refs_2_,, ...), custom_call_target="tpu_custom_call" | custom-call | flops 20000000000 | bytes 1 | tf_op jit(solution)/shard_map/pallas_call | solution.py:132
  31.3 4.2 %collective-permute-done.7.refs_5_.refs_4_ = bf16[144,768]{1,0:T(8,128)(2,1)S(1)} collective-permute-done((bf16[144,768]{1,0:T(8,128)(2,1)S(1)}, bf16[144,768]{1,0:T(8,128)(2,1)S(1)}, u32[]{:S(2)}, u32[]{:S(2)}) %collective-permute-start.7) | collective-permute-done | bytes 221216 | tf_op jit(solution)/shard_map/ppermute | solution.py:49
  37.5 1.6 collective-permute-start.11
  40.4 5.9 %collective-permute-done.10.refs_5_ = bf16[128,768]{1,0:T(8,128)(2,1)S(1)} collective-permute-done((bf16[128,768]{1,0:T(8,128)(2,1)S(1)}, bf16[128,768]{1,0:T(8,128)(2,1)S(1)}, u32[]{:S(2)}, u32[]{:S(2)}) %collective-permute-start.10) | collective-permute-done | bytes 196640 | tf_op jit(solution)/shard_map/ppermute | solution.py:49
  47.1 2.5 %collective-permute-start.23 = (bf16[128,768]{1,0:T(8,128)(2,1)S(1)}, bf16[128,768]{1,0:T(8,128)(2,1)S(1)}, u32[]{:S(2)}, u32[]{:S(2)}) collective-permute-start(bf16[128,768]{1,0:T(8,128)(2,1)S(1)} %get-tuple-element.111.refs_0_.refs_4_), channel_id=1, source_target_pairs={{0,24},{4,28},{8,16},{12,20},{16,8},{20,12},{24,0},{28,4},{1,25},{... | collective-permute-start | bytes 589832 | tf_op jit(solution)/shard_map/ppermute | solution.py:49
  49.6 1.9 collective-permute-start.19
  51.5 1.5 collective-permute-start.18
  53.0 7.0 %collective-permute-done.11.refs_6_ = bf16[4,144,768]{2,1,0:T(8,128)(2,1)S(1)} collective-permute-done((bf16[4,144,768]{2,1,0:T(8,128)(2,1)S(1)}, bf16[4,144,768]{2,1,0:T(8,128)(2,1)S(1)}, u32[]{:S(2)}, u32[]{:S(2)}) %collective-permute-start.11) | collective-permute-done | bytes 884768 | tf_op jit(solution)/shard_map/ppermute | solution.py:49
  60.0 1.8 shard_map.243
  63.0 1.5 collective-permute-start.24
  65.0 1.5 collective-permute-start.22
  68.0 2.8 %collective-permute-done.24.refs_11_ = bf16[128,768]{1,0:T(8,128)(2,1)S(1)} collective-permute-done((bf16[128,768]{1,0:T(8,128)(2,1)S(1)}, bf16[128,768]{1,0:T(8,128)(2,1)S(1)}, u32[]{:S(2)}, u32[]{:S(2)}) %collective-permute-start.24) | collective-permute-done | bytes 196640 | tf_op jit(solution)/shard_map/ppermute | solution.py:49
  70.8 4.2 %collective-permute-done.22.refs_9_ = bf16[128,768]{1,0:T(8,128)(2,1)S(1)} collective-permute-done((bf16[128,768]{1,0:T(8,128)(2,1)S(1)}, bf16[128,768]{1,0:T(8,128)(2,1)S(1)}, u32[]{:S(2)}, u32[]{:S(2)}) %collective-permute-start.22) | collective-permute-done | bytes 196640 | tf_op jit(solution)/shard_map/ppermute | solution.py:49
  75.0 2.1 collective-permute-done.20.refs_7_
  77.1 1.5 shard_map.245.refs_7_.refs_6_
  81.9 3.7 %shard_map.244 = (f32[256,768]{1,0:T(8,128)S(1)}, f32[256,768]{1,0:T(8,128)S(1)}, f32[256,768]{1,0:T(8,128)S(1)}, f32[256,768]{1,0:T(8,128)S(1)}, f32[256,128]{1...) custom-call(s32[3]{0:T(128)S(1)} %copy-done.12, ...), custom_call_target="tpu_custom_call" | custom-call | flops 1 | bytes 1 | tf_op jit(solution)/shard_map/pallas_call | solution.py:132
  85.6 4.2 %shard_map.246 = (bf16[256,768]{1,0:T(8,128)(2,1)S(1)}, bf16[256,768]{1,0:T(8,128)(2,1)S(1)}, bf16[512,768]{1,0:T(8,128)(2,1)S(1)}, bf16[512,768]{1,0:T(8,128)(2,1)S(1)}, bf16[512,128]{1,0:T(8,128)(2,1)S(1)}) custom-call(s32[3]{0:T(128)S(1)} %copy-done.12, f32[256,768]{1,0:T(8,128)S(1)} %get-tuple-element.122.refs_1_, ...), custom_call_target="tpu_custom_call" | custom-call | flops 1 | bytes 1 | tf_op jit(solution)/shard_map/pallas_call | solution.py:132
  90.3 1.7 collective-permute-done.27.refs_8_.refs_10_.refs_9_
  92.0 4.0 %shard_map.248 = (bf16[256,768]{1,0:T(8,128)(2,1)S(1)}, bf16[256,768]{1,0:T(8,128)(2,1)S(1)}, bf16[512,768]{1,0:T(8,128)(2,1)S(1)}, bf16[512,768]{1,0:T(8,128)(2,1)S(1)}, bf16[512,128]{1,0:T(8,128)(2,1)S(1)}) custom-call(s32[3]{0:T(128)S(1)} %copy-done.12, f32[256,768]{1,0:T(8,128)S(1)} %get-tuple-element.117.refs_1_, ...), custom_call_target="tpu_custom_call" | custom-call | flops 1 | bytes 1 | tf_op jit(solution)/shard_map/pallas_call | solution.py:132
  96.2 1.6 collective-permute-done.28
  97.9 2.4 %shard_map.249 = (bf16[256,768]{1,0:T(8,128)(2,1)S(1)}, bf16[256,768]{1,0:T(8,128)(2,1)S(1)}, bf16[2,256,768]{2,1,0:T(8,128)(2,1)S(1)}, f32[768,128]{1,0:T(8,128)S(1)}) custom-call(bf16[256,768]{1,0:T(8,128)(2,1)S(1)} %add_convert_fusion.refs_0_, s32[3]{0:T(128)S(1)} %copy-done.12, bf16[768,768]{1,0:T(8,128)(2,1)S(1)} %bitcast.24, ...), custom_call_target="tpu_custom_call" | custom-call | flops 1 | bytes 1 | tf_op jit(solution)/shard_map/pallas_call | solution.py:132
  101.8 1.3 collective-permute-done.32.refs_3_
  103.2 8.8 %collective-permute-done.33.refs_4_ = bf16[256,768]{1,0:T(8,128)(2,1)S(1)} collective-permute-done((bf16[256,768]{1,0:T(8,128)(2,1)S(1)}, bf16[256,768]{1,0:T(8,128)(2,1)S(1)}, u32[]{:S(2)}, u32[]{:S(2)}) %collective-permute-start.33) | collective-permute-done | bytes 393248 | tf_op jit(solution)/shard_map/ppermute | solution.py:49
  112.0 1.2 shard_map.252
  113.2 1.6 collective-permute-start.34
  115.3 1.5 collective-permute-start.37
  118.5 6.8 %collective-permute-done.35 = bf16[128,768]{1,0:T(8,128)(2,1)S(1)} collective-permute-done((bf16[128,768]{1,0:T(8,128)(2,1)S(1)}, bf16[128,768]{1,0:T(8,128)(2,1)S(1)}, u32[]{:S(2)}, u32[]{:S(2)}) %collective-permute-start.35) | collective-permute-done | bytes 196640 | tf_op jit(solution)/shard_map/ppermute | solution.py:49
  125.5 4.1 %collective-permute-done.37 = bf16[128,768]{1,0:T(8,128)(2,1)S(1)} collective-permute-done((bf16[128,768]{1,0:T(8,128)(2,1)S(1)}, bf16[128,768]{1,0:T(8,128)(2,1)S(1)}, u32[]{:S(2)}, u32[]{:S(2)}) %collective-permute-start.37) | collective-permute-done | bytes 196640 | tf_op jit(solution)/shard_map/ppermute | solution.py:49
  129.6 2.5 %collective-permute-start.38 = (bf16[128,768]{1,0:T(8,128)(2,1)S(1)}, bf16[128,768]{1,0:T(8,128)(2,1)S(1)}, u32[]{:S(2)}, u32[]{:S(2)}) collective-permute-start(bf16[128,768]{1,0:T(8,128)(2,1)S(1)} %add_convert_fusion.2), channel_id=1, source_target_pairs={{0,24},{4,28},{8,16},{12,20},{16,8},{20,12},{24,0},{28,4},{1,25},{... | collective-permute-start | bytes 589832 | tf_op jit(solution)/shard_map/ppermute | solution.py:49
  132.9 1.6 collective-permute-start.31
  134.6 6.1 %collective-permute-done.31.refs_4_ = bf16[256,768]{1,0:T(8,128)(2,1)S(1)} collective-permute-done((bf16[256,768]{1,0:T(8,128)(2,1)S(1)}, bf16[256,768]{1,0:T(8,128)(2,1)S(1)}, u32[]{:S(2)}, u32[]{:S(2)}) %collective-permute-start.31) | collective-permute-done | bytes 393248 | tf_op jit(solution)/shard_map/ppermute | solution.py:49
  140.7 1.1 shard_map.251
  144.3 4.7 %collective-permute-done.42.refs_12_ = bf16[128,768]{1,0:T(8,128)(2,1)S(1)} collective-permute-done((bf16[128,768]{1,0:T(8,128)(2,1)S(1)}, bf16[128,768]{1,0:T(8,128)(2,1)S(1)}, u32[]{:S(2)}, u32[]{:S(2)}) %collective-permute-start.42) | collective-permute-done | bytes 196640 | tf_op jit(solution)/shard_map/ppermute | solution.py:49
  149.4 2.5 %collective-permute-start.45 = (bf16[128,768]{1,0:T(8,128)(2,1)S(1)}, bf16[128,768]{1,0:T(8,128)(2,1)S(1)}, u32[]{:S(2)}, u32[]{:S(2)}) collective-permute-start(bf16[128,768]{1,0:T(8,128)(2,1)S(1)} %get-tuple-element.152), channel_id=1, source_target_pairs={{0,24},{4,28},{8,16},{12,20},{16,8},{20,12},{24,0},{28,4},{1,25},{... | collective-permute-start | bytes 589832 | tf_op jit(solution)/shard_map/ppermute | solution.py:49
  152.5 6.7 %shard_map.254 = (bf16[128,768]{1,0:T(8,128)(2,1)S(1)}, bf16[128,768]{1,0:T(8,128)(2,1)S(1)}, bf16[2,128,768]{2,1,0:T(8,128)(2,1)S(1)}, bf16[4,24,896]{2,1,0:T(8...) custom-call(s32[3]{0:T(128)S(1)} %copy-done.12, ...), custom_call_target="tpu_custom_call" | custom-call | flops 20000000000 | bytes 1 | tf_op jit(solution)/shard_map/pallas_call | solution.py:132
  159.2 6.5 %collective-permute-done.44.refs_4_ = bf16[128,768]{1,0:T(8,128)(2,1)S(1)} collective-permute-done((bf16[128,768]{1,0:T(8,128)(2,1)S(1)}, bf16[128,768]{1,0:T(8,128)(2,1)S(1)}, u32[]{:S(2)}, u32[]{:S(2)}) %collective-permute-start.44) | collective-permute-done | bytes 196640 | tf_op jit(solution)/shard_map/ppermute | solution.py:49
  165.7 1.3 collective-permute-done.46.refs_6_
  166.9 1.3 shard_map.255.refs_1_
  169.2 1.5 collective-permute-start.50
  171.2 1.5 collective-permute-start.54
  173.3 3.3 %collective-permute-done.50 = bf16[4,24,896]{2,1,0:T(8,128)(2,1)S(1)} collective-permute-done((bf16[4,24,896]{2,1,0:T(8,128)(2,1)S(1)}, bf16[4,24,896]{2,1,0:T(8,128)(2,1)S(1)}, u32[]{:S(2)}, u32[]{:S(2)}) %collective-permute-start.50) | collective-permute-done | bytes 172064 | tf_op jit(solution)/shard_map/ppermute | solution.py:49
  176.6 3.3 %collective-permute-start.51 = (bf16[4,24,896]{2,1,0:T(8,128)(2,1)S(1)}, bf16[4,24,896]{2,1,0:T(8,128)(2,1)S(1)}, u32[]{:S(2)}, u32[]{:S(2)}) collective-permute-start(bf16[4,24,896]{2,1,0:T(8,128)(2,1)S(1)} %add_convert_fusion.6), channel_id=1, source_target_pairs={{0,16},{4,20},{8,24},{12,28},{16,0},{20,4},{24,8},{28,12},{1,17},{... | collective-permute-start | bytes 516104 | tf_op jit(solution)/shard_map/ppermute | solution.py:49
  179.9 3.9 %collective-permute-done.54 = bf16[4,24,896]{2,1,0:T(8,128)(2,1)S(1)} collective-permute-done((bf16[4,24,896]{2,1,0:T(8,128)(2,1)S(1)}, bf16[4,24,896]{2,1,0:T(8,128)(2,1)S(1)}, u32[]{:S(2)}, u32[]{:S(2)}) %collective-permute-start.54) | collective-permute-done | bytes 172064 | tf_op jit(solution)/shard_map/ppermute | solution.py:49
  183.8 3.5 %collective-permute-start.55 = (bf16[4,24,896]{2,1,0:T(8,128)(2,1)S(1)}, bf16[4,24,896]{2,1,0:T(8,128)(2,1)S(1)}, u32[]{:S(2)}, u32[]{:S(2)}) collective-permute-start(bf16[4,24,896]{2,1,0:T(8,128)(2,1)S(1)} %add_convert_fusion.4), channel_id=1, source_target_pairs={{0,8},{4,12},{8,0},{12,4},{16,24},{20,28},{24,16},{28,20},{1,9},{5... | collective-permute-start | bytes 516104 | tf_op jit(solution)/shard_map/ppermute | solution.py:49
  187.4 1.4 collective-permute-start.53
  188.9 3.0 %collective-permute-done.55.refs_5_ = bf16[4,24,896]{2,1,0:T(8,128)(2,1)S(1)} collective-permute-done((bf16[4,24,896]{2,1,0:T(8,128)(2,1)S(1)}, bf16[4,24,896]{2,1,0:T(8,128)(2,1)S(1)}, u32[]{:S(2)}, u32[]{:S(2)}) %collective-permute-start.55) | collective-permute-done | bytes 172064 | tf_op jit(solution)/shard_map/ppermute | solution.py:49
  191.9 3.7 %collective-permute-done.53.refs_4_ = bf16[4,24,896]{2,1,0:T(8,128)(2,1)S(1)} collective-permute-done((bf16[4,24,896]{2,1,0:T(8,128)(2,1)S(1)}, bf16[4,24,896]{2,1,0:T(8,128)(2,1)S(1)}, u32[]{:S(2)}, u32[]{:S(2)}) %collective-permute-start.53) | collective-permute-done | bytes 172064 | tf_op jit(solution)/shard_map/ppermute | solution.py:49
  198.2 2.2 collective-permute-done.57.refs_3_
  201.6 2.1 collective-permute-start.64
  203.7 2.4 %collective-permute-start.62 = (bf16[24,3200]{1,0:T(8,128)(2,1)S(1)}, bf16[24,3200]{1,0:T(8,128)(2,1)S(1)}, u32[]{:S(2)}, u32[]{:S(2)}) collective-permute-start(bf16[24,3200]{1,0:T(8,128)(2,1)S(1)} %shard_map.259.refs_1_), channel_id=1, source_target_pairs={{0,16},{4,20},{8,24},{12,28},{16,0},{20,4},{24,8},{28,12},{1,17},{... | collective-permute-start | bytes 460808 | tf_op jit(solution)/shard_map/ppermute | solution.py:49
  207.2 1.5 collective-permute-start.59
  208.7 1.7 collective-permute-done.64.refs_7_
  210.4 1.5 collective-permute-start.65
  211.9 7.5 %collective-permute-done.62.refs_5_ = bf16[24,3200]{1,0:T(8,128)(2,1)S(1)} collective-permute-done((bf16[24,3200]{1,0:T(8,128)(2,1)S(1)}, bf16[24,3200]{1,0:T(8,128)(2,1)S(1)}, u32[]{:S(2)}, u32[]{:S(2)}) %collective-permute-start.62) | collective-permute-done | bytes 153632 | tf_op jit(solution)/shard_map/ppermute | solution.py:49
  219.4 1.5 collective-permute-start.63
  221.4 4.9 %shard_map.261 = (f32[1,768,768]{2,1,0:T(8,128)}, f32[1,768,768]{2,1,0:T(8,128)}) custom-call(bf16[4,24,896]{2,1,0:T(8,128)(2,1)S(1)} %get-tuple-element.162.refs_0_, s32[3]{0:T(128)S(1)} %copy-done.12, bf16[512,768]{1,0:T(8,128)(2,1)S(1)} %get-tuple-element.129.refs_3_.refs_2_, bf16[512,768]{1,0:T(8,128)(2,1)S(1)} %get-tuple-element.130.refs_4_.refs_3_, ...), custom_call_target="tpu_custom_call" | custom-call | flops 1 | bytes 1 | tf_op jit(solution)/shard_map/pallas_call | solution.py:132
  226.3 1.5 shard_map.256
  228.6 2.1 shard_map.260
  (154 shorter events, 34.0 us)
Async XLA Ops:
  0.6 8.8 %collective-permute-start.1 = (bf16[128,768]{1,0:T(8,128)(2,1)}, bf16[128,768]{1,0:T(8,128)(2,1)S(1)}, u32[]{:S(2)}, u32[]{:S(2)}) collective-permute-start(bf16[128,768]{1,0:T(8,128)(2,1)} %refs_1_.11), channel_id=1, source_target_pairs={{0,2},{1,3},{2,0},{3,1},{4,6},{5,7},{6,4},{7,5},{8,10},{9,11},{10,... | collective-permute-start | bytes 589832 | tf_op jit(solution)/shard_map/ppermute | solution.py:49
  7.3 8.9 %collective-permute-start.3 = (bf16[224,576]{1,0:T(8,128)(2,1)}, bf16[224,576]{1,0:T(8,128)(2,1)S(1)}, u32[]{:S(2)}, u32[]{:S(2)}) collective-permute-start(bf16[224,576]{1,0:T(8,128)(2,1)} %get-tuple-element.98), channel_id=1, source_target_pairs={{0,1},{1,0},{2,3},{3,2},{4,5},{5,4},{6,7},{7,6},{8,9},{9,8},{10,11... | collective-permute-start | bytes 774152 | tf_op jit(solution)/shard_map/ppermute | solution.py:49
  7.3 9.9 %collective-permute-start.4 = (bf16[224,576]{1,0:T(8,128)(2,1)}, bf16[224,576]{1,0:T(8,128)(2,1)S(1)}, u32[]{:S(2)}, u32[]{:S(2)}) collective-permute-start(bf16[224,576]{1,0:T(8,128)(2,1)} %get-tuple-element.99), channel_id=1, source_target_pairs={{0,2},{1,3},{2,0},{3,1},{4,6},{5,7},{6,4},{7,5},{8,10},{9,11},{10,... | collective-permute-start | bytes 774152 | tf_op jit(solution)/shard_map/ppermute | solution.py:49
  7.3 15.2 %collective-permute-start.5 = (bf16[224,576]{1,0:T(8,128)(2,1)}, bf16[224,576]{1,0:T(8,128)(2,1)S(1)}, u32[]{:S(2)}, u32[]{:S(2)}) collective-permute-start(bf16[224,576]{1,0:T(8,128)(2,1)} %get-tuple-element.100), channel_id=1, source_target_pairs={{0,3},{1,2},{2,1},{3,0},{4,7},{5,6},{6,5},{7,4},{8,11},{9,10},{10,... | collective-permute-start | bytes 774152 | tf_op jit(solution)/shard_map/ppermute | solution.py:49
  9.2 3.3 %collective-permute-start = (bf16[128,768]{1,0:T(8,128)(2,1)}, bf16[128,768]{1,0:T(8,128)(2,1)S(1)}, u32[]{:S(2)}, u32[]{:S(2)}) collective-permute-start(bf16[128,768]{1,0:T(8,128)(2,1)} %refs_1_.11), channel_id=1, source_target_pairs={{0,1},{1,0},{2,3},{3,2},{4,5},{5,4},{6,7},{7,6},{8,9},{9,8},{10,11... | collective-permute-start | bytes 589832 | tf_op jit(solution)/shard_map/ppermute | solution.py:49
  9.5 13.1 %collective-permute-start.2 = (bf16[128,768]{1,0:T(8,128)(2,1)S(1)}, bf16[128,768]{1,0:T(8,128)(2,1)S(1)}, u32[]{:S(2)}, u32[]{:S(2)}) collective-permute-start(bf16[128,768]{1,0:T(8,128)(2,1)S(1)} %collective-permute-done.1.refs_3_), channel_id=1, source_target_pairs={{0,1},{1,0},{2,3},{3,2},{4,5},{5,4},{6,7},{7,6},{8,9},{9,8},{10,11... | collective-permute-start | bytes 589832 | tf_op jit(solution)/shard_map/ppermute | solution.py:49
  12.6 18.8 %collective-permute-start.8 = (bf16[144,768]{1,0:T(8,128)(2,1)S(1)}, bf16[144,768]{1,0:T(8,128)(2,1)S(1)}, u32[]{:S(2)}, u32[]{:S(2)}) collective-permute-start(bf16[144,768]{1,0:T(8,128)(2,1)S(1)} %shard_map.240.refs_3_.refs_2_), channel_id=1, source_target_pairs={{0,24},{4,28},{8,16},{12,20},{16,8},{20,12},{24,0},{28,4},{1,25},{... | collective-permute-start | bytes 663560 | tf_op jit(solution)/shard_map/ppermute | solution.py:49
  16.2 19.3 %collective-permute-start.7 = (bf16[144,768]{1,0:T(8,128)(2,1)S(1)}, bf16[144,768]{1,0:T(8,128)(2,1)S(1)}, u32[]{:S(2)}, u32[]{:S(2)}) collective-permute-start(bf16[144,768]{1,0:T(8,128)(2,1)S(1)} %shard_map.240.refs_3_.refs_2_), channel_id=1, source_target_pairs={{0,16},{4,20},{8,24},{12,28},{16,0},{20,4},{24,8},{28,12},{1,17},{... | collective-permute-start | bytes 663560 | tf_op jit(solution)/shard_map/ppermute | solution.py:49
  17.2 18.3 %collective-permute-start.6 = (bf16[144,768]{1,0:T(8,128)(2,1)S(1)}, bf16[144,768]{1,0:T(8,128)(2,1)S(1)}, u32[]{:S(2)}, u32[]{:S(2)}) collective-permute-start(bf16[144,768]{1,0:T(8,128)(2,1)S(1)} %shard_map.240.refs_3_.refs_2_), channel_id=1, source_target_pairs={{0,8},{4,12},{8,0},{12,4},{16,24},{20,28},{24,16},{28,20},{1,9},{5... | collective-permute-start | bytes 663560 | tf_op jit(solution)/shard_map/ppermute | solution.py:49
  37.4 1.8 collective-permute-start.9
  37.5 22.5 %collective-permute-start.11 = (bf16[4,144,768]{2,1,0:T(8,128)(2,1)S(1)}, bf16[4,144,768]{2,1,0:T(8,128)(2,1)S(1)}, u32[]{:S(2)}, u32[]{:S(2)}) collective-permute-start(bf16[4,144,768]{2,1,0:T(8,128)(2,1)S(1)} %get-tuple-element.112), channel_id=1, source_target_pairs={{0,4},{4,0},{8,12},{12,8},{16,20},{20,16},{24,28},{28,24},{1,5},{5... | collective-permute-start | bytes 2654216 | tf_op jit(solution)/shard_map/ppermute | solution.py:49
  39.3 7.0 %collective-permute-start.10 = (bf16[128,768]{1,0:T(8,128)(2,1)S(1)}, bf16[128,768]{1,0:T(8,128)(2,1)S(1)}, u32[]{:S(2)}, u32[]{:S(2)}) collective-permute-start(bf16[128,768]{1,0:T(8,128)(2,1)S(1)} %fusion.2), channel_id=1, source_target_pairs={{0,2},{1,3},{2,0},{3,1},{4,6},{5,7},{6,4},{7,5},{8,10},{9,11},{10,... | collective-permute-start | bytes 589832 | tf_op jit(solution)/shard_map/ppermute | solution.py:49
  47.1 15.9 %collective-permute-start.23 = (bf16[128,768]{1,0:T(8,128)(2,1)S(1)}, bf16[128,768]{1,0:T(8,128)(2,1)S(1)}, u32[]{:S(2)}, u32[]{:S(2)}) collective-permute-start(bf16[128,768]{1,0:T(8,128)(2,1)S(1)} %get-tuple-element.111.refs_0_.refs_4_), channel_id=1, source_target_pairs={{0,24},{4,28},{8,16},{12,20},{16,8},{20,12},{24,0},{28,4},{1,25},{... | collective-permute-start | bytes 589832 | tf_op jit(solution)/shard_map/ppermute | solution.py:49
  49.6 15.4 %collective-permute-start.21 = (bf16[128,768]{1,0:T(8,128)(2,1)S(1)}, bf16[128,768]{1,0:T(8,128)(2,1)S(1)}, u32[]{:S(2)}, u32[]{:S(2)}) collective-permute-start(bf16[128,768]{1,0:T(8,128)(2,1)S(1)} %get-tuple-element.111.refs_0_.refs_4_), channel_id=1, source_target_pairs={{0,16},{4,20},{8,24},{12,28},{16,0},{20,4},{24,8},{28,12},{1,17},{... | collective-permute-start | bytes 589832 | tf_op jit(solution)/shard_map/ppermute | solution.py:49
  49.6 16.9 %collective-permute-start.19 = (bf16[128,768]{1,0:T(8,128)(2,1)S(1)}, bf16[128,768]{1,0:T(8,128)(2,1)S(1)}, u32[]{:S(2)}, u32[]{:S(2)}) collective-permute-start(bf16[128,768]{1,0:T(8,128)(2,1)S(1)} %get-tuple-element.111.refs_0_.refs_4_), channel_id=1, source_target_pairs={{0,8},{4,12},{8,0},{12,4},{16,24},{20,28},{24,16},{28,20},{1,9},{5... | collective-permute-start | bytes 589832 | tf_op jit(solution)/shard_map/ppermute | solution.py:49
  51.5 15.5 %collective-permute-start.18 = (bf16[128,768]{1,0:T(8,128)(2,1)S(1)}, bf16[128,768]{1,0:T(8,128)(2,1)S(1)}, u32[]{:S(2)}, u32[]{:S(2)}) collective-permute-start(bf16[128,768]{1,0:T(8,128)(2,1)S(1)} %get-tuple-element.111.refs_0_.refs_4_), channel_id=1, source_target_pairs={{0,4},{4,0},{8,12},{12,8},{16,20},{20,16},{24,28},{28,24},{1,5},{5... | collective-permute-start | bytes 589832 | tf_op jit(solution)/shard_map/ppermute | solution.py:49
  61.9 15.3 %collective-permute-start.15 = (bf16[144,768]{1,0:T(8,128)(2,1)S(1)}, bf16[144,768]{1,0:T(8,128)(2,1)S(1)}, u32[]{:S(2)}, u32[]{:S(2)}) collective-permute-start(bf16[144,768]{1,0:T(8,128)(2,1)S(1)} %get-tuple-element.116.refs_3_.refs_11_), channel_id=1, source_target_pairs={{0,2},{1,3},{2,0},{3,1},{4,6},{5,7},{6,4},{7,5},{8,10},{9,11},{10,... | collective-permute-start | bytes 663560 | tf_op jit(solution)/shard_map/ppermute | solution.py:49
  63.0 7.8 %collective-permute-start.24 = (bf16[128,768]{1,0:T(8,128)(2,1)S(1)}, bf16[128,768]{1,0:T(8,128)(2,1)S(1)}, u32[]{:S(2)}, u32[]{:S(2)}) collective-permute-start(bf16[128,768]{1,0:T(8,128)(2,1)S(1)} %collective-permute-done.23.refs_10_), channel_id=1, source_target_pairs={{0,4},{4,0},{8,12},{12,8},{16,20},{20,16},{24,28},{28,24},{1,5},{5... | collective-permute-start | bytes 589832 | tf_op jit(solution)/shard_map/ppermute | solution.py:49
  65.0 10.1 %collective-permute-start.22 = (bf16[128,768]{1,0:T(8,128)(2,1)S(1)}, bf16[128,768]{1,0:T(8,128)(2,1)S(1)}, u32[]{:S(2)}, u32[]{:S(2)}) collective-permute-start(bf16[128,768]{1,0:T(8,128)(2,1)S(1)} %collective-permute-done.21.refs_8_), channel_id=1, source_target_pairs={{0,4},{4,0},{8,12},{12,8},{16,20},{20,16},{24,28},{28,24},{1,5},{5... | collective-permute-start | bytes 589832 | tf_op jit(solution)/shard_map/ppermute | solution.py:49
  66.5 10.7 %collective-permute-start.20 = (bf16[128,768]{1,0:T(8,128)(2,1)S(1)}, bf16[128,768]{1,0:T(8,128)(2,1)S(1)}, u32[]{:S(2)}, u32[]{:S(2)}) collective-permute-start(bf16[128,768]{1,0:T(8,128)(2,1)S(1)} %collective-permute-done.19.refs_6_), channel_id=1, source_target_pairs={{0,4},{4,0},{8,12},{12,8},{16,20},{20,16},{24,28},{28,24},{1,5},{5... | collective-permute-start | bytes 589832 | tf_op jit(solution)/shard_map/ppermute | solution.py:49
  67.0 10.1 %collective-permute-start.14 = (bf16[128,768]{1,0:T(8,128)(2,1)S(1)}, bf16[128,768]{1,0:T(8,128)(2,1)S(1)}, u32[]{:S(2)}, u32[]{:S(2)}) collective-permute-start(bf16[128,768]{1,0:T(8,128)(2,1)S(1)} %get-tuple-element.115.refs_2_.refs_10_), channel_id=1, source_target_pairs={{0,2},{1,3},{2,0},{3,1},{4,6},{5,7},{6,4},{7,5},{8,10},{9,11},{10,... | collective-permute-start | bytes 589832 | tf_op jit(solution)/shard_map/ppermute | solution.py:49
  70.8 9.5 %collective-permute-start.12 = (bf16[128,768]{1,0:T(8,128)(2,1)S(1)}, bf16[128,768]{1,0:T(8,128)(2,1)S(1)}, u32[]{:S(2)}, u32[]{:S(2)}) collective-permute-start(bf16[128,768]{1,0:T(8,128)(2,1)S(1)} %get-tuple-element.115.refs_2_.refs_10_), channel_id=1, source_target_pairs={{0,1},{1,0},{2,3},{3,2},{4,5},{5,4},{6,7},{7,6},{8,9},{9,8},{10,11... | collective-permute-start | bytes 589832 | tf_op jit(solution)/shard_map/ppermute | solution.py:49
  78.7 6.9 %collective-permute-start.26 = (bf16[256,768]{1,0:T(8,128)(2,1)S(1)}, bf16[256,768]{1,0:T(8,128)(2,1)S(1)}, u32[]{:S(2)}, u32[]{:S(2)}) collective-permute-start(bf16[256,768]{1,0:T(8,128)(2,1)S(1)} %shard_map.245.refs_7_.refs_6_), channel_id=1, source_target_pairs={{0,1},{1,0},{2,3},{3,2},{4,5},{5,4},{6,7},{7,6},{8,9},{9,8},{10,11... | collective-permute-start | bytes 1179656 | tf_op jit(solution)/shard_map/ppermute | solution.py:49
  78.8 11.5 %collective-permute-start.25 = (bf16[256,768]{1,0:T(8,128)(2,1)S(1)}, bf16[256,768]{1,0:T(8,128)(2,1)S(1)}, u32[]{:S(2)}, u32[]{:S(2)}) collective-permute-start(bf16[256,768]{1,0:T(8,128)(2,1)S(1)} %shard_map.245.refs_7_.refs_6_), channel_id=1, source_target_pairs={{0,2},{1,3},{2,0},{3,1},{4,6},{5,7},{6,4},{7,5},{8,10},{9,11},{10,... | collective-permute-start | bytes 1179656 | tf_op jit(solution)/shard_map/ppermute | solution.py:49
  80.0 1.9 collective-permute-start.17
  90.3 1.7 collective-permute-start.27
  96.0 1.8 collective-permute-start.28
  100.3 17.1 %collective-permute-start.29 = (bf16[2,256,768]{2,1,0:T(8,128)(2,1)S(1)}, bf16[2,256,768]{2,1,0:T(8,128)(2,1)S(1)}, u32[]{:S(2)}, u32[]{:S(2)}) collective-permute-start(bf16[2,256,768]{2,1,0:T(8,128)(2,1)S(1)} %get-tuple-element.134), channel_id=1, source_target_pairs={{0,1},{1,0},{2,3},{3,2},{4,5},{5,4},{6,7},{7,6},{8,9},{9,8},{10,11... | collective-permute-start | bytes 2359304 | tf_op jit(solution)/shard_map/ppermute | solution.py:49
  100.5 2.7 %collective-permute-start.32 = (bf16[256,768]{1,0:T(8,128)(2,1)S(1)}, bf16[256,768]{1,0:T(8,128)(2,1)S(1)}, u32[]{:S(2)}, u32[]{:S(2)}) collective-permute-start(bf16[256,768]{1,0:T(8,128)(2,1)S(1)} %get-tuple-element.138), channel_id=1, source_target_pairs={{0,1},{1,0},{2,3},{3,2},{4,5},{5,4},{6,7},{7,6},{8,9},{9,8},{10,11... | collective-permute-start | bytes 1179656 | tf_op jit(solution)/shard_map/ppermute | solution.py:49
  100.8 11.2 %collective-permute-start.33 = (bf16[256,768]{1,0:T(8,128)(2,1)S(1)}, bf16[256,768]{1,0:T(8,128)(2,1)S(1)}, u32[]{:S(2)}, u32[]{:S(2)}) collective-permute-start(bf16[256,768]{1,0:T(8,128)(2,1)S(1)} %add_convert_fusion.refs_0_), channel_id=1, source_target_pairs={{0,2},{1,3},{2,0},{3,1},{4,6},{5,7},{6,4},{7,5},{8,10},{9,11},{10,... | collective-permute-start | bytes 1179656 | tf_op jit(solution)/shard_map/ppermute | solution.py:49
  113.2 28.6 %collective-permute-start.34 = (bf16[128,768]{1,0:T(8,128)(2,1)S(1)}, bf16[128,768]{1,0:T(8,128)(2,1)S(1)}, u32[]{:S(2)}, u32[]{:S(2)}) collective-permute-start(bf16[128,768]{1,0:T(8,128)(2,1)S(1)} %get-tuple-element.140), channel_id=1, source_target_pairs={{0,4},{4,0},{8,12},{12,8},{16,20},{20,16},{24,28},{28,24},{1,5},{5... | collective-permute-start | bytes 589832 | tf_op jit(solution)/shard_map/ppermute | solution.py:49
  114.8 10.5 %collective-permute-start.35 = (bf16[128,768]{1,0:T(8,128)(2,1)S(1)}, bf16[128,768]{1,0:T(8,128)(2,1)S(1)}, u32[]{:S(2)}, u32[]{:S(2)}) collective-permute-start(bf16[128,768]{1,0:T(8,128)(2,1)S(1)} %get-tuple-element.142), channel_id=1, source_target_pairs={{0,4},{4,0},{8,12},{12,8},{16,20},{20,16},{24,28},{28,24},{1,5},{5... | collective-permute-start | bytes 589832 | tf_op jit(solution)/shard_map/ppermute | solution.py:49
  115.3 14.2 %collective-permute-start.37 = (bf16[128,768]{1,0:T(8,128)(2,1)S(1)}, bf16[128,768]{1,0:T(8,128)(2,1)S(1)}, u32[]{:S(2)}, u32[]{:S(2)}) collective-permute-start(bf16[128,768]{1,0:T(8,128)(2,1)S(1)} %get-tuple-element.144), channel_id=1, source_target_pairs={{0,4},{4,0},{8,12},{12,8},{16,20},{20,16},{24,28},{28,24},{1,5},{5... | collective-permute-start | bytes 589832 | tf_op jit(solution)/shard_map/ppermute | solution.py:49
  116.8 17.6 %collective-permute-start.39 = (bf16[128,768]{1,0:T(8,128)(2,1)S(1)}, bf16[128,768]{1,0:T(8,128)(2,1)S(1)}, u32[]{:S(2)}, u32[]{:S(2)}) collective-permute-start(bf16[128,768]{1,0:T(8,128)(2,1)S(1)} %get-tuple-element.146), channel_id=1, source_target_pairs={{0,4},{4,0},{8,12},{12,8},{16,20},{20,16},{24,28},{28,24},{1,5},{5... | collective-permute-start | bytes 589832 | tf_op jit(solution)/shard_map/ppermute | solution.py:49
  117.4 14.7 %collective-permute-start.30 = (bf16[256,768]{1,0:T(8,128)(2,1)S(1)}, bf16[256,768]{1,0:T(8,128)(2,1)S(1)}, u32[]{:S(2)}, u32[]{:S(2)}) collective-permute-start(bf16[256,768]{1,0:T(8,128)(2,1)S(1)} %fusion), channel_id=1, source_target_pairs={{0,2},{1,3},{2,0},{3,1},{4,6},{5,7},{6,4},{7,5},{8,10},{9,11},{10,... | collective-permute-start | bytes 1179656 | tf_op jit(solution)/shard_map/ppermute | solution.py:49
  125.4 16.5 %collective-permute-start.36 = (bf16[128,768]{1,0:T(8,128)(2,1)S(1)}, bf16[128,768]{1,0:T(8,128)(2,1)S(1)}, u32[]{:S(2)}, u32[]{:S(2)}) collective-permute-start(bf16[128,768]{1,0:T(8,128)(2,1)S(1)} %add_convert_fusion.3), channel_id=1, source_target_pairs={{0,16},{4,20},{8,24},{12,28},{16,0},{20,4},{24,8},{28,12},{1,17},{... | collective-permute-start | bytes 589832 | tf_op jit(solution)/shard_map/ppermute | solution.py:49
  129.6 12.3 %collective-permute-start.38 = (bf16[128,768]{1,0:T(8,128)(2,1)S(1)}, bf16[128,768]{1,0:T(8,128)(2,1)S(1)}, u32[]{:S(2)}, u32[]{:S(2)}) collective-permute-start(bf16[128,768]{1,0:T(8,128)(2,1)S(1)} %add_convert_fusion.2), channel_id=1, source_target_pairs={{0,24},{4,28},{8,16},{12,20},{16,8},{20,12},{24,0},{28,4},{1,25},{... | collective-permute-start | bytes 589832 | tf_op jit(solution)/shard_map/ppermute | solution.py:49
  132.9 7.8 %collective-permute-start.31 = (bf16[256,768]{1,0:T(8,128)(2,1)S(1)}, bf16[256,768]{1,0:T(8,128)(2,1)S(1)}, u32[]{:S(2)}, u32[]{:S(2)}) collective-permute-start(bf16[256,768]{1,0:T(8,128)(2,1)S(1)} %shard_map.250.refs_3_), channel_id=1, source_target_pairs={{0,4},{4,0},{8,12},{12,8},{16,20},{20,16},{24,28},{28,24},{1,5},{5... | collective-permute-start | bytes 1179656 | tf_op jit(solution)/shard_map/ppermute | solution.py:49
  134.5 7.8 %collective-permute-start.40 = (bf16[128,768]{1,0:T(8,128)(2,1)S(1)}, bf16[128,768]{1,0:T(8,128)(2,1)S(1)}, u32[]{:S(2)}, u32[]{:S(2)}) collective-permute-start(bf16[128,768]{1,0:T(8,128)(2,1)S(1)} %add_convert_fusion.1), channel_id=1, source_target_pairs={{0,8},{4,12},{8,0},{12,4},{16,24},{20,28},{24,16},{28,20},{1,9},{5... | collective-permute-start | bytes 589832 | tf_op jit(solution)/shard_map/ppermute | solution.py:49
  143.2 5.8 %collective-permute-start.42 = (bf16[128,768]{1,0:T(8,128)(2,1)S(1)}, bf16[128,768]{1,0:T(8,128)(2,1)S(1)}, u32[]{:S(2)}, u32[]{:S(2)}) collective-permute-start(bf16[128,768]{1,0:T(8,128)(2,1)S(1)} %get-tuple-element.149.refs_10_), channel_id=1, source_target_pairs={{0,2},{1,3},{2,0},{3,1},{4,6},{5,7},{6,4},{7,5},{8,10},{9,11},{10,... | collective-permute-start | bytes 589832 | tf_op jit(solution)/shard_map/ppermute | solution.py:49
  144.3 8.2 %collective-permute-start.41 = (bf16[128,768]{1,0:T(8,128)(2,1)S(1)}, bf16[128,768]{1,0:T(8,128)(2,1)S(1)}, u32[]{:S(2)}, u32[]{:S(2)}) collective-permute-start(bf16[128,768]{1,0:T(8,128)(2,1)S(1)} %get-tuple-element.149.refs_10_), channel_id=1, source_target_pairs={{0,1},{1,0},{2,3},{3,2},{4,5},{5,4},{6,7},{7,6},{8,9},{9,8},{10,11... | collective-permute-start | bytes 589832 | tf_op jit(solution)/shard_map/ppermute | solution.py:49
  149.0 3.5 %collective-permute-start.43 = (bf16[128,768]{1,0:T(8,128)(2,1)S(1)}, bf16[128,768]{1,0:T(8,128)(2,1)S(1)}, u32[]{:S(2)}, u32[]{:S(2)}) collective-permute-start(bf16[128,768]{1,0:T(8,128)(2,1)S(1)} %collective-permute-done.42.refs_12_), channel_id=1, source_target_pairs={{0,1},{1,0},{2,3},{3,2},{4,5},{5,4},{6,7},{7,6},{8,9},{9,8},{10,11... | collective-permute-start | bytes 589832 | tf_op jit(solution)/shard_map/ppermute | solution.py:49
  149.0 16.7 %collective-permute-start.44 = (bf16[128,768]{1,0:T(8,128)(2,1)S(1)}, bf16[128,768]{1,0:T(8,128)(2,1)S(1)}, u32[]{:S(2)}, u32[]{:S(2)}) collective-permute-start(bf16[128,768]{1,0:T(8,128)(2,1)S(1)} %get-tuple-element.151), channel_id=1, source_target_pairs={{0,16},{4,20},{8,24},{12,28},{16,0},{20,4},{24,8},{28,12},{1,17},{... | collective-permute-start | bytes 589832 | tf_op jit(solution)/shard_map/ppermute | solution.py:49
  149.4 16.3 %collective-permute-start.45 = (bf16[128,768]{1,0:T(8,128)(2,1)S(1)}, bf16[128,768]{1,0:T(8,128)(2,1)S(1)}, u32[]{:S(2)}, u32[]{:S(2)}) collective-permute-start(bf16[128,768]{1,0:T(8,128)(2,1)S(1)} %get-tuple-element.152), channel_id=1, source_target_pairs={{0,24},{4,28},{8,16},{12,20},{16,8},{20,12},{24,0},{28,4},{1,25},{... | collective-permute-start | bytes 589832 | tf_op jit(solution)/shard_map/ppermute | solution.py:49
  151.9 15.1 %collective-permute-start.46 = (bf16[128,768]{1,0:T(8,128)(2,1)S(1)}, bf16[128,768]{1,0:T(8,128)(2,1)S(1)}, u32[]{:S(2)}, u32[]{:S(2)}) collective-permute-start(bf16[128,768]{1,0:T(8,128)(2,1)S(1)} %get-tuple-element.153), channel_id=1, source_target_pairs={{0,8},{4,12},{8,0},{12,4},{16,24},{20,28},{24,16},{28,20},{1,9},{5... | collective-permute-start | bytes 589832 | tf_op jit(solution)/shard_map/ppermute | solution.py:49
  169.2 7.3 %collective-permute-start.50 = (bf16[4,24,896]{2,1,0:T(8,128)(2,1)S(1)}, bf16[4,24,896]{2,1,0:T(8,128)(2,1)S(1)}, u32[]{:S(2)}, u32[]{:S(2)}) collective-permute-start(bf16[4,24,896]{2,1,0:T(8,128)(2,1)S(1)} %shard_map.257), channel_id=1, source_target_pairs={{0,4},{4,0},{8,12},{12,8},{16,20},{20,16},{24,28},{28,24},{1,5},{5... | collective-permute-start | bytes 516104 | tf_op jit(solution)/shard_map/ppermute | solution.py:49
  170.7 18.1 %collective-permute-start.49 = (bf16[4,24,896]{2,1,0:T(8,128)(2,1)S(1)}, bf16[4,24,896]{2,1,0:T(8,128)(2,1)S(1)}, u32[]{:S(2)}, u32[]{:S(2)}) collective-permute-start(bf16[4,24,896]{2,1,0:T(8,128)(2,1)S(1)} %get-tuple-element.158), channel_id=1, source_target_pairs={{0,4},{4,0},{8,12},{12,8},{16,20},{20,16},{24,28},{28,24},{1,5},{5... | collective-permute-start | bytes 516104 | tf_op jit(solution)/shard_map/ppermute | solution.py:49
  171.2 12.6 %collective-permute-start.54 = (bf16[4,24,896]{2,1,0:T(8,128)(2,1)S(1)}, bf16[4,24,896]{2,1,0:T(8,128)(2,1)S(1)}, u32[]{:S(2)}, u32[]{:S(2)}) collective-permute-start(bf16[4,24,896]{2,1,0:T(8,128)(2,1)S(1)} %get-tuple-element.164), channel_id=1, source_target_pairs={{0,4},{4,0},{8,12},{12,8},{16,20},{20,16},{24,28},{28,24},{1,5},{5... | collective-permute-start | bytes 516104 | tf_op jit(solution)/shard_map/ppermute | solution.py:49
  172.8 14.6 %collective-permute-start.52 = (bf16[4,24,896]{2,1,0:T(8,128)(2,1)S(1)}, bf16[4,24,896]{2,1,0:T(8,128)(2,1)S(1)}, u32[]{:S(2)}, u32[]{:S(2)}) collective-permute-start(bf16[4,24,896]{2,1,0:T(8,128)(2,1)S(1)} %get-tuple-element.162.refs_0_), channel_id=1, source_target_pairs={{0,4},{4,0},{8,12},{12,8},{16,20},{20,16},{24,28},{28,24},{1,5},{5... | collective-permute-start | bytes 516104 | tf_op jit(solution)/shard_map/ppermute | solution.py:49
  173.3 32.8 %collective-permute-start.47 = (bf16[2,128,768]{2,1,0:T(8,128)(2,1)S(1)}, bf16[2,128,768]{2,1,0:T(8,128)(2,1)S(1)}, u32[]{:S(2)}, u32[]{:S(2)}) collective-permute-start(bf16[2,128,768]{2,1,0:T(8,128)(2,1)S(1)} %get-tuple-element.156), channel_id=1, source_target_pairs={{0,1},{1,0},{2,3},{3,2},{4,5},{5,4},{6,7},{7,6},{8,9},{9,8},{10,11... | collective-permute-start | bytes 1179656 | tf_op jit(solution)/shard_map/ppermute | solution.py:49
  176.6 12.3 %collective-permute-start.51 = (bf16[4,24,896]{2,1,0:T(8,128)(2,1)S(1)}, bf16[4,24,896]{2,1,0:T(8,128)(2,1)S(1)}, u32[]{:S(2)}, u32[]{:S(2)}) collective-permute-start(bf16[4,24,896]{2,1,0:T(8,128)(2,1)S(1)} %add_convert_fusion.6), channel_id=1, source_target_pairs={{0,16},{4,20},{8,24},{12,28},{16,0},{20,4},{24,8},{28,12},{1,17},{... | collective-permute-start | bytes 516104 | tf_op jit(solution)/shard_map/ppermute | solution.py:49
  183.8 8.0 %collective-permute-start.55 = (bf16[4,24,896]{2,1,0:T(8,128)(2,1)S(1)}, bf16[4,24,896]{2,1,0:T(8,128)(2,1)S(1)}, u32[]{:S(2)}, u32[]{:S(2)}) collective-permute-start(bf16[4,24,896]{2,1,0:T(8,128)(2,1)S(1)} %add_convert_fusion.4), channel_id=1, source_target_pairs={{0,8},{4,12},{8,0},{12,4},{16,24},{20,28},{24,16},{28,20},{1,9},{5... | collective-permute-start | bytes 516104 | tf_op jit(solution)/shard_map/ppermute | solution.py:49
  187.4 8.2 %collective-permute-start.53 = (bf16[4,24,896]{2,1,0:T(8,128)(2,1)S(1)}, bf16[4,24,896]{2,1,0:T(8,128)(2,1)S(1)}, u32[]{:S(2)}, u32[]{:S(2)}) collective-permute-start(bf16[4,24,896]{2,1,0:T(8,128)(2,1)S(1)} %add_convert_fusion.5), channel_id=1, source_target_pairs={{0,24},{4,28},{8,16},{12,20},{16,8},{20,12},{24,0},{28,4},{1,25},{... | collective-permute-start | bytes 516104 | tf_op jit(solution)/shard_map/ppermute | solution.py:49
  196.3 1.9 collective-permute-start.56
  196.4 4.0 %collective-permute-start.57 = (bf16[24,704]{1,0:T(8,128)(2,1)S(1)}, bf16[24,704]{1,0:T(8,128)(2,1)S(1)}, u32[]{:S(2)}, u32[]{:S(2)}) collective-permute-start(bf16[24,704]{1,0:T(8,128)(2,1)S(1)} %get-tuple-element.167), channel_id=1, source_target_pairs={{0,2},{1,3},{2,0},{3,1},{4,6},{5,7},{6,4},{7,5},{8,10},{9,11},{10,... | collective-permute-start | bytes 101384 | tf_op jit(solution)/shard_map/ppermute | solution.py:49
  197.5 3.4 %collective-permute-start.58 = (bf16[24,704]{1,0:T(8,128)(2,1)S(1)}, bf16[24,704]{1,0:T(8,128)(2,1)S(1)}, u32[]{:S(2)}, u32[]{:S(2)}) collective-permute-start(bf16[24,704]{1,0:T(8,128)(2,1)S(1)} %get-tuple-element.168), channel_id=1, source_target_pairs={{0,3},{1,2},{2,1},{3,0},{4,7},{5,6},{6,5},{7,4},{8,11},{9,10},{10,... | collective-permute-start | bytes 101384 | tf_op jit(solution)/shard_map/ppermute | solution.py:49
  201.6 8.8 %collective-permute-start.64 = (bf16[24,3200]{1,0:T(8,128)(2,1)S(1)}, bf16[24,3200]{1,0:T(8,128)(2,1)S(1)}, u32[]{:S(2)}, u32[]{:S(2)}) collective-permute-start(bf16[24,3200]{1,0:T(8,128)(2,1)S(1)} %shard_map.259.refs_1_), channel_id=1, source_target_pairs={{0,24},{4,28},{8,16},{12,20},{16,8},{20,12},{24,0},{28,4},{1,25},{... | collective-permute-start | bytes 460808 | tf_op jit(solution)/shard_map/ppermute | solution.py:49
  203.7 15.7 %collective-permute-start.62 = (bf16[24,3200]{1,0:T(8,128)(2,1)S(1)}, bf16[24,3200]{1,0:T(8,128)(2,1)S(1)}, u32[]{:S(2)}, u32[]{:S(2)}) collective-permute-start(bf16[24,3200]{1,0:T(8,128)(2,1)S(1)} %shard_map.259.refs_1_), channel_id=1, source_target_pairs={{0,16},{4,20},{8,24},{12,28},{16,0},{20,4},{24,8},{28,12},{1,17},{... | collective-permute-start | bytes 460808 | tf_op jit(solution)/shard_map/ppermute | solution.py:49
  206.0 14.9 %collective-permute-start.60 = (bf16[24,3200]{1,0:T(8,128)(2,1)S(1)}, bf16[24,3200]{1,0:T(8,128)(2,1)S(1)}, u32[]{:S(2)}, u32[]{:S(2)}) collective-permute-start(bf16[24,3200]{1,0:T(8,128)(2,1)S(1)} %shard_map.259.refs_1_), channel_id=1, source_target_pairs={{0,8},{4,12},{8,0},{12,4},{16,24},{20,28},{24,16},{28,20},{1,9},{5... | collective-permute-start | bytes 460808 | tf_op jit(solution)/shard_map/ppermute | solution.py:49
  206.1 20.2 %collective-permute-start.48 = (bf16[128,768]{1,0:T(8,128)(2,1)S(1)}, bf16[128,768]{1,0:T(8,128)(2,1)S(1)}, u32[]{:S(2)}, u32[]{:S(2)}) collective-permute-start(bf16[128,768]{1,0:T(8,128)(2,1)S(1)} %fusion.1), channel_id=1, source_target_pairs={{0,2},{1,3},{2,0},{3,1},{4,6},{5,7},{6,4},{7,5},{8,10},{9,11},{10,... | collective-permute-start | bytes 589832 | tf_op jit(solution)/shard_map/ppermute | solution.py:49
  207.2 20.7 %collective-permute-start.59 = (bf16[24,3200]{1,0:T(8,128)(2,1)S(1)}, bf16[24,3200]{1,0:T(8,128)(2,1)S(1)}, u32[]{:S(2)}, u32[]{:S(2)}) collective-permute-start(bf16[24,3200]{1,0:T(8,128)(2,1)S(1)} %shard_map.259.refs_1_), channel_id=1, source_target_pairs={{0,4},{4,0},{8,12},{12,8},{16,20},{20,16},{24,28},{28,24},{1,5},{5... | collective-permute-start | bytes 460808 | tf_op jit(solution)/shard_map/ppermute | solution.py:49
  210.4 17.5 %collective-permute-start.65 = (bf16[24,3200]{1,0:T(8,128)(2,1)S(1)}, bf16[24,3200]{1,0:T(8,128)(2,1)S(1)}, u32[]{:S(2)}, u32[]{:S(2)}) collective-permute-start(bf16[24,3200]{1,0:T(8,128)(2,1)S(1)} %collective-permute-done.64.refs_7_), channel_id=1, source_target_pairs={{0,4},{4,0},{8,12},{12,8},{16,20},{20,16},{24,28},{28,24},{1,5},{5... | collective-permute-start | bytes 460808 | tf_op jit(solution)/shard_map/ppermute | solution.py:49
  219.4 8.5 %collective-permute-start.63 = (bf16[24,3200]{1,0:T(8,128)(2,1)S(1)}, bf16[24,3200]{1,0:T(8,128)(2,1)S(1)}, u32[]{:S(2)}, u32[]{:S(2)}) collective-permute-start(bf16[24,3200]{1,0:T(8,128)(2,1)S(1)} %collective-permute-done.62.refs_5_), channel_id=1, source_target_pairs={{0,4},{4,0},{8,12},{12,8},{16,20},{20,16},{24,28},{28,24},{1,5},{5... | collective-permute-start | bytes 460808 | tf_op jit(solution)/shard_map/ppermute | solution.py:49
  220.9 7.7 %collective-permute-start.61 = (bf16[24,3200]{1,0:T(8,128)(2,1)S(1)}, bf16[24,3200]{1,0:T(8,128)(2,1)S(1)}, u32[]{:S(2)}, u32[]{:S(2)}) collective-permute-start(bf16[24,3200]{1,0:T(8,128)(2,1)S(1)} %collective-permute-done.60.refs_3_), channel_id=1, source_target_pairs={{0,4},{4,0},{8,12},{12,8},{16,20},{20,16},{24,28},{28,24},{1,5},{5... | collective-permute-start | bytes 460808 | tf_op jit(solution)/shard_map/ppermute | solution.py:49
  (27 other events, 235.4 us)

commit v2 on v1

--- a/solution.py
+++ b/solution.py
@@ -94,8 +94,8 @@
         me = lax.axis_index(E)
         whole = jnp.stack(parts)[me ^ jnp.arange(count, dtype=jnp.int32)]
         return [lax.psum_scatter(whole, E, scatter_dimension=0)]
-    got = {s: swap(parts[s ^ 1], E, 1) for s in (4, 6, 2, 0)}
-    terms = [parts[0], got[0]]
+    got = {s: swap(parts[s ^ 1], E, 1) for s in (4, 6, 2)}
+    terms = [parts[0], swap(tie(parts[1], got[4]), E, 1)]
     for s in (4, 6, 2):
         part = (parts[s].astype(wide) + got[s].astype(wide)).astype(low)
         terms.append(swap(part, E, s))
@@ -363,15 +363,11 @@
 
 
 def result_kernel(order, me_ref, weight_ref, act_a, act_b, logits_a, logits_b, *refs):
-    rows, (own_ref, across_ref, pair_ref, router_ref) = refs[:SHARDS], refs[SHARDS:]
+    rows, outs, router_ref = refs[:SHARDS], refs[SHARDS:-1], refs[-1]
     router = jnp.zeros(router_ref.shape, wide)
     for k, s in enumerate(order):
         here = slice((k % 2) * CAP, (k % 2 + 1) * CAP)
-        result = matmul((act_a, act_b)[k // 2][here, :], weight_ref[...]).astype(low)
-        if s % 2 == 0:
-            (own_ref, across_ref)[s // 2][...] = result
-        else:
-            pair_ref[(3 - s) // 2] = result
+        outs[s][...] = matmul((act_a, act_b)[k // 2][here, :], weight_ref[...]).astype(low)
         router = router + along_first(rows[s][...], (logits_a, logits_b)[k // 2][here, :])
     router_ref[...] = router
 
@@ -641,6 +637,7 @@
         me,
         cotangent,
         routes.T,
+        room=FULL,
     )
     sent = [sent, swap(sent, E, 2), swap(sent, E, 4), swap(sent, E, 6)] if quick else gather_e(sent)
 
@@ -662,19 +659,17 @@
         *tokens_rel,
         *weight_rel,
         segments,
-        room=FULL,
         cover=20,
     )
     tokens_all, first, qkv, probs, attended, weight, small, router = outs
-    near_sent = sent if quick else sent[:4]
     *branches, stacked = call(
         branch_kernel,
-        three_rows + [((len(near_sent), rows + 16, width), low)],
+        three_rows + [((4, rows + 16, width), low)],
         [((SHARDS, rows, width), low)],
         me,
         attended,
         output_weight,
-        *near_sent,
+        *sent[:4],
     )
     branch_terms, _ = sum_w(*branches)
     resid, second = call(
@@ -752,21 +747,9 @@
     halves.append(expert_half(1, ()))
     near = swap(halves[1][1], W, 1)
     across = (halves[1][0].astype(wide) + near.astype(wide)).astype(low)
-    back_parts = call(
-        unpack_kernel,
-        [(row, low)] * experts,
-        [],
-        me,
-        dispatch,
-        halves[0][0],
-        swap(halves[0][1], W, 1),
-        swap(across, W, 2),
-    )
-    back_terms = sum_e(back_parts)
-
     *results, router_grad = call(
         lambda *refs: result_kernel(order, *refs),
-        [(packed_row, low), (packed_row, low), ((2,) + packed_row, low), ((width, LANES), wide)],
+        [(packed_row, low)] * SHARDS + [((width, LANES), wide)],
         [],
         me,
         second_local,
@@ -777,7 +760,22 @@
         *rows_rel,
         after=(across,),
     )
-    result_terms, _ = sum_w(*results)
+    back_parts = call(
+        unpack_kernel,
+        [(row, low)] * experts,
+        [],
+        me,
+        dispatch,
+        halves[0][0],
+        swap(halves[0][1], W, 1),
+        swap(across, W, 2),
+        after=(results[0],),
+    )
+    back_terms = sum_e(back_parts)
+
+    near = swap(results[3], W, 1)
+    across = (results[2].astype(wide) + near.astype(wide)).astype(low)
+    result_terms = [results[0], swap(results[1], W, 1), swap(across, W, 2)]
     if quick:
         (mixed,) = call(total_kernel, [(packed_row, low)], [], me, *result_terms)
         mixed_parts = call(
@@ -799,7 +797,7 @@
         *back_terms,
         after=(mixed_parts[0],),
     )
-    back_rel = gather_w(back_branch)
+    back_rel = exchange_w([back_branch] * SHARDS)
     columns = 3 * shard + LANES
     piece = shard // experts
     part = (SHARDS, piece, columns + shard)
@@ -822,9 +820,9 @@
         cover=20,
     )
     grads = list(outs[3:])
-    (layer_out,) = call(layer_kernel, [(row, low)], [], me, resid, *mixed_terms, after=(grads[0],))
+    (layer_out,) = call(layer_kernel, [(row, low)], [], me, resid, *mixed_terms, after=(grads[-1],))
     if quick:
-        grads[5] = tie(grads[5], layer_out)
+        grads[5] = tie(grads[5], *mixed_terms[1:])
     back_terms, _ = sum_w(*outs[:3])
     (tokens_grad,) = call(
         tokens_back_kernel,

time: 232 us -> 217 us (0.935)
  waiting for transfers between devices: 103 us -> 75.9 us
  starting transfers between devices: 67.5 us -> 83.7 us
    ppermute x66 -> x67, waiting for transfers between devices: 103 us -> 75.9 us  [swap(): return lax.ppermute(value, axis, [(i, i ^ step) for i in range(count)])]
    ppermute x66 -> x67, starting transfers between devices: 67.5 us -> 83.7 us  [swap(): return lax.ppermute(value, axis, [(i, i ^ step) for i in range(count)])]
    unnamed x51 -> x23, local copies, waits for them, and re-layouts: 5.6 us -> 3.92 us
  transfers between devices with their start and end apart: 66 -> 67, of which waited for: 33 -> 31; matrix products, arithmetic and copies ran while one was open for 0% -> 1% of each run, Pallas kernels for 17% -> 20%
where the time goes in v2:
time: 217 us
  starting transfers between devices  83.7 us (39%)
  waiting for transfers between devices  75.9 us (35%)
  Pallas kernels  50.6 us (23%)
  local copies, waits for them, and re-layouts  3.92 us (2%)
    ppermute x67, starting transfers between devices, swap(): return lax.ppermute(value, axis, [(i, i ^ step) for i in range(count)])  83.7 us
    ppermute x67, waiting for transfers between devices, swap(): return lax.ppermute(value, axis, [(i, i ^ step) for i in range(count)])  75.9 us
    pallas_call x22, Pallas kernels, call(): pl.pallas_call(lambda *refs: kernel(*refs[skip:]), out_shape=tuple((jax.S...  50.6 us
  transfers between devices with their start and end apart: 67, of which 31 were waited for; matrix products, arithmetic and copies ran while one was open for 1% of the time, Pallas kernels for 20%

profile of v2, /device:TPU:0, one launch (start us, length us, event | category | flops | bytes accessed | tf_op | source)
XLA Modules:
  0.0 216.8 jit_solution(8404070005872211448)
XLA Ops:
  0.6 3.0 %collective-permute-start.1 = (bf16[128,768]{1,0:T(8,128)(2,1)}, bf16[128,768]{1,0:T(8,128)(2,1)S(1)}, u32[]{:S(2)}, u32[]{:S(2)}) collective-permute-start(bf16[128,768]{1,0:T(8,128)(2,1)} %refs_1_.11), channel_id=1, source_target_pairs={{0,2},{1,3},{2,0},{3,1},{4,6},{5,7},{6,4},{7,5},{8,10},{9,11},{10,... | collective-permute-start | bytes 589832 | tf_op jit(solution)/shard_map/ppermute | solution.py:49
  4.9 2.4 %shard_map.238 = (bf16[224,576]{1,0:T(8,128)(2,1)}, bf16[224,576]{1,0:T(8,128)(2,1)}, bf16[224,576]{1,0:T(8,128)(2,1)}, bf16[224,576]{1,0:T(8,128)(2,1)}) custom-call(s32[3]{0:T(128)} %pad_add_fusion.refs_0_.refs_1_.refs_2_, bf16[192,768]{1,0:T(8,128)(2,1)} %refs_1_.6, bf16[192,768]{1,0:T(8,128)(2,1)} %refs_2_.2, bf16[192,768]{1,0:T(8,128)(2,1)} %refs_3_.1, ...), custom_call_target="tpu_custom_call" | custom-call | flops 1 | bytes 1 | tf_op jit(solution)/shard_map/pallas_call | solution.py:132
  7.3 1.8 collective-permute-start.5
  9.7 1.6 shard_map.240.refs_3_.refs_2_
  11.4 1.6 collective-permute-start.6
  12.9 2.6 %collective-permute-start.7 = (bf16[144,768]{1,0:T(8,128)(2,1)}, bf16[144,768]{1,0:T(8,128)(2,1)S(1)}, u32[]{:S(2)}, u32[]{:S(2)}) collective-permute-start(bf16[144,768]{1,0:T(8,128)(2,1)} %shard_map.240.refs_3_.refs_2_), channel_id=1, source_target_pairs={{0,16},{4,20},{8,24},{12,28},{16,0},{20,4},{24,8},{28,12},{1,17},{... | collective-permute-start | bytes 663560 | tf_op jit(solution)/shard_map/ppermute | solution.py:49
  15.5 1.7 collective-permute-done.4.refs_7_
  17.2 3.6 %collective-permute-start.8 = (bf16[144,768]{1,0:T(8,128)(2,1)}, bf16[144,768]{1,0:T(8,128)(2,1)S(1)}, u32[]{:S(2)}, u32[]{:S(2)}) collective-permute-start(bf16[144,768]{1,0:T(8,128)(2,1)} %shard_map.240.refs_3_.refs_2_), channel_id=1, source_target_pairs={{0,24},{4,28},{8,16},{12,20},{16,8},{20,12},{24,0},{28,4},{1,25},{... | collective-permute-start | bytes 663560 | tf_op jit(solution)/shard_map/ppermute | solution.py:49
  20.8 1.8 collective-permute-done.5.refs_8_
  25.8 5.3 %shard_map.239 = (bf16[4,128,768]{2,1,0:T(8,128)(2,1)S(1)}, bf16[512,768]{1,0:T(8,128)(2,1)S(1)}, bf16[512,576]{1,0:T(8,128)(2,1)S(1)}, bf16[3,512,512]{2,1,0:T(...) custom-call(s32[3]{0:T(128)S(1)} %copy-done.7, ...), custom_call_target="tpu_custom_call" | custom-call | flops 20000000000 | bytes 1 | tf_op jit(solution)/shard_map/pallas_call | solution.py:132
  32.9 1.6 collective-permute-start.11
  35.6 6.2 %collective-permute-done.10.refs_5_ = bf16[128,768]{1,0:T(8,128)(2,1)S(1)} collective-permute-done((bf16[128,768]{1,0:T(8,128)(2,1)S(1)}, bf16[128,768]{1,0:T(8,128)(2,1)S(1)}, u32[]{:S(2)}, u32[]{:S(2)}) %collective-permute-start.10) | collective-permute-done | bytes 196640 | tf_op jit(solution)/shard_map/ppermute | solution.py:49
  42.5 4.4 %collective-permute-start.19 = (bf16[128,768]{1,0:T(8,128)(2,1)S(1)}, bf16[128,768]{1,0:T(8,128)(2,1)S(1)}, u32[]{:S(2)}, u32[]{:S(2)}) collective-permute-start(bf16[128,768]{1,0:T(8,128)(2,1)S(1)} %get-tuple-element.112.refs_0_.refs_4_), channel_id=1, source_target_pairs={{0,8},{4,12},{8,0},{12,4},{16,24},{20,28},{24,16},{28,20},{1,9},{5... | collective-permute-start | bytes 589832 | tf_op jit(solution)/shard_map/ppermute | solution.py:49
  48.0 1.4 collective-permute-start.23
  49.4 1.5 collective-permute-start.18
  50.9 4.6 %collective-permute-done.11.refs_6_ = bf16[4,144,768]{2,1,0:T(8,128)(2,1)S(1)} collective-permute-done((bf16[4,144,768]{2,1,0:T(8,128)(2,1)S(1)}, bf16[4,144,768]{2,1,0:T(8,128)(2,1)S(1)}, u32[]{:S(2)}, u32[]{:S(2)}) %collective-permute-start.11) | collective-permute-done | bytes 884768 | tf_op jit(solution)/shard_map/ppermute | solution.py:49
  55.5 1.8 shard_map.243
  58.2 1.5 collective-permute-start.20
  59.7 4.4 %collective-permute-done.21.refs_8_ = bf16[128,768]{1,0:T(8,128)(2,1)S(1)} collective-permute-done((bf16[128,768]{1,0:T(8,128)(2,1)S(1)}, bf16[128,768]{1,0:T(8,128)(2,1)S(1)}, u32[]{:S(2)}, u32[]{:S(2)}) %collective-permute-start.21) | collective-permute-done | bytes 196640 | tf_op jit(solution)/shard_map/ppermute | solution.py:49
  64.1 1.5 collective-permute-start.22
  67.1 3.1 %collective-permute-done.22.refs_9_ = bf16[128,768]{1,0:T(8,128)(2,1)S(1)} collective-permute-done((bf16[128,768]{1,0:T(8,128)(2,1)S(1)}, bf16[128,768]{1,0:T(8,128)(2,1)S(1)}, u32[]{:S(2)}, u32[]{:S(2)}) %collective-permute-start.22) | collective-permute-done | bytes 196640 | tf_op jit(solution)/shard_map/ppermute | solution.py:49
  70.2 2.1 collective-permute-done.24.refs_11_
  72.3 1.5 shard_map.245.refs_7_.refs_6_
  73.9 1.3 collective-permute-start.25
  77.3 3.7 %shard_map.244 = (f32[256,768]{1,0:T(8,128)S(1)}, f32[256,768]{1,0:T(8,128)S(1)}, f32[256,768]{1,0:T(8,128)S(1)}, f32[256,768]{1,0:T(8,128)S(1)}, f32[256,128]{1...) custom-call(s32[3]{0:T(128)S(1)} %copy-done.7, ...), custom_call_target="tpu_custom_call" | custom-call | flops 1 | bytes 1 | tf_op jit(solution)/shard_map/pallas_call | solution.py:132
  81.0 4.2 %shard_map.246 = (bf16[256,768]{1,0:T(8,128)(2,1)S(1)}, bf16[256,768]{1,0:T(8,128)(2,1)S(1)}, bf16[512,768]{1,0:T(8,128)(2,1)S(1)}, bf16[512,768]{1,0:T(8,128)(2,1)S(1)}, bf16[512,128]{1,0:T(8,128)(2,1)S(1)}) custom-call(s32[3]{0:T(128)S(1)} %copy-done.7, f32[256,768]{1,0:T(8,128)S(1)} %get-tuple-element.123.refs_1_, ...), custom_call_target="tpu_custom_call" | custom-call | flops 1 | bytes 1 | tf_op jit(solution)/shard_map/pallas_call | solution.py:132
  85.5 1.7 collective-permute-done.27.refs_8_.refs_10_.refs_9_
  87.2 4.0 %shard_map.248 = (bf16[256,768]{1,0:T(8,128)(2,1)S(1)}, bf16[256,768]{1,0:T(8,128)(2,1)S(1)}, bf16[512,768]{1,0:T(8,128)(2,1)S(1)}, bf16[512,768]{1,0:T(8,128)(2,1)S(1)}, bf16[512,128]{1,0:T(8,128)(2,1)S(1)}) custom-call(s32[3]{0:T(128)S(1)} %copy-done.7, f32[256,768]{1,0:T(8,128)S(1)} %get-tuple-element.118.refs_1_, ...), custom_call_target="tpu_custom_call" | custom-call | flops 1 | bytes 1 | tf_op jit(solution)/shard_map/pallas_call | solution.py:132
  93.1 1.3 collective-permute-start.34
  94.4 2.4 %shard_map.249 = (bf16[256,768]{1,0:T(8,128)(2,1)S(1)}, bf16[256,768]{1,0:T(8,128)(2,1)S(1)}, bf16[256,768]{1,0:T(8,128)(2,1)S(1)}, bf16[256,768]{1,0:T(8,128)(2,1)S(1)}, f32[768,128]{1,0:T(8,128)S(1)}) custom-call(bf16[256,768]{1,0:T(8,128)(2,1)S(1)} %add_convert_fusion.1.refs_0_, s32[3]{0:T(128)S(1)} %copy-done.7, bf16[768,768]{1,0:T(8,128)(2,1)S(1)} %bitcast.19, ...), custom_call_target="tpu_custom_call" | custom-call | flops 1 | bytes 1 | tf_op jit(solution)/shard_map/pallas_call | solution.py:132
  97.3 7.0 %collective-permute-done.34.refs_5_ = bf16[256,768]{1,0:T(8,128)(2,1)S(1)} collective-permute-done((bf16[256,768]{1,0:T(8,128)(2,1)S(1)}, bf16[256,768]{1,0:T(8,128)(2,1)S(1)}, u32[]{:S(2)}, u32[]{:S(2)}) %collective-permute-start.34) | collective-permute-done | bytes 393248 | tf_op jit(solution)/shard_map/ppermute | solution.py:49
  105.5 1.6 collective-permute-start.35
  107.2 1.3 collective-permute-start.31
  109.0 1.5 collective-permute-start.40
  110.6 2.9 %collective-permute-done.35.refs_1_ = bf16[128,768]{1,0:T(8,128)(2,1)S(1)} collective-permute-done((bf16[128,768]{1,0:T(8,128)(2,1)S(1)}, bf16[128,768]{1,0:T(8,128)(2,1)S(1)}, u32[]{:S(2)}, u32[]{:S(2)}) %collective-permute-start.35) | collective-permute-done | bytes 196640 | tf_op jit(solution)/shard_map/ppermute | solution.py:49
  113.4 1.5 collective-permute-start.36
  115.0 2.6 %collective-permute-done.38 = bf16[128,768]{1,0:T(8,128)(2,1)S(1)} collective-permute-done((bf16[128,768]{1,0:T(8,128)(2,1)S(1)}, bf16[128,768]{1,0:T(8,128)(2,1)S(1)}, u32[]{:S(2)}, u32[]{:S(2)}) %collective-permute-start.38) | collective-permute-done | bytes 196640 | tf_op jit(solution)/shard_map/ppermute | solution.py:49
  117.7 5.6 %collective-permute-start.37 = (bf16[128,768]{1,0:T(8,128)(2,1)S(1)}, bf16[128,768]{1,0:T(8,128)(2,1)S(1)}, u32[]{:S(2)}, u32[]{:S(2)}) collective-permute-start(bf16[128,768]{1,0:T(8,128)(2,1)S(1)} %add_convert_fusion.4), channel_id=1, source_target_pairs={{0,16},{4,20},{8,24},{12,28},{16,0},{20,4},{24,8},{28,12},{1,17},{... | collective-permute-start | bytes 589832 | tf_op jit(solution)/shard_map/ppermute | solution.py:49
  123.3 1.4 collective-permute-start.39
  125.5 1.6 collective-permute-start.32
  127.2 6.1 %collective-permute-done.32.refs_4_ = bf16[256,768]{1,0:T(8,128)(2,1)S(1)} collective-permute-done((bf16[256,768]{1,0:T(8,128)(2,1)S(1)}, bf16[256,768]{1,0:T(8,128)(2,1)S(1)}, u32[]{:S(2)}, u32[]{:S(2)}) %collective-permute-start.32) | collective-permute-done | bytes 393248 | tf_op jit(solution)/shard_map/ppermute | solution.py:49
  138.6 3.8 %collective-permute-start.45 = (bf16[128,768]{1,0:T(8,128)(2,1)S(1)}, bf16[128,768]{1,0:T(8,128)(2,1)S(1)}, u32[]{:S(2)}, u32[]{:S(2)}) collective-permute-start(bf16[128,768]{1,0:T(8,128)(2,1)S(1)} %get-tuple-element.153), channel_id=1, source_target_pairs={{0,16},{4,20},{8,24},{12,28},{16,0},{20,4},{24,8},{28,12},{1,17},{... | collective-permute-start | bytes 589832 | tf_op jit(solution)/shard_map/ppermute | solution.py:49
  142.4 1.4 collective-permute-start.46
  144.5 3.3 %collective-permute-done.44.refs_13_ = bf16[128,768]{1,0:T(8,128)(2,1)S(1)} collective-permute-done((bf16[128,768]{1,0:T(8,128)(2,1)S(1)}, bf16[128,768]{1,0:T(8,128)(2,1)S(1)}, u32[]{:S(2)}, u32[]{:S(2)}) %collective-permute-start.44) | collective-permute-done | bytes 196640 | tf_op jit(solution)/shard_map/ppermute | solution.py:49
  147.8 6.7 %shard_map.255 = (bf16[128,768]{1,0:T(8,128)(2,1)S(1)}, bf16[128,768]{1,0:T(8,128)(2,1)S(1)}, bf16[2,128,768]{2,1,0:T(8,128)(2,1)S(1)}, bf16[4,24,896]{2,1,0:T(8...) custom-call(s32[3]{0:T(128)S(1)} %copy-done.8, ...), custom_call_target="tpu_custom_call" | custom-call | flops 20000000000 | bytes 1 | tf_op jit(solution)/shard_map/pallas_call | solution.py:132
  154.5 2.1 collective-permute-done.45.refs_4_.refs_1_
  157.6 1.5 collective-permute-start.50
  159.6 1.5 collective-permute-start.55
  161.2 2.7 %collective-permute-done.50.refs_1_ = bf16[4,24,896]{2,1,0:T(8,128)(2,1)S(1)} collective-permute-done((bf16[4,24,896]{2,1,0:T(8,128)(2,1)S(1)}, bf16[4,24,896]{2,1,0:T(8,128)(2,1)S(1)}, u32[]{:S(2)}, u32[]{:S(2)}) %collective-permute-start.50) | collective-permute-done | bytes 172064 | tf_op jit(solution)/shard_map/ppermute | solution.py:49
  163.9 2.5 %collective-permute-start.51 = (bf16[4,24,896]{2,1,0:T(8,128)(2,1)S(1)}, bf16[4,24,896]{2,1,0:T(8,128)(2,1)S(1)}, u32[]{:S(2)}, u32[]{:S(2)}) collective-permute-start(bf16[4,24,896]{2,1,0:T(8,128)(2,1)S(1)} %shard_map.259), channel_id=1, source_target_pairs={{0,4},{4,0},{8,12},{12,8},{16,20},{20,16},{24,28},{28,24},{1,5},{5... | collective-permute-start | bytes 516104 | tf_op jit(solution)/shard_map/ppermute | solution.py:49
  166.4 3.5 %collective-permute-start.52 = (bf16[4,24,896]{2,1,0:T(8,128)(2,1)S(1)}, bf16[4,24,896]{2,1,0:T(8,128)(2,1)S(1)}, u32[]{:S(2)}, u32[]{:S(2)}) collective-permute-start(bf16[4,24,896]{2,1,0:T(8,128)(2,1)S(1)} %add_convert_fusion.7), channel_id=1, source_target_pairs={{0,16},{4,20},{8,24},{12,28},{16,0},{20,4},{24,8},{28,12},{1,17},{... | collective-permute-start | bytes 516104 | tf_op jit(solution)/shard_map/ppermute | solution.py:49
  169.9 2.5 %collective-permute-start.54 = (bf16[4,24,896]{2,1,0:T(8,128)(2,1)S(1)}, bf16[4,24,896]{2,1,0:T(8,128)(2,1)S(1)}, u32[]{:S(2)}, u32[]{:S(2)}) collective-permute-start(bf16[4,24,896]{2,1,0:T(8,128)(2,1)S(1)} %add_convert_fusion.6), channel_id=1, source_target_pairs={{0,24},{4,28},{8,16},{12,20},{16,8},{20,12},{24,0},{28,4},{1,25},{... | collective-permute-start | bytes 516104 | tf_op jit(solution)/shard_map/ppermute | solution.py:49
  172.5 3.3 %collective-permute-start.56 = (bf16[4,24,896]{2,1,0:T(8,128)(2,1)S(1)}, bf16[4,24,896]{2,1,0:T(8,128)(2,1)S(1)}, u32[]{:S(2)}, u32[]{:S(2)}) collective-permute-start(bf16[4,24,896]{2,1,0:T(8,128)(2,1)S(1)} %add_convert_fusion.5), channel_id=1, source_target_pairs={{0,8},{4,12},{8,0},{12,4},{16,24},{20,28},{24,16},{28,20},{1,9},{5... | collective-permute-start | bytes 516104 | tf_op jit(solution)/shard_map/ppermute | solution.py:49
  175.8 5.5 %collective-permute-done.52.refs_3_ = bf16[4,24,896]{2,1,0:T(8,128)(2,1)S(1)} collective-permute-done((bf16[4,24,896]{2,1,0:T(8,128)(2,1)S(1)}, bf16[4,24,896]{2,1,0:T(8,128)(2,1)S(1)}, u32[]{:S(2)}, u32[]{:S(2)}) %collective-permute-start.52) | collective-permute-done | bytes 172064 | tf_op jit(solution)/shard_map/ppermute | solution.py:49
  184.5 2.2 collective-permute-done.58.refs_3_
  187.9 2.0 collective-permute-start.61
  190.6 1.7 collective-permute-start.65
  194.8 1.9 collective-permute-done.61.refs_3_
  197.8 6.4 %collective-permute-done.63.refs_5_ = bf16[24,3200]{1,0:T(8,128)(2,1)S(1)} collective-permute-done((bf16[24,3200]{1,0:T(8,128)(2,1)S(1)}, bf16[24,3200]{1,0:T(8,128)(2,1)S(1)}, u32[]{:S(2)}, u32[]{:S(2)}) %collective-permute-start.63) | collective-permute-done | bytes 153632 | tf_op jit(solution)/shard_map/ppermute | solution.py:49
  204.7 1.5 collective-permute-start.66
  206.2 1.3 shard_map.256
  207.6 4.9 %shard_map.263 = (f32[1,768,768]{2,1,0:T(8,128)}, f32[1,768,768]{2,1,0:T(8,128)}) custom-call(bf16[4,24,896]{2,1,0:T(8,128)(2,1)S(1)} %get-tuple-element.152.refs_0_, s32[3]{0:T(128)S(1)} %copy-done.8, bf16[512,768]{1,0:T(8,128)(2,1)S(1)} %get-tuple-element.130.refs_3_.refs_2_, bf16[512,768]{1,0:T(8,128)(2,1)S(1)} %get-tuple-element.131.refs_4_.refs_3_, ...), custom_call_target="tpu_custom_call" | custom-call | flops 1 | bytes 1 | tf_op jit(solution)/shard_map/pallas_call | solution.py:132
  212.5 1.5 shard_map.257
  214.0 2.1 shard_map.262
  (130 shorter events, 36.7 us)
Async XLA Ops:
  0.6 8.8 %collective-permute-start.1 = (bf16[128,768]{1,0:T(8,128)(2,1)}, bf16[128,768]{1,0:T(8,128)(2,1)S(1)}, u32[]{:S(2)}, u32[]{:S(2)}) collective-permute-start(bf16[128,768]{1,0:T(8,128)(2,1)} %refs_1_.11), channel_id=1, source_target_pairs={{0,2},{1,3},{2,0},{3,1},{4,6},{5,7},{6,4},{7,5},{8,10},{9,11},{10,... | collective-permute-start | bytes 589832 | tf_op jit(solution)/shard_map/ppermute | solution.py:49
  7.3 5.6 %collective-permute-start.3 = (bf16[224,576]{1,0:T(8,128)(2,1)}, bf16[224,576]{1,0:T(8,128)(2,1)S(1)}, u32[]{:S(2)}, u32[]{:S(2)}) collective-permute-start(bf16[224,576]{1,0:T(8,128)(2,1)} %get-tuple-element.99), channel_id=1, source_target_pairs={{0,1},{1,0},{2,3},{3,2},{4,5},{5,4},{6,7},{7,6},{8,9},{9,8},{10,11... | collective-permute-start | bytes 774152 | tf_op jit(solution)/shard_map/ppermute | solution.py:49
  7.3 9.9 %collective-permute-start.4 = (bf16[224,576]{1,0:T(8,128)(2,1)}, bf16[224,576]{1,0:T(8,128)(2,1)S(1)}, u32[]{:S(2)}, u32[]{:S(2)}) collective-permute-start(bf16[224,576]{1,0:T(8,128)(2,1)} %get-tuple-element.100), channel_id=1, source_target_pairs={{0,2},{1,3},{2,0},{3,1},{4,6},{5,7},{6,4},{7,5},{8,10},{9,11},{10,... | collective-permute-start | bytes 774152 | tf_op jit(solution)/shard_map/ppermute | solution.py:49
  7.3 15.2 %collective-permute-start.5 = (bf16[224,576]{1,0:T(8,128)(2,1)}, bf16[224,576]{1,0:T(8,128)(2,1)S(1)}, u32[]{:S(2)}, u32[]{:S(2)}) collective-permute-start(bf16[224,576]{1,0:T(8,128)(2,1)} %get-tuple-element.101), channel_id=1, source_target_pairs={{0,3},{1,2},{2,1},{3,0},{4,7},{5,6},{6,5},{7,4},{8,11},{9,10},{10,... | collective-permute-start | bytes 774152 | tf_op jit(solution)/shard_map/ppermute | solution.py:49
  9.2 2.2 collective-permute-start
  9.5 13.1 %collective-permute-start.2 = (bf16[128,768]{1,0:T(8,128)(2,1)S(1)}, bf16[128,768]{1,0:T(8,128)(2,1)S(1)}, u32[]{:S(2)}, u32[]{:S(2)}) collective-permute-start(bf16[128,768]{1,0:T(8,128)(2,1)S(1)} %collective-permute-done.1.refs_3_), channel_id=1, source_target_pairs={{0,1},{1,0},{2,3},{3,2},{4,5},{5,4},{6,7},{7,6},{8,9},{9,8},{10,11... | collective-permute-start | bytes 589832 | tf_op jit(solution)/shard_map/ppermute | solution.py:49
  11.4 19.8 %collective-permute-start.6 = (bf16[144,768]{1,0:T(8,128)(2,1)}, bf16[144,768]{1,0:T(8,128)(2,1)S(1)}, u32[]{:S(2)}, u32[]{:S(2)}) collective-permute-start(bf16[144,768]{1,0:T(8,128)(2,1)} %shard_map.240.refs_3_.refs_2_), channel_id=1, source_target_pairs={{0,8},{4,12},{8,0},{12,4},{16,24},{20,28},{24,16},{28,20},{1,9},{5... | collective-permute-start | bytes 663560 | tf_op jit(solution)/shard_map/ppermute | solution.py:49
  12.9 18.9 %collective-permute-start.7 = (bf16[144,768]{1,0:T(8,128)(2,1)}, bf16[144,768]{1,0:T(8,128)(2,1)S(1)}, u32[]{:S(2)}, u32[]{:S(2)}) collective-permute-start(bf16[144,768]{1,0:T(8,128)(2,1)} %shard_map.240.refs_3_.refs_2_), channel_id=1, source_target_pairs={{0,16},{4,20},{8,24},{12,28},{16,0},{20,4},{24,8},{28,12},{1,17},{... | collective-permute-start | bytes 663560 | tf_op jit(solution)/shard_map/ppermute | solution.py:49
  17.2 14.7 %collective-permute-start.8 = (bf16[144,768]{1,0:T(8,128)(2,1)}, bf16[144,768]{1,0:T(8,128)(2,1)S(1)}, u32[]{:S(2)}, u32[]{:S(2)}) collective-permute-start(bf16[144,768]{1,0:T(8,128)(2,1)} %shard_map.240.refs_3_.refs_2_), channel_id=1, source_target_pairs={{0,24},{4,28},{8,16},{12,20},{16,8},{20,12},{24,0},{28,4},{1,25},{... | collective-permute-start | bytes 663560 | tf_op jit(solution)/shard_map/ppermute | solution.py:49
  32.9 1.8 collective-permute-start.9
  32.9 22.5 %collective-permute-start.11 = (bf16[4,144,768]{2,1,0:T(8,128)(2,1)S(1)}, bf16[4,144,768]{2,1,0:T(8,128)(2,1)S(1)}, u32[]{:S(2)}, u32[]{:S(2)}) collective-permute-start(bf16[4,144,768]{2,1,0:T(8,128)(2,1)S(1)} %get-tuple-element.113), channel_id=1, source_target_pairs={{0,4},{4,0},{8,12},{12,8},{16,20},{20,16},{24,28},{28,24},{1,5},{5... | collective-permute-start | bytes 2654216 | tf_op jit(solution)/shard_map/ppermute | solution.py:49
  34.7 7.0 %collective-permute-start.10 = (bf16[128,768]{1,0:T(8,128)(2,1)S(1)}, bf16[128,768]{1,0:T(8,128)(2,1)S(1)}, u32[]{:S(2)}, u32[]{:S(2)}) collective-permute-start(bf16[128,768]{1,0:T(8,128)(2,1)S(1)} %fusion.1), channel_id=1, source_target_pairs={{0,2},{1,3},{2,0},{3,1},{4,6},{5,7},{6,4},{7,5},{8,10},{9,11},{10,... | collective-permute-start | bytes 589832 | tf_op jit(solution)/shard_map/ppermute | solution.py:49
  42.5 15.7 %collective-permute-start.19 = (bf16[128,768]{1,0:T(8,128)(2,1)S(1)}, bf16[128,768]{1,0:T(8,128)(2,1)S(1)}, u32[]{:S(2)}, u32[]{:S(2)}) collective-permute-start(bf16[128,768]{1,0:T(8,128)(2,1)S(1)} %get-tuple-element.112.refs_0_.refs_4_), channel_id=1, source_target_pairs={{0,8},{4,12},{8,0},{12,4},{16,24},{20,28},{24,16},{28,20},{1,9},{5... | collective-permute-start | bytes 589832 | tf_op jit(solution)/shard_map/ppermute | solution.py:49
  46.9 17.2 %collective-permute-start.21 = (bf16[128,768]{1,0:T(8,128)(2,1)S(1)}, bf16[128,768]{1,0:T(8,128)(2,1)S(1)}, u32[]{:S(2)}, u32[]{:S(2)}) collective-permute-start(bf16[128,768]{1,0:T(8,128)(2,1)S(1)} %get-tuple-element.112.refs_0_.refs_4_), channel_id=1, source_target_pairs={{0,16},{4,20},{8,24},{12,28},{16,0},{20,4},{24,8},{28,12},{1,17},{... | collective-permute-start | bytes 589832 | tf_op jit(solution)/shard_map/ppermute | solution.py:49
  48.0 17.6 %collective-permute-start.23 = (bf16[128,768]{1,0:T(8,128)(2,1)S(1)}, bf16[128,768]{1,0:T(8,128)(2,1)S(1)}, u32[]{:S(2)}, u32[]{:S(2)}) collective-permute-start(bf16[128,768]{1,0:T(8,128)(2,1)S(1)} %get-tuple-element.112.refs_0_.refs_4_), channel_id=1, source_target_pairs={{0,24},{4,28},{8,16},{12,20},{16,8},{20,12},{24,0},{28,4},{1,25},{... | collective-permute-start | bytes 589832 | tf_op jit(solution)/shard_map/ppermute | solution.py:49
  49.4 16.7 %collective-permute-start.18 = (bf16[128,768]{1,0:T(8,128)(2,1)S(1)}, bf16[128,768]{1,0:T(8,128)(2,1)S(1)}, u32[]{:S(2)}, u32[]{:S(2)}) collective-permute-start(bf16[128,768]{1,0:T(8,128)(2,1)S(1)} %get-tuple-element.112.refs_0_.refs_4_), channel_id=1, source_target_pairs={{0,4},{4,0},{8,12},{12,8},{16,20},{20,16},{24,28},{28,24},{1,5},{5... | collective-permute-start | bytes 589832 | tf_op jit(solution)/shard_map/ppermute | solution.py:49
  57.3 15.0 %collective-permute-start.15 = (bf16[144,768]{1,0:T(8,128)(2,1)S(1)}, bf16[144,768]{1,0:T(8,128)(2,1)S(1)}, u32[]{:S(2)}, u32[]{:S(2)}) collective-permute-start(bf16[144,768]{1,0:T(8,128)(2,1)S(1)} %get-tuple-element.117.refs_3_.refs_11_), channel_id=1, source_target_pairs={{0,2},{1,3},{2,0},{3,1},{4,6},{5,7},{6,4},{7,5},{8,10},{9,11},{10,... | collective-permute-start | bytes 663560 | tf_op jit(solution)/shard_map/ppermute | solution.py:49
  58.2 9.0 %collective-permute-start.20 = (bf16[128,768]{1,0:T(8,128)(2,1)S(1)}, bf16[128,768]{1,0:T(8,128)(2,1)S(1)}, u32[]{:S(2)}, u32[]{:S(2)}) collective-permute-start(bf16[128,768]{1,0:T(8,128)(2,1)S(1)} %collective-permute-done.19.refs_6_), channel_id=1, source_target_pairs={{0,4},{4,0},{8,12},{12,8},{16,20},{20,16},{24,28},{28,24},{1,5},{5... | collective-permute-start | bytes 589832 | tf_op jit(solution)/shard_map/ppermute | solution.py:49
  64.1 6.1 %collective-permute-start.22 = (bf16[128,768]{1,0:T(8,128)(2,1)S(1)}, bf16[128,768]{1,0:T(8,128)(2,1)S(1)}, u32[]{:S(2)}, u32[]{:S(2)}) collective-permute-start(bf16[128,768]{1,0:T(8,128)(2,1)S(1)} %collective-permute-done.21.refs_8_), channel_id=1, source_target_pairs={{0,4},{4,0},{8,12},{12,8},{16,20},{20,16},{24,28},{28,24},{1,5},{5... | collective-permute-start | bytes 589832 | tf_op jit(solution)/shard_map/ppermute | solution.py:49
  65.6 6.7 %collective-permute-start.24 = (bf16[128,768]{1,0:T(8,128)(2,1)S(1)}, bf16[128,768]{1,0:T(8,128)(2,1)S(1)}, u32[]{:S(2)}, u32[]{:S(2)}) collective-permute-start(bf16[128,768]{1,0:T(8,128)(2,1)S(1)} %collective-permute-done.23.refs_10_), channel_id=1, source_target_pairs={{0,4},{4,0},{8,12},{12,8},{16,20},{20,16},{24,28},{28,24},{1,5},{5... | collective-permute-start | bytes 589832 | tf_op jit(solution)/shard_map/ppermute | solution.py:49
  66.1 6.2 %collective-permute-start.14 = (bf16[128,768]{1,0:T(8,128)(2,1)S(1)}, bf16[128,768]{1,0:T(8,128)(2,1)S(1)}, u32[]{:S(2)}, u32[]{:S(2)}) collective-permute-start(bf16[128,768]{1,0:T(8,128)(2,1)S(1)} %get-tuple-element.116.refs_2_.refs_10_), channel_id=1, source_target_pairs={{0,2},{1,3},{2,0},{3,1},{4,6},{5,7},{6,4},{7,5},{8,10},{9,11},{10,... | collective-permute-start | bytes 589832 | tf_op jit(solution)/shard_map/ppermute | solution.py:49
  67.1 8.6 %collective-permute-start.12 = (bf16[128,768]{1,0:T(8,128)(2,1)S(1)}, bf16[128,768]{1,0:T(8,128)(2,1)S(1)}, u32[]{:S(2)}, u32[]{:S(2)}) collective-permute-start(bf16[128,768]{1,0:T(8,128)(2,1)S(1)} %get-tuple-element.116.refs_2_.refs_10_), channel_id=1, source_target_pairs={{0,1},{1,0},{2,3},{3,2},{4,5},{5,4},{6,7},{7,6},{8,9},{9,8},{10,11... | collective-permute-start | bytes 589832 | tf_op jit(solution)/shard_map/ppermute | solution.py:49
  73.9 7.2 %collective-permute-start.26 = (bf16[256,768]{1,0:T(8,128)(2,1)S(1)}, bf16[256,768]{1,0:T(8,128)(2,1)S(1)}, u32[]{:S(2)}, u32[]{:S(2)}) collective-permute-start(bf16[256,768]{1,0:T(8,128)(2,1)S(1)} %shard_map.245.refs_7_.refs_6_), channel_id=1, source_target_pairs={{0,1},{1,0},{2,3},{3,2},{4,5},{5,4},{6,7},{7,6},{8,9},{9,8},{10,11... | collective-permute-start | bytes 1179656 | tf_op jit(solution)/shard_map/ppermute | solution.py:49
  73.9 11.5 %collective-permute-start.25 = (bf16[256,768]{1,0:T(8,128)(2,1)S(1)}, bf16[256,768]{1,0:T(8,128)(2,1)S(1)}, u32[]{:S(2)}, u32[]{:S(2)}) collective-permute-start(bf16[256,768]{1,0:T(8,128)(2,1)S(1)} %shard_map.245.refs_7_.refs_6_), channel_id=1, source_target_pairs={{0,2},{1,3},{2,0},{3,1},{4,6},{5,7},{6,4},{7,5},{8,10},{9,11},{10,... | collective-permute-start | bytes 1179656 | tf_op jit(solution)/shard_map/ppermute | solution.py:49
  75.4 1.9 collective-permute-start.17
  91.2 1.8 collective-permute-start.28
  91.4 6.0 %collective-permute-start.33 = (bf16[256,768]{1,0:T(8,128)(2,1)S(1)}, bf16[256,768]{1,0:T(8,128)(2,1)S(1)}, u32[]{:S(2)}, u32[]{:S(2)}) collective-permute-start(bf16[256,768]{1,0:T(8,128)(2,1)S(1)} %get-tuple-element.140), channel_id=1, source_target_pairs={{0,1},{1,0},{2,3},{3,2},{4,5},{5,4},{6,7},{7,6},{8,9},{9,8},{10,11... | collective-permute-start | bytes 1179656 | tf_op jit(solution)/shard_map/ppermute | solution.py:49
  93.1 11.2 %collective-permute-start.34 = (bf16[256,768]{1,0:T(8,128)(2,1)S(1)}, bf16[256,768]{1,0:T(8,128)(2,1)S(1)}, u32[]{:S(2)}, u32[]{:S(2)}) collective-permute-start(bf16[256,768]{1,0:T(8,128)(2,1)S(1)} %add_convert_fusion.1.refs_0_), channel_id=1, source_target_pairs={{0,2},{1,3},{2,0},{3,1},{4,6},{5,7},{6,4},{7,5},{8,10},{9,11},{10,... | collective-permute-start | bytes 1179656 | tf_op jit(solution)/shard_map/ppermute | solution.py:49
  96.8 10.4 %collective-permute-start.30 = (bf16[256,768]{1,0:T(8,128)(2,1)S(1)}, bf16[256,768]{1,0:T(8,128)(2,1)S(1)}, u32[]{:S(2)}, u32[]{:S(2)}) collective-permute-start(bf16[256,768]{1,0:T(8,128)(2,1)S(1)} %get-tuple-element.137), channel_id=1, source_target_pairs={{0,1},{1,0},{2,3},{3,2},{4,5},{5,4},{6,7},{7,6},{8,9},{9,8},{10,11... | collective-permute-start | bytes 1179656 | tf_op jit(solution)/shard_map/ppermute | solution.py:49
  96.8 26.5 %collective-permute-start.29 = (bf16[256,768]{1,0:T(8,128)(2,1)S(1)}, bf16[256,768]{1,0:T(8,128)(2,1)S(1)}, u32[]{:S(2)}, u32[]{:S(2)}) collective-permute-start(bf16[256,768]{1,0:T(8,128)(2,1)S(1)} %get-tuple-element.135), channel_id=1, source_target_pairs={{0,1},{1,0},{2,3},{3,2},{4,5},{5,4},{6,7},{7,6},{8,9},{9,8},{10,11... | collective-permute-start | bytes 1179656 | tf_op jit(solution)/shard_map/ppermute | solution.py:49
  105.5 7.9 %collective-permute-start.35 = (bf16[128,768]{1,0:T(8,128)(2,1)S(1)}, bf16[128,768]{1,0:T(8,128)(2,1)S(1)}, u32[]{:S(2)}, u32[]{:S(2)}) collective-permute-start(bf16[128,768]{1,0:T(8,128)(2,1)S(1)} %get-tuple-element.143), channel_id=1, source_target_pairs={{0,4},{4,0},{8,12},{12,8},{16,20},{20,16},{24,28},{28,24},{1,5},{5... | collective-permute-start | bytes 589832 | tf_op jit(solution)/shard_map/ppermute | solution.py:49
  107.2 17.5 %collective-permute-start.31 = (bf16[256,768]{1,0:T(8,128)(2,1)S(1)}, bf16[256,768]{1,0:T(8,128)(2,1)S(1)}, u32[]{:S(2)}, u32[]{:S(2)}) collective-permute-start(bf16[256,768]{1,0:T(8,128)(2,1)S(1)} %add_convert_fusion), channel_id=1, source_target_pairs={{0,2},{1,3},{2,0},{3,1},{4,6},{5,7},{6,4},{7,5},{8,10},{9,11},{10,... | collective-permute-start | bytes 1179656 | tf_op jit(solution)/shard_map/ppermute | solution.py:49
  108.5 9.1 %collective-permute-start.38 = (bf16[128,768]{1,0:T(8,128)(2,1)S(1)}, bf16[128,768]{1,0:T(8,128)(2,1)S(1)}, u32[]{:S(2)}, u32[]{:S(2)}) collective-permute-start(bf16[128,768]{1,0:T(8,128)(2,1)S(1)} %get-tuple-element.146), channel_id=1, source_target_pairs={{0,4},{4,0},{8,12},{12,8},{16,20},{20,16},{24,28},{28,24},{1,5},{5... | collective-permute-start | bytes 589832 | tf_op jit(solution)/shard_map/ppermute | solution.py:49
  109.0 18.0 %collective-permute-start.40 = (bf16[128,768]{1,0:T(8,128)(2,1)S(1)}, bf16[128,768]{1,0:T(8,128)(2,1)S(1)}, u32[]{:S(2)}, u32[]{:S(2)}) collective-permute-start(bf16[128,768]{1,0:T(8,128)(2,1)S(1)} %get-tuple-element.148), channel_id=1, source_target_pairs={{0,4},{4,0},{8,12},{12,8},{16,20},{20,16},{24,28},{28,24},{1,5},{5... | collective-permute-start | bytes 589832 | tf_op jit(solution)/shard_map/ppermute | solution.py:49
  113.4 21.0 %collective-permute-start.36 = (bf16[128,768]{1,0:T(8,128)(2,1)S(1)}, bf16[128,768]{1,0:T(8,128)(2,1)S(1)}, u32[]{:S(2)}, u32[]{:S(2)}) collective-permute-start(bf16[128,768]{1,0:T(8,128)(2,1)S(1)} %shard_map.253), channel_id=1, source_target_pairs={{0,4},{4,0},{8,12},{12,8},{16,20},{20,16},{24,28},{28,24},{1,5},{5... | collective-permute-start | bytes 589832 | tf_op jit(solution)/shard_map/ppermute | solution.py:49
  117.7 17.1 %collective-permute-start.37 = (bf16[128,768]{1,0:T(8,128)(2,1)S(1)}, bf16[128,768]{1,0:T(8,128)(2,1)S(1)}, u32[]{:S(2)}, u32[]{:S(2)}) collective-permute-start(bf16[128,768]{1,0:T(8,128)(2,1)S(1)} %add_convert_fusion.4), channel_id=1, source_target_pairs={{0,16},{4,20},{8,24},{12,28},{16,0},{20,4},{24,8},{28,12},{1,17},{... | collective-permute-start | bytes 589832 | tf_op jit(solution)/shard_map/ppermute | solution.py:49
  123.3 11.4 %collective-permute-start.39 = (bf16[128,768]{1,0:T(8,128)(2,1)S(1)}, bf16[128,768]{1,0:T(8,128)(2,1)S(1)}, u32[]{:S(2)}, u32[]{:S(2)}) collective-permute-start(bf16[128,768]{1,0:T(8,128)(2,1)S(1)} %add_convert_fusion.3), channel_id=1, source_target_pairs={{0,24},{4,28},{8,16},{12,20},{16,8},{20,12},{24,0},{28,4},{1,25},{... | collective-permute-start | bytes 589832 | tf_op jit(solution)/shard_map/ppermute | solution.py:49
  125.5 7.8 %collective-permute-start.32 = (bf16[256,768]{1,0:T(8,128)(2,1)S(1)}, bf16[256,768]{1,0:T(8,128)(2,1)S(1)}, u32[]{:S(2)}, u32[]{:S(2)}) collective-permute-start(bf16[256,768]{1,0:T(8,128)(2,1)S(1)} %shard_map.250.refs_3_), channel_id=1, source_target_pairs={{0,4},{4,0},{8,12},{12,8},{16,20},{20,16},{24,28},{28,24},{1,5},{5... | collective-permute-start | bytes 1179656 | tf_op jit(solution)/shard_map/ppermute | solution.py:49
  127.1 8.7 %collective-permute-start.41 = (bf16[128,768]{1,0:T(8,128)(2,1)S(1)}, bf16[128,768]{1,0:T(8,128)(2,1)S(1)}, u32[]{:S(2)}, u32[]{:S(2)}) collective-permute-start(bf16[128,768]{1,0:T(8,128)(2,1)S(1)} %add_convert_fusion.2), channel_id=1, source_target_pairs={{0,8},{4,12},{8,0},{12,4},{16,24},{20,28},{24,16},{28,20},{1,9},{5... | collective-permute-start | bytes 589832 | tf_op jit(solution)/shard_map/ppermute | solution.py:49
  136.7 7.1 %collective-permute-start.42 = (bf16[128,768]{1,0:T(8,128)(2,1)S(1)}, bf16[128,768]{1,0:T(8,128)(2,1)S(1)}, u32[]{:S(2)}, u32[]{:S(2)}) collective-permute-start(bf16[128,768]{1,0:T(8,128)(2,1)S(1)} %get-tuple-element.151.refs_10_), channel_id=1, source_target_pairs={{0,1},{1,0},{2,3},{3,2},{4,5},{5,4},{6,7},{7,6},{8,9},{9,8},{10,11... | collective-permute-start | bytes 589832 | tf_op jit(solution)/shard_map/ppermute | solution.py:49
  136.8 7.8 %collective-permute-start.43 = (bf16[128,768]{1,0:T(8,128)(2,1)S(1)}, bf16[128,768]{1,0:T(8,128)(2,1)S(1)}, u32[]{:S(2)}, u32[]{:S(2)}) collective-permute-start(bf16[128,768]{1,0:T(8,128)(2,1)S(1)} %get-tuple-element.151.refs_10_), channel_id=1, source_target_pairs={{0,2},{1,3},{2,0},{3,1},{4,6},{5,7},{6,4},{7,5},{8,10},{9,11},{10,... | collective-permute-start | bytes 589832 | tf_op jit(solution)/shard_map/ppermute | solution.py:49
  137.8 10.0 %collective-permute-start.44 = (bf16[128,768]{1,0:T(8,128)(2,1)S(1)}, bf16[128,768]{1,0:T(8,128)(2,1)S(1)}, u32[]{:S(2)}, u32[]{:S(2)}) collective-permute-start(bf16[128,768]{1,0:T(8,128)(2,1)S(1)} %get-tuple-element.151.refs_10_), channel_id=1, source_target_pairs={{0,3},{1,2},{2,1},{3,0},{4,7},{5,6},{6,5},{7,4},{8,11},{9,10},{10,... | collective-permute-start | bytes 589832 | tf_op jit(solution)/shard_map/ppermute | solution.py:49
  138.6 18.0 %collective-permute-start.45 = (bf16[128,768]{1,0:T(8,128)(2,1)S(1)}, bf16[128,768]{1,0:T(8,128)(2,1)S(1)}, u32[]{:S(2)}, u32[]{:S(2)}) collective-permute-start(bf16[128,768]{1,0:T(8,128)(2,1)S(1)} %get-tuple-element.153), channel_id=1, source_target_pairs={{0,16},{4,20},{8,24},{12,28},{16,0},{20,4},{24,8},{28,12},{1,17},{... | collective-permute-start | bytes 589832 | tf_op jit(solution)/shard_map/ppermute | solution.py:49
  142.4 14.2 %collective-permute-start.46 = (bf16[128,768]{1,0:T(8,128)(2,1)S(1)}, bf16[128,768]{1,0:T(8,128)(2,1)S(1)}, u32[]{:S(2)}, u32[]{:S(2)}) collective-permute-start(bf16[128,768]{1,0:T(8,128)(2,1)S(1)} %get-tuple-element.154), channel_id=1, source_target_pairs={{0,24},{4,28},{8,16},{12,20},{16,8},{20,12},{24,0},{28,4},{1,25},{... | collective-permute-start | bytes 589832 | tf_op jit(solution)/shard_map/ppermute | solution.py:49
  143.8 13.8 %collective-permute-start.47 = (bf16[128,768]{1,0:T(8,128)(2,1)S(1)}, bf16[128,768]{1,0:T(8,128)(2,1)S(1)}, u32[]{:S(2)}, u32[]{:S(2)}) collective-permute-start(bf16[128,768]{1,0:T(8,128)(2,1)S(1)} %get-tuple-element.155), channel_id=1, source_target_pairs={{0,8},{4,12},{8,0},{12,4},{16,24},{20,28},{24,16},{28,20},{1,9},{5... | collective-permute-start | bytes 589832 | tf_op jit(solution)/shard_map/ppermute | solution.py:49
  157.6 6.2 %collective-permute-start.50 = (bf16[4,24,896]{2,1,0:T(8,128)(2,1)S(1)}, bf16[4,24,896]{2,1,0:T(8,128)(2,1)S(1)}, u32[]{:S(2)}, u32[]{:S(2)}) collective-permute-start(bf16[4,24,896]{2,1,0:T(8,128)(2,1)S(1)} %shard_map.258), channel_id=1, source_target_pairs={{0,4},{4,0},{8,12},{12,8},{16,20},{20,16},{24,28},{28,24},{1,5},{5... | collective-permute-start | bytes 516104 | tf_op jit(solution)/shard_map/ppermute | solution.py:49
  159.1 33.2 %collective-permute-start.48 = (bf16[2,128,768]{2,1,0:T(8,128)(2,1)S(1)}, bf16[2,128,768]{2,1,0:T(8,128)(2,1)S(1)}, u32[]{:S(2)}, u32[]{:S(2)}) collective-permute-start(bf16[2,128,768]{2,1,0:T(8,128)(2,1)S(1)} %get-tuple-element.158), channel_id=1, source_target_pairs={{0,1},{1,0},{2,3},{3,2},{4,5},{5,4},{6,7},{7,6},{8,9},{9,8},{10,11... | collective-permute-start | bytes 1179656 | tf_op jit(solution)/shard_map/ppermute | solution.py:49
  159.1 10.8 %collective-permute-start.53 = (bf16[4,24,896]{2,1,0:T(8,128)(2,1)S(1)}, bf16[4,24,896]{2,1,0:T(8,128)(2,1)S(1)}, u32[]{:S(2)}, u32[]{:S(2)}) collective-permute-start(bf16[4,24,896]{2,1,0:T(8,128)(2,1)S(1)} %get-tuple-element.152.refs_0_), channel_id=1, source_target_pairs={{0,4},{4,0},{8,12},{12,8},{16,20},{20,16},{24,28},{28,24},{1,5},{5... | collective-permute-start | bytes 516104 | tf_op jit(solution)/shard_map/ppermute | solution.py:49
  159.6 12.8 %collective-permute-start.55 = (bf16[4,24,896]{2,1,0:T(8,128)(2,1)S(1)}, bf16[4,24,896]{2,1,0:T(8,128)(2,1)S(1)}, u32[]{:S(2)}, u32[]{:S(2)}) collective-permute-start(bf16[4,24,896]{2,1,0:T(8,128)(2,1)S(1)} %get-tuple-element.166), channel_id=1, source_target_pairs={{0,4},{4,0},{8,12},{12,8},{16,20},{20,16},{24,28},{28,24},{1,5},{5... | collective-permute-start | bytes 516104 | tf_op jit(solution)/shard_map/ppermute | solution.py:49
  163.9 12.0 %collective-permute-start.51 = (bf16[4,24,896]{2,1,0:T(8,128)(2,1)S(1)}, bf16[4,24,896]{2,1,0:T(8,128)(2,1)S(1)}, u32[]{:S(2)}, u32[]{:S(2)}) collective-permute-start(bf16[4,24,896]{2,1,0:T(8,128)(2,1)S(1)} %shard_map.259), channel_id=1, source_target_pairs={{0,4},{4,0},{8,12},{12,8},{16,20},{20,16},{24,28},{28,24},{1,5},{5... | collective-permute-start | bytes 516104 | tf_op jit(solution)/shard_map/ppermute | solution.py:49
  166.4 14.9 %collective-permute-start.52 = (bf16[4,24,896]{2,1,0:T(8,128)(2,1)S(1)}, bf16[4,24,896]{2,1,0:T(8,128)(2,1)S(1)}, u32[]{:S(2)}, u32[]{:S(2)}) collective-permute-start(bf16[4,24,896]{2,1,0:T(8,128)(2,1)S(1)} %add_convert_fusion.7), channel_id=1, source_target_pairs={{0,16},{4,20},{8,24},{12,28},{16,0},{20,4},{24,8},{28,12},{1,17},{... | collective-permute-start | bytes 516104 | tf_op jit(solution)/shard_map/ppermute | solution.py:49
  169.9 11.4 %collective-permute-start.54 = (bf16[4,24,896]{2,1,0:T(8,128)(2,1)S(1)}, bf16[4,24,896]{2,1,0:T(8,128)(2,1)S(1)}, u32[]{:S(2)}, u32[]{:S(2)}) collective-permute-start(bf16[4,24,896]{2,1,0:T(8,128)(2,1)S(1)} %add_convert_fusion.6), channel_id=1, source_target_pairs={{0,24},{4,28},{8,16},{12,20},{16,8},{20,12},{24,0},{28,4},{1,25},{... | collective-permute-start | bytes 516104 | tf_op jit(solution)/shard_map/ppermute | solution.py:49
  172.5 9.3 %collective-permute-start.56 = (bf16[4,24,896]{2,1,0:T(8,128)(2,1)S(1)}, bf16[4,24,896]{2,1,0:T(8,128)(2,1)S(1)}, u32[]{:S(2)}, u32[]{:S(2)}) collective-permute-start(bf16[4,24,896]{2,1,0:T(8,128)(2,1)S(1)} %add_convert_fusion.5), channel_id=1, source_target_pairs={{0,8},{4,12},{8,0},{12,4},{16,24},{20,28},{24,16},{28,20},{1,9},{5... | collective-permute-start | bytes 516104 | tf_op jit(solution)/shard_map/ppermute | solution.py:49
  182.5 1.9 collective-permute-start.57
  182.6 4.0 %collective-permute-start.58 = (bf16[24,704]{1,0:T(8,128)(2,1)S(1)}, bf16[24,704]{1,0:T(8,128)(2,1)S(1)}, u32[]{:S(2)}, u32[]{:S(2)}) collective-permute-start(bf16[24,704]{1,0:T(8,128)(2,1)S(1)} %get-tuple-element.169), channel_id=1, source_target_pairs={{0,2},{1,3},{2,0},{3,1},{4,6},{5,7},{6,4},{7,5},{8,10},{9,11},{10,... | collective-permute-start | bytes 101384 | tf_op jit(solution)/shard_map/ppermute | solution.py:49
  183.7 3.4 %collective-permute-start.59 = (bf16[24,704]{1,0:T(8,128)(2,1)S(1)}, bf16[24,704]{1,0:T(8,128)(2,1)S(1)}, u32[]{:S(2)}, u32[]{:S(2)}) collective-permute-start(bf16[24,704]{1,0:T(8,128)(2,1)S(1)} %get-tuple-element.170), channel_id=1, source_target_pairs={{0,3},{1,2},{2,1},{3,0},{4,7},{5,6},{6,5},{7,4},{8,11},{9,10},{10,... | collective-permute-start | bytes 101384 | tf_op jit(solution)/shard_map/ppermute | solution.py:49
  187.9 8.8 %collective-permute-start.61 = (bf16[24,3200]{1,0:T(8,128)(2,1)S(1)}, bf16[24,3200]{1,0:T(8,128)(2,1)S(1)}, u32[]{:S(2)}, u32[]{:S(2)}) collective-permute-start(bf16[24,3200]{1,0:T(8,128)(2,1)S(1)} %shard_map.261.refs_1_), channel_id=1, source_target_pairs={{0,8},{4,12},{8,0},{12,4},{16,24},{20,28},{24,16},{28,20},{1,9},{5... | collective-permute-start | bytes 460808 | tf_op jit(solution)/shard_map/ppermute | solution.py:49
  189.9 14.3 %collective-permute-start.63 = (bf16[24,3200]{1,0:T(8,128)(2,1)S(1)}, bf16[24,3200]{1,0:T(8,128)(2,1)S(1)}, u32[]{:S(2)}, u32[]{:S(2)}) collective-permute-start(bf16[24,3200]{1,0:T(8,128)(2,1)S(1)} %shard_map.261.refs_1_), channel_id=1, source_target_pairs={{0,16},{4,20},{8,24},{12,28},{16,0},{20,4},{24,8},{28,12},{1,17},{... | collective-permute-start | bytes 460808 | tf_op jit(solution)/shard_map/ppermute | solution.py:49
  190.6 14.1 %collective-permute-start.65 = (bf16[24,3200]{1,0:T(8,128)(2,1)S(1)}, bf16[24,3200]{1,0:T(8,128)(2,1)S(1)}, u32[]{:S(2)}, u32[]{:S(2)}) collective-permute-start(bf16[24,3200]{1,0:T(8,128)(2,1)S(1)} %shard_map.261.refs_1_), channel_id=1, source_target_pairs={{0,24},{4,28},{8,16},{12,20},{16,8},{20,12},{24,0},{28,4},{1,25},{... | collective-permute-start | bytes 460808 | tf_op jit(solution)/shard_map/ppermute | solution.py:49
  192.4 20.1 %collective-permute-start.49 = (bf16[128,768]{1,0:T(8,128)(2,1)S(1)}, bf16[128,768]{1,0:T(8,128)(2,1)S(1)}, u32[]{:S(2)}, u32[]{:S(2)}) collective-permute-start(bf16[128,768]{1,0:T(8,128)(2,1)S(1)} %fusion), channel_id=1, source_target_pairs={{0,2},{1,3},{2,0},{3,1},{4,6},{5,7},{6,4},{7,5},{8,10},{9,11},{10,... | collective-permute-start | bytes 589832 | tf_op jit(solution)/shard_map/ppermute | solution.py:49
  193.4 20.6 %collective-permute-start.60 = (bf16[24,3200]{1,0:T(8,128)(2,1)S(1)}, bf16[24,3200]{1,0:T(8,128)(2,1)S(1)}, u32[]{:S(2)}, u32[]{:S(2)}) collective-permute-start(bf16[24,3200]{1,0:T(8,128)(2,1)S(1)} %shard_map.261.refs_1_), channel_id=1, source_target_pairs={{0,4},{4,0},{8,12},{12,8},{16,20},{20,16},{24,28},{28,24},{1,5},{5... | collective-permute-start | bytes 460808 | tf_op jit(solution)/shard_map/ppermute | solution.py:49
  196.6 17.4 %collective-permute-start.62 = (bf16[24,3200]{1,0:T(8,128)(2,1)S(1)}, bf16[24,3200]{1,0:T(8,128)(2,1)S(1)}, u32[]{:S(2)}, u32[]{:S(2)}) collective-permute-start(bf16[24,3200]{1,0:T(8,128)(2,1)S(1)} %collective-permute-done.61.refs_3_), channel_id=1, source_target_pairs={{0,4},{4,0},{8,12},{12,8},{16,20},{20,16},{24,28},{28,24},{1,5},{5... | collective-permute-start | bytes 460808 | tf_op jit(solution)/shard_map/ppermute | solution.py:49
  204.2 9.8 %collective-permute-start.64 = (bf16[24,3200]{1,0:T(8,128)(2,1)S(1)}, bf16[24,3200]{1,0:T(8,128)(2,1)S(1)}, u32[]{:S(2)}, u32[]{:S(2)}) collective-permute-start(bf16[24,3200]{1,0:T(8,128)(2,1)S(1)} %collective-permute-done.63.refs_5_), channel_id=1, source_target_pairs={{0,4},{4,0},{8,12},{12,8},{16,20},{20,16},{24,28},{28,24},{1,5},{5... | collective-permute-start | bytes 460808 | tf_op jit(solution)/shard_map/ppermute | solution.py:49
  204.7 9.3 %collective-permute-start.66 = (bf16[24,3200]{1,0:T(8,128)(2,1)S(1)}, bf16[24,3200]{1,0:T(8,128)(2,1)S(1)}, u32[]{:S(2)}, u32[]{:S(2)}) collective-permute-start(bf16[24,3200]{1,0:T(8,128)(2,1)S(1)} %collective-permute-done.65.refs_7_), channel_id=1, source_target_pairs={{0,4},{4,0},{8,12},{12,8},{16,20},{20,16},{24,28},{28,24},{1,5},{5... | collective-permute-start | bytes 460808 | tf_op jit(solution)/shard_map/ppermute | solution.py:49
  (14 other events, 79.3 us)

commit v3 on v2

--- a/solution.py
+++ b/solution.py
@@ -337,13 +337,14 @@
     out_ref[...] = total.astype(low)
 
 
-def expert_kernel(me_ref, back_a, back_b, choice_a, choice_b, weight_ref, router_ref, *refs):
-    rows, outs, (act_ref, back_pre_ref, logits_ref) = refs[:2], refs[2:4], refs[4:]
-    for k in range(2):
+def expert_kernel(count, me_ref, weight_ref, router_ref, *refs):
+    backs, choices, rows, outs = (refs[k * count : (k + 1) * count] for k in range(4))
+    act_ref, back_pre_ref, logits_ref = refs[4 * count :]
+    for k in range(count):
         here = slice(k * CAP, (k + 1) * CAP)
         block = rows[k][...]
-        choice = (choice_a, choice_b)[k][...]
-        back = (back_a, back_b)[k][...]
+        choice = choices[k][...]
+        back = backs[k][...]
         chosen = jnp.sum(along_last(block, router_ref[...]) * choice, axis=1, keepdims=True)
         gate = jax.nn.sigmoid(chosen)
         pre = along_last(block, weight_ref[...])
@@ -362,30 +363,29 @@
         outs[k][...] = (matmul(back_pre, weight_ref[...]) + matmul(logits, router_ref[...])).astype(low)
 
 
-def result_kernel(order, me_ref, weight_ref, act_a, act_b, logits_a, logits_b, *refs):
-    rows, outs, router_ref = refs[:SHARDS], refs[SHARDS:-1], refs[-1]
-    router = jnp.zeros(router_ref.shape, wide)
-    for k, s in enumerate(order):
-        here = slice((k % 2) * CAP, (k % 2 + 1) * CAP)
-        outs[s][...] = matmul((act_a, act_b)[k // 2][here, :], weight_ref[...]).astype(low)
-        router = router + along_first(rows[s][...], (logits_a, logits_b)[k // 2][here, :])
-    router_ref[...] = router
+def result_kernel(me_ref, weight_ref, *refs):
+    acts, logits, rows, outs = refs[:3], refs[3:6], refs[6 : 6 + SHARDS], refs[6 + SHARDS : -1]
+    router = jnp.zeros(refs[-1].shape, wide)
+    for s in range(SHARDS):
+        k, here = (0, slice(s * CAP, (s + 1) * CAP)) if s < 2 else (s - 1, slice(0, CAP))
+        outs[s][...] = matmul(acts[k][here, :], weight_ref[...]).astype(low)
+        router = router + along_first(rows[s][...], logits[k][here, :])
+    refs[-1][...] = router
 
 
 def layer_kernel(me_ref, resid_ref, *refs):
     refs[-1][...] = (resid_ref[...] + total_of(refs[:-1])).astype(low)
 
 
-def grads_kernel(order, me_ref, *refs):
-    acts, pres = refs[0:2], refs[2:4]
-    rows, ups = refs[4 : 4 + SHARDS], refs[4 + SHARDS : 4 + 3 * SHARDS]
-    first_ref, second_ref = refs[4 + 3 * SHARDS :]
+def grads_kernel(me_ref, *refs):
+    acts, pres, rows, ups = refs[:3], refs[3:6], refs[6 : 6 + SHARDS], refs[6 + SHARDS : 6 + 3 * SHARDS]
+    first_ref, second_ref, flag_ref = refs[6 + 3 * SHARDS :]
+    flag_ref[...] = jnp.zeros_like(flag_ref)
     acts = jnp.concatenate([ref[...] for ref in acts], axis=0)
     pres = jnp.concatenate([ref[...] for ref in pres], axis=0)
-    block = jnp.concatenate([rows[s][...] for s in order], axis=0)
-    first_ref[0] = along_first(pres, block)
+    first_ref[0] = along_first(pres, jnp.concatenate([ref[...] for ref in rows], axis=0))
     half = CAP - ups[0].shape[0]
-    ups = jnp.concatenate([ref[...] for s in order for ref in (ups[2 * s], ups[2 * s + 1].at[:half])], axis=0)
+    ups = jnp.concatenate([ref[...] for s in range(SHARDS) for ref in (ups[2 * s], ups[2 * s + 1].at[:half])], axis=0)
     second_ref[0] = along_first(acts, ups)
 
 
@@ -551,7 +551,7 @@
     held = refs[-1]
     piece = parts[0].shape[0]
     width = outs[0].shape[1]
-    experts = outs[6].shape[1]
+    experts = outs[6].shape[0]
     for s, ref in enumerate(parts):
         here = pl.ds(pl.multiple_of((me_ref[1] ^ s) * piece, 8), piece)
         block = ref[...].astype(wide)
@@ -563,9 +563,9 @@
     i = lax.broadcasted_iota(jnp.int32, (shard, shard), 0)
     j = lax.broadcasted_iota(jnp.int32, (shard, shard), 1)
     turned = along_first(extra.astype(low), (i == j).astype(low))
-    outs[4][...] = turned[0:1]
-    outs[5][...] = turned[1:2]
-    outs[6][...] = extra[:, 2 : 2 + experts]
+    outs[4][...] = turned[0]
+    outs[5][...] = turned[1]
+    outs[6][...] = turned[2 : 2 + experts]
     outs[7][...] = extra[: outs[7].shape[0], 2 + experts : 2 + experts + HEADS]
 
 
@@ -720,45 +720,54 @@
         *second_rel,
         after=upstream_rel[2],
     )
-    half = (2 * CAP, width)
-
-    def expert_half(k, after):
-        return call(
-            expert_kernel,
-            [(packed_row, low)] * 2 + [(half, low), (half, low), ((2 * CAP, LANES), low)],
+
+    def expert_rows(parts, after=()):
+        tall = len(parts) * CAP
+        *outs, act, pre, logits = call(
+            lambda *refs: expert_kernel(len(parts), *refs),
+            [(packed_row, low)] * len(parts) + [((tall, width), low), ((tall, width), low), ((tall, LANES), low)],
             [],
             me,
-            back_act[2 * k],
-            back_act[2 * k + 1],
-            choice[2 * k],
-            choice[2 * k + 1],
             first_local,
             router,
-            rows_rel[order[2 * k]],
-            rows_rel[order[2 * k + 1]],
+            *[back_act[s] for s in parts],
+            *[choice[s] for s in parts],
+            *[rows_rel[s] for s in parts],
             after=after,
         )
+        return outs, act, pre, logits
 
     far = swap(packed, W, 2)
     rows_rel = [packed, swap(packed, W, 1)]
-    halves = [expert_half(0, ())]
-    far = tie(far, halves[0][0])
+    (own_rows, near_rows), *kept_a = expert_rows((0, 1))
+    far = tie(far, own_rows)
     rows_rel = rows_rel + [far, swap(far, W, 1)]
-    halves.append(expert_half(1, ()))
-    near = swap(halves[1][1], W, 1)
-    across = (halves[1][0].astype(wide) + near.astype(wide)).astype(low)
+    (across_rows,), *kept_b = expert_rows((2,))
+    (last_rows,), *kept_c = expert_rows((3,), after=(kept_b[2],))
+    acts, pres, logits = zip(kept_a, kept_b, kept_c)
+    near = swap(last_rows, W, 1)
+    across = (across_rows.astype(wide) + near.astype(wide)).astype(low)
     *results, router_grad = call(
-        lambda *refs: result_kernel(order, *refs),
+        result_kernel,
         [(packed_row, low)] * SHARDS + [((width, LANES), wide)],
         [],
         me,
         second_local,
-        halves[0][2],
-        halves[1][2],
-        halves[0][4],
-        halves[1][4],
+        *acts,
+        *logits,
         *rows_rel,
         after=(across,),
+    )
+    first_grad, second_grad, flag = call(
+        grads_kernel,
+        [((1,) + first_local.shape, wide), ((1,) + second_local.shape, wide), ((8, LANES), wide)],
+        [],
+        me,
+        *acts,
+        *pres,
+        *rows_rel,
+        *[piece for pieces in upstream_rel for piece in pieces],
+        after=(results[0],),
     )
     back_parts = call(
         unpack_kernel,
@@ -766,10 +775,10 @@
         [],
         me,
         dispatch,
-        halves[0][0],
-        swap(halves[0][1], W, 1),
+        own_rows,
+        swap(near_rows, W, 1),
         swap(across, W, 2),
-        after=(results[0],),
+        after=(results[0], flag),
     )
     back_terms = sum_e(back_parts)
 
@@ -833,20 +842,6 @@
         small,
         back_resid,
         *back_terms,
-    )
-
-    first_grad, second_grad = call(
-        lambda *refs: grads_kernel(order, *refs),
-        [((1,) + first_local.shape, wide), ((1,) + second_local.shape, wide)],
-        [],
-        me,
-        halves[0][2],
-        halves[1][2],
-        halves[0][3],
-        halves[1][3],
-        *rows_rel,
-        *[piece for pieces in upstream_rel for piece in pieces],
-        after=(grads[-1],),
     )
 
     if quick:
@@ -870,15 +865,15 @@
         outs = call(
             final_kernel,
             [(shape, wide)] * 4
-            + [((1, shard), wide)] * 2
-            + [((shard, experts), wide), ((table_rows, HEADS), wide)],
+            + [((shard,), wide)] * 2
+            + [((experts, shard), wide), ((table_rows, HEADS), wide)],
             [((shard, LANES), wide)],
             me,
             *gather_e(grads),
         )
         query_grad, key_grad, value_grad, output_grad = outs[:4]
-        gain_one_grad, gain_two_grad = outs[4].reshape(shard), outs[5].reshape(shard)
-        router_grad, table_grad = outs[6], outs[7]
+        gain_one_grad, gain_two_grad = outs[4], outs[5]
+        router_grad, table_grad = outs[6].T, outs[7]
     else:
         grads = lax.psum(grads[0], E).astype(wide).reshape(SHARDS, shard, columns + shard)
         output_grad = grads[:, :, columns:].transpose(1, 0, 2).reshape(shard, width)

time: 217 us -> 213 us (0.982)
  waiting for transfers between devices: 75.9 us -> 71.9 us
    ppermute x67, waiting for transfers between devices: 75.9 us -> 71.9 us  [swap(): return lax.ppermute(value, axis, [(i, i ^ step) for i in range(count)])]
    pallas_call x22 -> x23, Pallas kernels: 50.6 us -> 51.1 us  [call(): pl.pallas_call(lambda *refs: kernel(*refs[skip:]), out_shape=tuple((jax.S...]
  transfers between devices with their start and end apart: 67 -> 67, of which waited for: 31 -> 32; matrix products, arithmetic and copies ran while one was open for 1% -> 1% of each run, Pallas kernels for 20% -> 21%
where the time goes in v3:
time: 213 us
  starting transfers between devices  83.6 us (39%)
  waiting for transfers between devices  71.9 us (34%)
  Pallas kernels  51.1 us (24%)
  local copies, waits for them, and re-layouts  3.26 us (2%)
    ppermute x67, starting transfers between devices, swap(): return lax.ppermute(value, axis, [(i, i ^ step) for i in range(count)])  83.6 us
    ppermute x67, waiting for transfers between devices, swap(): return lax.ppermute(value, axis, [(i, i ^ step) for i in range(count)])  71.9 us
    pallas_call x23, Pallas kernels, call(): pl.pallas_call(lambda *refs: kernel(*refs[skip:]), out_shape=tuple((jax.S...  51.1 us
  transfers between devices with their start and end apart: 67, of which 32 were waited for; matrix products, arithmetic and copies ran while one was open for 1% of the time, Pallas kernels for 21%

profile of v3, /device:TPU:0, one launch (start us, length us, event | category | flops | bytes accessed | tf_op | source)
XLA Modules:
  0.0 212.8 jit_solution(3053951497888825302)
XLA Ops:
  0.6 3.0 %collective-permute-start.1 = (bf16[128,768]{1,0:T(8,128)(2,1)}, bf16[128,768]{1,0:T(8,128)(2,1)S(1)}, u32[]{:S(2)}, u32[]{:S(2)}) collective-permute-start(bf16[128,768]{1,0:T(8,128)(2,1)} %refs_1_.11), channel_id=1, source_target_pairs={{0,2},{1,3},{2,0},{3,1},{4,6},{5,7},{6,4},{7,5},{8,10},{9,11},{10,... | collective-permute-start | bytes 589832 | tf_op jit(solution)/shard_map/ppermute | solution.py:49
  4.9 2.4 %shard_map.238 = (bf16[224,576]{1,0:T(8,128)(2,1)}, bf16[224,576]{1,0:T(8,128)(2,1)}, bf16[224,576]{1,0:T(8,128)(2,1)}, bf16[224,576]{1,0:T(8,128)(2,1)}) custom-call(s32[3]{0:T(128)} %pad_add_fusion.refs_0_.refs_1_.refs_2_, bf16[192,768]{1,0:T(8,128)(2,1)} %refs_1_.6, bf16[192,768]{1,0:T(8,128)(2,1)} %refs_2_.2, bf16[192,768]{1,0:T(8,128)(2,1)} %refs_3_.1, ...), custom_call_target="tpu_custom_call" | custom-call | flops 1 | bytes 1 | tf_op jit(solution)/shard_map/pallas_call | solution.py:132
  7.3 1.8 collective-permute-start.5
  9.7 1.6 shard_map.240.refs_3_.refs_2_
  11.4 1.6 collective-permute-start.6
  12.9 2.6 %collective-permute-start.7 = (bf16[144,768]{1,0:T(8,128)(2,1)}, bf16[144,768]{1,0:T(8,128)(2,1)S(1)}, u32[]{:S(2)}, u32[]{:S(2)}) collective-permute-start(bf16[144,768]{1,0:T(8,128)(2,1)} %shard_map.240.refs_3_.refs_2_), channel_id=1, source_target_pairs={{0,16},{4,20},{8,24},{12,28},{16,0},{20,4},{24,8},{28,12},{1,17},{... | collective-permute-start | bytes 663560 | tf_op jit(solution)/shard_map/ppermute | solution.py:49
  15.5 1.7 collective-permute-done.4.refs_7_
  17.2 3.6 %collective-permute-start.8 = (bf16[144,768]{1,0:T(8,128)(2,1)}, bf16[144,768]{1,0:T(8,128)(2,1)S(1)}, u32[]{:S(2)}, u32[]{:S(2)}) collective-permute-start(bf16[144,768]{1,0:T(8,128)(2,1)} %shard_map.240.refs_3_.refs_2_), channel_id=1, source_target_pairs={{0,24},{4,28},{8,16},{12,20},{16,8},{20,12},{24,0},{28,4},{1,25},{... | collective-permute-start | bytes 663560 | tf_op jit(solution)/shard_map/ppermute | solution.py:49
  20.8 1.8 collective-permute-done.5.refs_8_
  25.8 5.3 %shard_map.239 = (bf16[4,128,768]{2,1,0:T(8,128)(2,1)S(1)}, bf16[512,768]{1,0:T(8,128)(2,1)S(1)}, bf16[512,576]{1,0:T(8,128)(2,1)S(1)}, bf16[3,512,512]{2,1,0:T(...) custom-call(s32[3]{0:T(128)S(1)} %copy-done.7, ...), custom_call_target="tpu_custom_call" | custom-call | flops 20000000000 | bytes 1 | tf_op jit(solution)/shard_map/pallas_call | solution.py:132
  32.9 1.6 collective-permute-start.11
  35.6 6.2 %collective-permute-done.10.refs_5_ = bf16[128,768]{1,0:T(8,128)(2,1)S(1)} collective-permute-done((bf16[128,768]{1,0:T(8,128)(2,1)S(1)}, bf16[128,768]{1,0:T(8,128)(2,1)S(1)}, u32[]{:S(2)}, u32[]{:S(2)}) %collective-permute-start.10) | collective-permute-done | bytes 196640 | tf_op jit(solution)/shard_map/ppermute | solution.py:49
  42.5 4.4 %collective-permute-start.19 = (bf16[128,768]{1,0:T(8,128)(2,1)S(1)}, bf16[128,768]{1,0:T(8,128)(2,1)S(1)}, u32[]{:S(2)}, u32[]{:S(2)}) collective-permute-start(bf16[128,768]{1,0:T(8,128)(2,1)S(1)} %get-tuple-element.116.refs_0_.refs_4_), channel_id=1, source_target_pairs={{0,8},{4,12},{8,0},{12,4},{16,24},{20,28},{24,16},{28,20},{1,9},{5... | collective-permute-start | bytes 589832 | tf_op jit(solution)/shard_map/ppermute | solution.py:49
  48.0 1.4 collective-permute-start.23
  49.4 1.5 collective-permute-start.18
  50.9 4.6 %collective-permute-done.11.refs_6_ = bf16[4,144,768]{2,1,0:T(8,128)(2,1)S(1)} collective-permute-done((bf16[4,144,768]{2,1,0:T(8,128)(2,1)S(1)}, bf16[4,144,768]{2,1,0:T(8,128)(2,1)S(1)}, u32[]{:S(2)}, u32[]{:S(2)}) %collective-permute-start.11) | collective-permute-done | bytes 884768 | tf_op jit(solution)/shard_map/ppermute | solution.py:49
  55.5 1.8 shard_map.243
  58.2 1.5 collective-permute-start.20
  59.7 4.4 %collective-permute-done.21.refs_8_ = bf16[128,768]{1,0:T(8,128)(2,1)S(1)} collective-permute-done((bf16[128,768]{1,0:T(8,128)(2,1)S(1)}, bf16[128,768]{1,0:T(8,128)(2,1)S(1)}, u32[]{:S(2)}, u32[]{:S(2)}) %collective-permute-start.21) | collective-permute-done | bytes 196640 | tf_op jit(solution)/shard_map/ppermute | solution.py:49
  64.1 1.5 collective-permute-start.22
  67.1 3.1 %collective-permute-done.22.refs_9_ = bf16[128,768]{1,0:T(8,128)(2,1)S(1)} collective-permute-done((bf16[128,768]{1,0:T(8,128)(2,1)S(1)}, bf16[128,768]{1,0:T(8,128)(2,1)S(1)}, u32[]{:S(2)}, u32[]{:S(2)}) %collective-permute-start.22) | collective-permute-done | bytes 196640 | tf_op jit(solution)/shard_map/ppermute | solution.py:49
  70.2 2.1 collective-permute-done.24.refs_11_
  72.3 1.5 shard_map.245.refs_7_.refs_9_.refs_8_
  77.3 3.7 %shard_map.244 = (f32[256,768]{1,0:T(8,128)S(1)}, f32[256,768]{1,0:T(8,128)S(1)}, f32[256,768]{1,0:T(8,128)S(1)}, f32[256,768]{1,0:T(8,128)S(1)}, f32[256,128]{1...) custom-call(s32[3]{0:T(128)S(1)} %copy-done.7, ...), custom_call_target="tpu_custom_call" | custom-call | flops 1 | bytes 1 | tf_op jit(solution)/shard_map/pallas_call | solution.py:132
  81.0 4.1 %shard_map.246 = (bf16[256,768]{1,0:T(8,128)(2,1)S(1)}, bf16[256,768]{1,0:T(8,128)(2,1)S(1)}, bf16[512,768]{1,0:T(8,128)(2,1)S(1)}, bf16[512,768]{1,0:T(8,128)(2,1)S(1)}, bf16[512,128]{1,0:T(8,128)(2,1)S(1)}) custom-call(s32[3]{0:T(128)S(1)} %copy-done.7, bf16[768,768]{1,0:T(8,128)(2,1)S(1)} %bitcast.17, ...), custom_call_target="tpu_custom_call" | custom-call | flops 1 | bytes 1 | tf_op jit(solution)/shard_map/pallas_call | solution.py:132
  85.5 2.3 %shard_map.248 = (bf16[256,768]{1,0:T(8,128)(2,1)S(1)}, bf16[256,768]{1,0:T(8,128)(2,1)S(1)}, bf16[256,768]{1,0:T(8,128)(2,1)S(1)}, bf16[256,128]{1,0:T(8,128)(2,1)S(1)}) custom-call(s32[3]{0:T(128)S(1)} %copy-done.7, bf16[768,768]{1,0:T(8,128)(2,1)S(1)} %bitcast.18, bf16[128,768]{1,0:T(8,128)(2,1)S(1)} %get-tuple-element.120.refs_2_.refs_3_, ...), custom_call_target="tpu_custom_call" | custom-call | flops 1 | bytes 1 | tf_op jit(solution)/shard_map/pallas_call | solution.py:132
  87.8 2.3 %shard_map.249 = (bf16[256,768]{1,0:T(8,128)(2,1)S(1)}, bf16[256,768]{1,0:T(8,128)(2,1)S(1)}, bf16[256,768]{1,0:T(8,128)(2,1)S(1)}, bf16[256,128]{1,0:T(8,128)(2,1)S(1)}) custom-call(bf16[256,128]{1,0:T(8,128)(2,1)S(1)} %get-tuple-element.131.refs_0_.refs_7_, s32[3]{0:T(128)S(1)} %copy-done.8, bf16[768,768]{1,0:T(8,128)(2,1)S(1)} %bitcast.19, ...), custom_call_target="tpu_custom_call" | custom-call | flops 1 | bytes 1 | tf_op jit(solution)/shard_map/pallas_call | solution.py:132
  92.2 1.3 collective-permute-start.34
  93.5 2.4 %shard_map.250 = (bf16[256,768]{1,0:T(8,128)(2,1)S(1)}, bf16[256,768]{1,0:T(8,128)(2,1)S(1)}, bf16[256,768]{1,0:T(8,128)(2,1)S(1)}, bf16[256,768]{1,0:T(8,128)(2,1)S(1)}, f32[768,128]{1,0:T(8,128)S(1)}) custom-call(bf16[256,768]{1,0:T(8,128)(2,1)S(1)} %add_convert_fusion.1.refs_0_, s32[3]{0:T(128)S(1)} %copy-done.8, bf16[768,768]{1,0:T(8,128)(2,1)S(1)} %bitcast.21, ...), custom_call_target="tpu_custom_call" | custom-call | flops 1 | bytes 1 | tf_op jit(solution)/shard_map/pallas_call | solution.py:132
  96.4 4.9 %shard_map.253 = (f32[1,768,768]{2,1,0:T(8,128)}, f32[1,768,768]{2,1,0:T(8,128)}, f32[8,128]{1,0:T(8,128)S(1)}) custom-call(bf16[256,768]{1,0:T(8,128)(2,1)S(1)} %get-tuple-element.140.refs_1_.refs_0_, s32[3]{0:T(128)S(1)} %copy-done.8, bf16[512,768]{1,0:T(8,128)(2,1)S(1)} %get-tuple-element.135.refs_3_.refs_2_, ...), custom_call_target="tpu_custom_call" | custom-call | flops 1 | bytes 1 | tf_op jit(solution)/shard_map/pallas_call | solution.py:132
  101.3 2.3 %collective-permute-done.34.refs_6_ = bf16[256,768]{1,0:T(8,128)(2,1)S(1)} collective-permute-done((bf16[256,768]{1,0:T(8,128)(2,1)S(1)}, bf16[256,768]{1,0:T(8,128)(2,1)S(1)}, u32[]{:S(2)}, u32[]{:S(2)}) %collective-permute-start.34) | collective-permute-done | bytes 393248 | tf_op jit(solution)/shard_map/ppermute | solution.py:49
  104.9 1.6 collective-permute-start.35
  106.6 1.3 collective-permute-start.31
  108.4 1.5 collective-permute-start.40
  109.9 2.9 %collective-permute-done.35.refs_1_ = bf16[128,768]{1,0:T(8,128)(2,1)S(1)} collective-permute-done((bf16[128,768]{1,0:T(8,128)(2,1)S(1)}, bf16[128,768]{1,0:T(8,128)(2,1)S(1)}, u32[]{:S(2)}, u32[]{:S(2)}) %collective-permute-start.35) | collective-permute-done | bytes 196640 | tf_op jit(solution)/shard_map/ppermute | solution.py:49
  112.8 1.5 collective-permute-start.36
  114.3 2.6 %collective-permute-done.38 = bf16[128,768]{1,0:T(8,128)(2,1)S(1)} collective-permute-done((bf16[128,768]{1,0:T(8,128)(2,1)S(1)}, bf16[128,768]{1,0:T(8,128)(2,1)S(1)}, u32[]{:S(2)}, u32[]{:S(2)}) %collective-permute-start.38) | collective-permute-done | bytes 196640 | tf_op jit(solution)/shard_map/ppermute | solution.py:49
  117.0 5.6 %collective-permute-start.37 = (bf16[128,768]{1,0:T(8,128)(2,1)S(1)}, bf16[128,768]{1,0:T(8,128)(2,1)S(1)}, u32[]{:S(2)}, u32[]{:S(2)}) collective-permute-start(bf16[128,768]{1,0:T(8,128)(2,1)S(1)} %add_convert_fusion.4), channel_id=1, source_target_pairs={{0,16},{4,20},{8,24},{12,28},{16,0},{20,4},{24,8},{28,12},{1,17},{... | collective-permute-start | bytes 589832 | tf_op jit(solution)/shard_map/ppermute | solution.py:49
  122.7 1.4 collective-permute-start.39
  124.8 1.6 collective-permute-start.32
  126.5 6.1 %collective-permute-done.32.refs_4_ = bf16[256,768]{1,0:T(8,128)(2,1)S(1)} collective-permute-done((bf16[256,768]{1,0:T(8,128)(2,1)S(1)}, bf16[256,768]{1,0:T(8,128)(2,1)S(1)}, u32[]{:S(2)}, u32[]{:S(2)}) %collective-permute-start.32) | collective-permute-done | bytes 393248 | tf_op jit(solution)/shard_map/ppermute | solution.py:49
  138.3 3.8 %collective-permute-start.45 = (bf16[128,768]{1,0:T(8,128)(2,1)S(1)}, bf16[128,768]{1,0:T(8,128)(2,1)S(1)}, u32[]{:S(2)}, u32[]{:S(2)}) collective-permute-start(bf16[128,768]{1,0:T(8,128)(2,1)S(1)} %get-tuple-element.163), channel_id=1, source_target_pairs={{0,16},{4,20},{8,24},{12,28},{16,0},{20,4},{24,8},{28,12},{1,17},{... | collective-permute-start | bytes 589832 | tf_op jit(solution)/shard_map/ppermute | solution.py:49
  142.0 1.4 collective-permute-start.46
  144.2 3.3 %collective-permute-done.44.refs_13_ = bf16[128,768]{1,0:T(8,128)(2,1)S(1)} collective-permute-done((bf16[128,768]{1,0:T(8,128)(2,1)S(1)}, bf16[128,768]{1,0:T(8,128)(2,1)S(1)}, u32[]{:S(2)}, u32[]{:S(2)}) %collective-permute-start.44) | collective-permute-done | bytes 196640 | tf_op jit(solution)/shard_map/ppermute | solution.py:49
  147.5 6.6 %shard_map.257 = (bf16[128,768]{1,0:T(8,128)(2,1)S(1)}, bf16[128,768]{1,0:T(8,128)(2,1)S(1)}, bf16[2,128,768]{2,1,0:T(8,128)(2,1)S(1)}, bf16[4,24,896]{2,1,0:T(8...) custom-call(s32[3]{0:T(128)S(1)} %copy-done.8, ...), custom_call_target="tpu_custom_call" | custom-call | flops 20000000000 | bytes 1 | tf_op jit(solution)/shard_map/pallas_call | solution.py:132
  154.0 2.2 %collective-permute-done.45.refs_4_.refs_1_ = bf16[128,768]{1,0:T(8,128)(2,1)S(1)} collective-permute-done((bf16[128,768]{1,0:T(8,128)(2,1)S(1)}, bf16[128,768]{1,0:T(8,128)(2,1)S(1)}, u32[]{:S(2)}, u32[]{:S(2)}) %collective-permute-start.45) | collective-permute-done | bytes 196640 | tf_op jit(solution)/shard_map/ppermute | solution.py:49
  157.2 1.5 collective-permute-start.50
  159.3 1.5 collective-permute-start.55
  160.8 2.7 %collective-permute-done.50.refs_1_ = bf16[4,24,896]{2,1,0:T(8,128)(2,1)S(1)} collective-permute-done((bf16[4,24,896]{2,1,0:T(8,128)(2,1)S(1)}, bf16[4,24,896]{2,1,0:T(8,128)(2,1)S(1)}, u32[]{:S(2)}, u32[]{:S(2)}) %collective-permute-start.50) | collective-permute-done | bytes 172064 | tf_op jit(solution)/shard_map/ppermute | solution.py:49
  163.5 2.5 %collective-permute-start.51 = (bf16[4,24,896]{2,1,0:T(8,128)(2,1)S(1)}, bf16[4,24,896]{2,1,0:T(8,128)(2,1)S(1)}, u32[]{:S(2)}, u32[]{:S(2)}) collective-permute-start(bf16[4,24,896]{2,1,0:T(8,128)(2,1)S(1)} %shard_map.261), channel_id=1, source_target_pairs={{0,4},{4,0},{8,12},{12,8},{16,20},{20,16},{24,28},{28,24},{1,5},{5... | collective-permute-start | bytes 516104 | tf_op jit(solution)/shard_map/ppermute | solution.py:49
  166.0 3.5 %collective-permute-start.52 = (bf16[4,24,896]{2,1,0:T(8,128)(2,1)S(1)}, bf16[4,24,896]{2,1,0:T(8,128)(2,1)S(1)}, u32[]{:S(2)}, u32[]{:S(2)}) collective-permute-start(bf16[4,24,896]{2,1,0:T(8,128)(2,1)S(1)} %add_convert_fusion.7), channel_id=1, source_target_pairs={{0,16},{4,20},{8,24},{12,28},{16,0},{20,4},{24,8},{28,12},{1,17},{... | collective-permute-start | bytes 516104 | tf_op jit(solution)/shard_map/ppermute | solution.py:49
  169.6 2.5 %collective-permute-start.54 = (bf16[4,24,896]{2,1,0:T(8,128)(2,1)S(1)}, bf16[4,24,896]{2,1,0:T(8,128)(2,1)S(1)}, u32[]{:S(2)}, u32[]{:S(2)}) collective-permute-start(bf16[4,24,896]{2,1,0:T(8,128)(2,1)S(1)} %add_convert_fusion.6), channel_id=1, source_target_pairs={{0,24},{4,28},{8,16},{12,20},{16,8},{20,12},{24,0},{28,4},{1,25},{... | collective-permute-start | bytes 516104 | tf_op jit(solution)/shard_map/ppermute | solution.py:49
  172.1 3.3 %collective-permute-start.56 = (bf16[4,24,896]{2,1,0:T(8,128)(2,1)S(1)}, bf16[4,24,896]{2,1,0:T(8,128)(2,1)S(1)}, u32[]{:S(2)}, u32[]{:S(2)}) collective-permute-start(bf16[4,24,896]{2,1,0:T(8,128)(2,1)S(1)} %add_convert_fusion.5), channel_id=1, source_target_pairs={{0,8},{4,12},{8,0},{12,4},{16,24},{20,28},{24,16},{28,20},{1,9},{5... | collective-permute-start | bytes 516104 | tf_op jit(solution)/shard_map/ppermute | solution.py:49
  175.5 5.5 %collective-permute-done.52.refs_3_ = bf16[4,24,896]{2,1,0:T(8,128)(2,1)S(1)} collective-permute-done((bf16[4,24,896]{2,1,0:T(8,128)(2,1)S(1)}, bf16[4,24,896]{2,1,0:T(8,128)(2,1)S(1)}, u32[]{:S(2)}, u32[]{:S(2)}) %collective-permute-start.52) | collective-permute-done | bytes 172064 | tf_op jit(solution)/shard_map/ppermute | solution.py:49
  184.2 2.2 %collective-permute-done.58.refs_3_ = bf16[24,704]{1,0:T(8,128)(2,1)S(1)} collective-permute-done((bf16[24,704]{1,0:T(8,128)(2,1)S(1)}, bf16[24,704]{1,0:T(8,128)(2,1)S(1)}, u32[]{:S(2)}, u32[]{:S(2)}) %collective-permute-start.58) | collective-permute-done | bytes 33824 | tf_op jit(solution)/shard_map/ppermute | solution.py:49
  187.5 1.9 collective-permute-start.61
  190.3 1.7 collective-permute-start.65
  194.4 1.9 collective-permute-done.61.refs_3_
  197.5 6.4 %collective-permute-done.63.refs_5_ = bf16[24,3200]{1,0:T(8,128)(2,1)S(1)} collective-permute-done((bf16[24,3200]{1,0:T(8,128)(2,1)S(1)}, bf16[24,3200]{1,0:T(8,128)(2,1)S(1)}, u32[]{:S(2)}, u32[]{:S(2)}) %collective-permute-start.63) | collective-permute-done | bytes 153632 | tf_op jit(solution)/shard_map/ppermute | solution.py:49
  204.3 1.5 collective-permute-start.66
  205.8 1.3 shard_map.258
  207.2 1.5 shard_map.259
  209.0 1.6 collective-permute-done.66.refs_8_
  210.7 2.1 shard_map.264
  (130 shorter events, 38.1 us)
Async XLA Ops:
  0.6 8.8 %collective-permute-start.1 = (bf16[128,768]{1,0:T(8,128)(2,1)}, bf16[128,768]{1,0:T(8,128)(2,1)S(1)}, u32[]{:S(2)}, u32[]{:S(2)}) collective-permute-start(bf16[128,768]{1,0:T(8,128)(2,1)} %refs_1_.11), channel_id=1, source_target_pairs={{0,2},{1,3},{2,0},{3,1},{4,6},{5,7},{6,4},{7,5},{8,10},{9,11},{10,... | collective-permute-start | bytes 589832 | tf_op jit(solution)/shard_map/ppermute | solution.py:49
  7.3 5.6 %collective-permute-start.3 = (bf16[224,576]{1,0:T(8,128)(2,1)}, bf16[224,576]{1,0:T(8,128)(2,1)S(1)}, u32[]{:S(2)}, u32[]{:S(2)}) collective-permute-start(bf16[224,576]{1,0:T(8,128)(2,1)} %get-tuple-element.103), channel_id=1, source_target_pairs={{0,1},{1,0},{2,3},{3,2},{4,5},{5,4},{6,7},{7,6},{8,9},{9,8},{10,11... | collective-permute-start | bytes 774152 | tf_op jit(solution)/shard_map/ppermute | solution.py:49
  7.3 9.9 %collective-permute-start.4 = (bf16[224,576]{1,0:T(8,128)(2,1)}, bf16[224,576]{1,0:T(8,128)(2,1)S(1)}, u32[]{:S(2)}, u32[]{:S(2)}) collective-permute-start(bf16[224,576]{1,0:T(8,128)(2,1)} %get-tuple-element.104), channel_id=1, source_target_pairs={{0,2},{1,3},{2,0},{3,1},{4,6},{5,7},{6,4},{7,5},{8,10},{9,11},{10,... | collective-permute-start | bytes 774152 | tf_op jit(solution)/shard_map/ppermute | solution.py:49
  7.3 15.2 %collective-permute-start.5 = (bf16[224,576]{1,0:T(8,128)(2,1)}, bf16[224,576]{1,0:T(8,128)(2,1)S(1)}, u32[]{:S(2)}, u32[]{:S(2)}) collective-permute-start(bf16[224,576]{1,0:T(8,128)(2,1)} %get-tuple-element.105), channel_id=1, source_target_pairs={{0,3},{1,2},{2,1},{3,0},{4,7},{5,6},{6,5},{7,4},{8,11},{9,10},{10,... | collective-permute-start | bytes 774152 | tf_op jit(solution)/shard_map/ppermute | solution.py:49
  9.2 2.2 %collective-permute-start = (bf16[128,768]{1,0:T(8,128)(2,1)}, bf16[128,768]{1,0:T(8,128)(2,1)S(1)}, u32[]{:S(2)}, u32[]{:S(2)}) collective-permute-start(bf16[128,768]{1,0:T(8,128)(2,1)} %refs_1_.11), channel_id=1, source_target_pairs={{0,1},{1,0},{2,3},{3,2},{4,5},{5,4},{6,7},{7,6},{8,9},{9,8},{10,11... | collective-permute-start | bytes 589832 | tf_op jit(solution)/shard_map/ppermute | solution.py:49
  9.5 13.1 %collective-permute-start.2 = (bf16[128,768]{1,0:T(8,128)(2,1)S(1)}, bf16[128,768]{1,0:T(8,128)(2,1)S(1)}, u32[]{:S(2)}, u32[]{:S(2)}) collective-permute-start(bf16[128,768]{1,0:T(8,128)(2,1)S(1)} %collective-permute-done.1.refs_3_), channel_id=1, source_target_pairs={{0,1},{1,0},{2,3},{3,2},{4,5},{5,4},{6,7},{7,6},{8,9},{9,8},{10,11... | collective-permute-start | bytes 589832 | tf_op jit(solution)/shard_map/ppermute | solution.py:49
  11.4 19.8 %collective-permute-start.6 = (bf16[144,768]{1,0:T(8,128)(2,1)}, bf16[144,768]{1,0:T(8,128)(2,1)S(1)}, u32[]{:S(2)}, u32[]{:S(2)}) collective-permute-start(bf16[144,768]{1,0:T(8,128)(2,1)} %shard_map.240.refs_3_.refs_2_), channel_id=1, source_target_pairs={{0,8},{4,12},{8,0},{12,4},{16,24},{20,28},{24,16},{28,20},{1,9},{5... | collective-permute-start | bytes 663560 | tf_op jit(solution)/shard_map/ppermute | solution.py:49
  12.9 18.9 %collective-permute-start.7 = (bf16[144,768]{1,0:T(8,128)(2,1)}, bf16[144,768]{1,0:T(8,128)(2,1)S(1)}, u32[]{:S(2)}, u32[]{:S(2)}) collective-permute-start(bf16[144,768]{1,0:T(8,128)(2,1)} %shard_map.240.refs_3_.refs_2_), channel_id=1, source_target_pairs={{0,16},{4,20},{8,24},{12,28},{16,0},{20,4},{24,8},{28,12},{1,17},{... | collective-permute-start | bytes 663560 | tf_op jit(solution)/shard_map/ppermute | solution.py:49
  17.2 14.7 %collective-permute-start.8 = (bf16[144,768]{1,0:T(8,128)(2,1)}, bf16[144,768]{1,0:T(8,128)(2,1)S(1)}, u32[]{:S(2)}, u32[]{:S(2)}) collective-permute-start(bf16[144,768]{1,0:T(8,128)(2,1)} %shard_map.240.refs_3_.refs_2_), channel_id=1, source_target_pairs={{0,24},{4,28},{8,16},{12,20},{16,8},{20,12},{24,0},{28,4},{1,25},{... | collective-permute-start | bytes 663560 | tf_op jit(solution)/shard_map/ppermute | solution.py:49
  32.9 22.5 %collective-permute-start.11 = (bf16[4,144,768]{2,1,0:T(8,128)(2,1)S(1)}, bf16[4,144,768]{2,1,0:T(8,128)(2,1)S(1)}, u32[]{:S(2)}, u32[]{:S(2)}) collective-permute-start(bf16[4,144,768]{2,1,0:T(8,128)(2,1)S(1)} %get-tuple-element.117), channel_id=1, source_target_pairs={{0,4},{4,0},{8,12},{12,8},{16,20},{20,16},{24,28},{28,24},{1,5},{5... | collective-permute-start | bytes 2654216 | tf_op jit(solution)/shard_map/ppermute | solution.py:49
  34.7 7.0 %collective-permute-start.10 = (bf16[128,768]{1,0:T(8,128)(2,1)S(1)}, bf16[128,768]{1,0:T(8,128)(2,1)S(1)}, u32[]{:S(2)}, u32[]{:S(2)}) collective-permute-start(bf16[128,768]{1,0:T(8,128)(2,1)S(1)} %fusion.1), channel_id=1, source_target_pairs={{0,2},{1,3},{2,0},{3,1},{4,6},{5,7},{6,4},{7,5},{8,10},{9,11},{10,... | collective-permute-start | bytes 589832 | tf_op jit(solution)/shard_map/ppermute | solution.py:49
  42.5 15.7 %collective-permute-start.19 = (bf16[128,768]{1,0:T(8,128)(2,1)S(1)}, bf16[128,768]{1,0:T(8,128)(2,1)S(1)}, u32[]{:S(2)}, u32[]{:S(2)}) collective-permute-start(bf16[128,768]{1,0:T(8,128)(2,1)S(1)} %get-tuple-element.116.refs_0_.refs_4_), channel_id=1, source_target_pairs={{0,8},{4,12},{8,0},{12,4},{16,24},{20,28},{24,16},{28,20},{1,9},{5... | collective-permute-start | bytes 589832 | tf_op jit(solution)/shard_map/ppermute | solution.py:49
  46.9 17.2 %collective-permute-start.21 = (bf16[128,768]{1,0:T(8,128)(2,1)S(1)}, bf16[128,768]{1,0:T(8,128)(2,1)S(1)}, u32[]{:S(2)}, u32[]{:S(2)}) collective-permute-start(bf16[128,768]{1,0:T(8,128)(2,1)S(1)} %get-tuple-element.116.refs_0_.refs_4_), channel_id=1, source_target_pairs={{0,16},{4,20},{8,24},{12,28},{16,0},{20,4},{24,8},{28,12},{1,17},{... | collective-permute-start | bytes 589832 | tf_op jit(solution)/shard_map/ppermute | solution.py:49
  48.0 17.6 %collective-permute-start.23 = (bf16[128,768]{1,0:T(8,128)(2,1)S(1)}, bf16[128,768]{1,0:T(8,128)(2,1)S(1)}, u32[]{:S(2)}, u32[]{:S(2)}) collective-permute-start(bf16[128,768]{1,0:T(8,128)(2,1)S(1)} %get-tuple-element.116.refs_0_.refs_4_), channel_id=1, source_target_pairs={{0,24},{4,28},{8,16},{12,20},{16,8},{20,12},{24,0},{28,4},{1,25},{... | collective-permute-start | bytes 589832 | tf_op jit(solution)/shard_map/ppermute | solution.py:49
  49.4 16.7 %collective-permute-start.18 = (bf16[128,768]{1,0:T(8,128)(2,1)S(1)}, bf16[128,768]{1,0:T(8,128)(2,1)S(1)}, u32[]{:S(2)}, u32[]{:S(2)}) collective-permute-start(bf16[128,768]{1,0:T(8,128)(2,1)S(1)} %get-tuple-element.116.refs_0_.refs_4_), channel_id=1, source_target_pairs={{0,4},{4,0},{8,12},{12,8},{16,20},{20,16},{24,28},{28,24},{1,5},{5... | collective-permute-start | bytes 589832 | tf_op jit(solution)/shard_map/ppermute | solution.py:49
  57.3 15.0 %collective-permute-start.15 = (bf16[144,768]{1,0:T(8,128)(2,1)S(1)}, bf16[144,768]{1,0:T(8,128)(2,1)S(1)}, u32[]{:S(2)}, u32[]{:S(2)}) collective-permute-start(bf16[144,768]{1,0:T(8,128)(2,1)S(1)} %get-tuple-element.122.refs_3_.refs_13_), channel_id=1, source_target_pairs={{0,2},{1,3},{2,0},{3,1},{4,6},{5,7},{6,4},{7,5},{8,10},{9,11},{10,... | collective-permute-start | bytes 663560 | tf_op jit(solution)/shard_map/ppermute | solution.py:49
  58.2 9.0 %collective-permute-start.20 = (bf16[128,768]{1,0:T(8,128)(2,1)S(1)}, bf16[128,768]{1,0:T(8,128)(2,1)S(1)}, u32[]{:S(2)}, u32[]{:S(2)}) collective-permute-start(bf16[128,768]{1,0:T(8,128)(2,1)S(1)} %collective-permute-done.19.refs_6_), channel_id=1, source_target_pairs={{0,4},{4,0},{8,12},{12,8},{16,20},{20,16},{24,28},{28,24},{1,5},{5... | collective-permute-start | bytes 589832 | tf_op jit(solution)/shard_map/ppermute | solution.py:49
  64.1 6.1 %collective-permute-start.22 = (bf16[128,768]{1,0:T(8,128)(2,1)S(1)}, bf16[128,768]{1,0:T(8,128)(2,1)S(1)}, u32[]{:S(2)}, u32[]{:S(2)}) collective-permute-start(bf16[128,768]{1,0:T(8,128)(2,1)S(1)} %collective-permute-done.21.refs_8_), channel_id=1, source_target_pairs={{0,4},{4,0},{8,12},{12,8},{16,20},{20,16},{24,28},{28,24},{1,5},{5... | collective-permute-start | bytes 589832 | tf_op jit(solution)/shard_map/ppermute | solution.py:49
  65.6 6.7 %collective-permute-start.24 = (bf16[128,768]{1,0:T(8,128)(2,1)S(1)}, bf16[128,768]{1,0:T(8,128)(2,1)S(1)}, u32[]{:S(2)}, u32[]{:S(2)}) collective-permute-start(bf16[128,768]{1,0:T(8,128)(2,1)S(1)} %collective-permute-done.23.refs_10_), channel_id=1, source_target_pairs={{0,4},{4,0},{8,12},{12,8},{16,20},{20,16},{24,28},{28,24},{1,5},{5... | collective-permute-start | bytes 589832 | tf_op jit(solution)/shard_map/ppermute | solution.py:49
  66.1 6.2 %collective-permute-start.14 = (bf16[128,768]{1,0:T(8,128)(2,1)S(1)}, bf16[128,768]{1,0:T(8,128)(2,1)S(1)}, u32[]{:S(2)}, u32[]{:S(2)}) collective-permute-start(bf16[128,768]{1,0:T(8,128)(2,1)S(1)} %get-tuple-element.121.refs_2_.refs_12_), channel_id=1, source_target_pairs={{0,2},{1,3},{2,0},{3,1},{4,6},{5,7},{6,4},{7,5},{8,10},{9,11},{10,... | collective-permute-start | bytes 589832 | tf_op jit(solution)/shard_map/ppermute | solution.py:49
  67.1 8.6 %collective-permute-start.12 = (bf16[128,768]{1,0:T(8,128)(2,1)S(1)}, bf16[128,768]{1,0:T(8,128)(2,1)S(1)}, u32[]{:S(2)}, u32[]{:S(2)}) collective-permute-start(bf16[128,768]{1,0:T(8,128)(2,1)S(1)} %get-tuple-element.121.refs_2_.refs_12_), channel_id=1, source_target_pairs={{0,1},{1,0},{2,3},{3,2},{4,5},{5,4},{6,7},{7,6},{8,9},{9,8},{10,11... | collective-permute-start | bytes 589832 | tf_op jit(solution)/shard_map/ppermute | solution.py:49
  73.8 7.2 %collective-permute-start.26 = (bf16[256,768]{1,0:T(8,128)(2,1)S(1)}, bf16[256,768]{1,0:T(8,128)(2,1)S(1)}, u32[]{:S(2)}, u32[]{:S(2)}) collective-permute-start(bf16[256,768]{1,0:T(8,128)(2,1)S(1)} %shard_map.245.refs_7_.refs_9_.refs_8_), channel_id=1, source_target_pairs={{0,1},{1,0},{2,3},{3,2},{4,5},{5,4},{6,7},{7,6},{8,9},{9,8},{10,11... | collective-permute-start | bytes 1179656 | tf_op jit(solution)/shard_map/ppermute | solution.py:49
  73.9 11.5 %collective-permute-start.25 = (bf16[256,768]{1,0:T(8,128)(2,1)S(1)}, bf16[256,768]{1,0:T(8,128)(2,1)S(1)}, u32[]{:S(2)}, u32[]{:S(2)}) collective-permute-start(bf16[256,768]{1,0:T(8,128)(2,1)S(1)} %shard_map.245.refs_7_.refs_9_.refs_8_), channel_id=1, source_target_pairs={{0,2},{1,3},{2,0},{3,1},{4,6},{5,7},{6,4},{7,5},{8,10},{9,11},{10,... | collective-permute-start | bytes 1179656 | tf_op jit(solution)/shard_map/ppermute | solution.py:49
  75.4 1.9 collective-permute-start.17
  85.5 2.4 %collective-permute-start.27 = (bf16[256,768]{1,0:T(8,128)(2,1)S(1)}, bf16[256,768]{1,0:T(8,128)(2,1)S(1)}, u32[]{:S(2)}, u32[]{:S(2)}) collective-permute-start(bf16[256,768]{1,0:T(8,128)(2,1)S(1)} %shard_map.247.refs_5_.refs_11_.refs_10_), channel_id=1, source_target_pairs={{0,1},{1,0},{2,3},{3,2},{4,5},{5,4},{6,7},{7,6},{8,9},{9,8},{10,11... | collective-permute-start | bytes 1179656 | tf_op jit(solution)/shard_map/ppermute | solution.py:49
  90.2 1.9 collective-permute-start.28
  90.7 10.6 %collective-permute-start.33 = (bf16[256,768]{1,0:T(8,128)(2,1)S(1)}, bf16[256,768]{1,0:T(8,128)(2,1)S(1)}, u32[]{:S(2)}, u32[]{:S(2)}) collective-permute-start(bf16[256,768]{1,0:T(8,128)(2,1)S(1)} %get-tuple-element.150), channel_id=1, source_target_pairs={{0,1},{1,0},{2,3},{3,2},{4,5},{5,4},{6,7},{7,6},{8,9},{9,8},{10,11... | collective-permute-start | bytes 1179656 | tf_op jit(solution)/shard_map/ppermute | solution.py:49
  92.2 11.5 %collective-permute-start.34 = (bf16[256,768]{1,0:T(8,128)(2,1)S(1)}, bf16[256,768]{1,0:T(8,128)(2,1)S(1)}, u32[]{:S(2)}, u32[]{:S(2)}) collective-permute-start(bf16[256,768]{1,0:T(8,128)(2,1)S(1)} %add_convert_fusion.1.refs_0_), channel_id=1, source_target_pairs={{0,2},{1,3},{2,0},{3,1},{4,6},{5,7},{6,4},{7,5},{8,10},{9,11},{10,... | collective-permute-start | bytes 1179656 | tf_op jit(solution)/shard_map/ppermute | solution.py:49
  95.9 10.6 %collective-permute-start.30 = (bf16[256,768]{1,0:T(8,128)(2,1)S(1)}, bf16[256,768]{1,0:T(8,128)(2,1)S(1)}, u32[]{:S(2)}, u32[]{:S(2)}) collective-permute-start(bf16[256,768]{1,0:T(8,128)(2,1)S(1)} %get-tuple-element.143), channel_id=1, source_target_pairs={{0,1},{1,0},{2,3},{3,2},{4,5},{5,4},{6,7},{7,6},{8,9},{9,8},{10,11... | collective-permute-start | bytes 1179656 | tf_op jit(solution)/shard_map/ppermute | solution.py:49
  96.0 26.6 %collective-permute-start.29 = (bf16[256,768]{1,0:T(8,128)(2,1)S(1)}, bf16[256,768]{1,0:T(8,128)(2,1)S(1)}, u32[]{:S(2)}, u32[]{:S(2)}) collective-permute-start(bf16[256,768]{1,0:T(8,128)(2,1)S(1)} %get-tuple-element.141), channel_id=1, source_target_pairs={{0,1},{1,0},{2,3},{3,2},{4,5},{5,4},{6,7},{7,6},{8,9},{9,8},{10,11... | collective-permute-start | bytes 1179656 | tf_op jit(solution)/shard_map/ppermute | solution.py:49
  104.9 7.9 %collective-permute-start.35 = (bf16[128,768]{1,0:T(8,128)(2,1)S(1)}, bf16[128,768]{1,0:T(8,128)(2,1)S(1)}, u32[]{:S(2)}, u32[]{:S(2)}) collective-permute-start(bf16[128,768]{1,0:T(8,128)(2,1)S(1)} %get-tuple-element.153), channel_id=1, source_target_pairs={{0,4},{4,0},{8,12},{12,8},{16,20},{20,16},{24,28},{28,24},{1,5},{5... | collective-permute-start | bytes 589832 | tf_op jit(solution)/shard_map/ppermute | solution.py:49
  106.6 17.5 %collective-permute-start.31 = (bf16[256,768]{1,0:T(8,128)(2,1)S(1)}, bf16[256,768]{1,0:T(8,128)(2,1)S(1)}, u32[]{:S(2)}, u32[]{:S(2)}) collective-permute-start(bf16[256,768]{1,0:T(8,128)(2,1)S(1)} %add_convert_fusion), channel_id=1, source_target_pairs={{0,2},{1,3},{2,0},{3,1},{4,6},{5,7},{6,4},{7,5},{8,10},{9,11},{10,... | collective-permute-start | bytes 1179656 | tf_op jit(solution)/shard_map/ppermute | solution.py:49
  107.9 9.1 %collective-permute-start.38 = (bf16[128,768]{1,0:T(8,128)(2,1)S(1)}, bf16[128,768]{1,0:T(8,128)(2,1)S(1)}, u32[]{:S(2)}, u32[]{:S(2)}) collective-permute-start(bf16[128,768]{1,0:T(8,128)(2,1)S(1)} %get-tuple-element.156), channel_id=1, source_target_pairs={{0,4},{4,0},{8,12},{12,8},{16,20},{20,16},{24,28},{28,24},{1,5},{5... | collective-permute-start | bytes 589832 | tf_op jit(solution)/shard_map/ppermute | solution.py:49
  108.4 18.0 %collective-permute-start.40 = (bf16[128,768]{1,0:T(8,128)(2,1)S(1)}, bf16[128,768]{1,0:T(8,128)(2,1)S(1)}, u32[]{:S(2)}, u32[]{:S(2)}) collective-permute-start(bf16[128,768]{1,0:T(8,128)(2,1)S(1)} %get-tuple-element.158), channel_id=1, source_target_pairs={{0,4},{4,0},{8,12},{12,8},{16,20},{20,16},{24,28},{28,24},{1,5},{5... | collective-permute-start | bytes 589832 | tf_op jit(solution)/shard_map/ppermute | solution.py:49
  112.8 21.0 %collective-permute-start.36 = (bf16[128,768]{1,0:T(8,128)(2,1)S(1)}, bf16[128,768]{1,0:T(8,128)(2,1)S(1)}, u32[]{:S(2)}, u32[]{:S(2)}) collective-permute-start(bf16[128,768]{1,0:T(8,128)(2,1)S(1)} %shard_map.255), channel_id=1, source_target_pairs={{0,4},{4,0},{8,12},{12,8},{16,20},{20,16},{24,28},{28,24},{1,5},{5... | collective-permute-start | bytes 589832 | tf_op jit(solution)/shard_map/ppermute | solution.py:49
  117.0 17.6 %collective-permute-start.37 = (bf16[128,768]{1,0:T(8,128)(2,1)S(1)}, bf16[128,768]{1,0:T(8,128)(2,1)S(1)}, u32[]{:S(2)}, u32[]{:S(2)}) collective-permute-start(bf16[128,768]{1,0:T(8,128)(2,1)S(1)} %add_convert_fusion.4), channel_id=1, source_target_pairs={{0,16},{4,20},{8,24},{12,28},{16,0},{20,4},{24,8},{28,12},{1,17},{... | collective-permute-start | bytes 589832 | tf_op jit(solution)/shard_map/ppermute | solution.py:49
  122.7 12.0 %collective-permute-start.39 = (bf16[128,768]{1,0:T(8,128)(2,1)S(1)}, bf16[128,768]{1,0:T(8,128)(2,1)S(1)}, u32[]{:S(2)}, u32[]{:S(2)}) collective-permute-start(bf16[128,768]{1,0:T(8,128)(2,1)S(1)} %add_convert_fusion.3), channel_id=1, source_target_pairs={{0,24},{4,28},{8,16},{12,20},{16,8},{20,12},{24,0},{28,4},{1,25},{... | collective-permute-start | bytes 589832 | tf_op jit(solution)/shard_map/ppermute | solution.py:49
  124.8 7.8 %collective-permute-start.32 = (bf16[256,768]{1,0:T(8,128)(2,1)S(1)}, bf16[256,768]{1,0:T(8,128)(2,1)S(1)}, u32[]{:S(2)}, u32[]{:S(2)}) collective-permute-start(bf16[256,768]{1,0:T(8,128)(2,1)S(1)} %shard_map.251.refs_3_), channel_id=1, source_target_pairs={{0,4},{4,0},{8,12},{12,8},{16,20},{20,16},{24,28},{28,24},{1,5},{5... | collective-permute-start | bytes 1179656 | tf_op jit(solution)/shard_map/ppermute | solution.py:49
  126.4 9.0 %collective-permute-start.41 = (bf16[128,768]{1,0:T(8,128)(2,1)S(1)}, bf16[128,768]{1,0:T(8,128)(2,1)S(1)}, u32[]{:S(2)}, u32[]{:S(2)}) collective-permute-start(bf16[128,768]{1,0:T(8,128)(2,1)S(1)} %add_convert_fusion.2), channel_id=1, source_target_pairs={{0,8},{4,12},{8,0},{12,4},{16,24},{20,28},{24,16},{28,20},{1,9},{5... | collective-permute-start | bytes 589832 | tf_op jit(solution)/shard_map/ppermute | solution.py:49
  136.3 7.1 %collective-permute-start.42 = (bf16[128,768]{1,0:T(8,128)(2,1)S(1)}, bf16[128,768]{1,0:T(8,128)(2,1)S(1)}, u32[]{:S(2)}, u32[]{:S(2)}) collective-permute-start(bf16[128,768]{1,0:T(8,128)(2,1)S(1)} %get-tuple-element.161.refs_10_), channel_id=1, source_target_pairs={{0,1},{1,0},{2,3},{3,2},{4,5},{5,4},{6,7},{7,6},{8,9},{9,8},{10,11... | collective-permute-start | bytes 589832 | tf_op jit(solution)/shard_map/ppermute | solution.py:49
  136.4 7.8 %collective-permute-start.43 = (bf16[128,768]{1,0:T(8,128)(2,1)S(1)}, bf16[128,768]{1,0:T(8,128)(2,1)S(1)}, u32[]{:S(2)}, u32[]{:S(2)}) collective-permute-start(bf16[128,768]{1,0:T(8,128)(2,1)S(1)} %get-tuple-element.161.refs_10_), channel_id=1, source_target_pairs={{0,2},{1,3},{2,0},{3,1},{4,6},{5,7},{6,4},{7,5},{8,10},{9,11},{10,... | collective-permute-start | bytes 589832 | tf_op jit(solution)/shard_map/ppermute | solution.py:49
  137.5 10.0 %collective-permute-start.44 = (bf16[128,768]{1,0:T(8,128)(2,1)S(1)}, bf16[128,768]{1,0:T(8,128)(2,1)S(1)}, u32[]{:S(2)}, u32[]{:S(2)}) collective-permute-start(bf16[128,768]{1,0:T(8,128)(2,1)S(1)} %get-tuple-element.161.refs_10_), channel_id=1, source_target_pairs={{0,3},{1,2},{2,1},{3,0},{4,7},{5,6},{6,5},{7,4},{8,11},{9,10},{10,... | collective-permute-start | bytes 589832 | tf_op jit(solution)/shard_map/ppermute | solution.py:49
  138.3 18.0 %collective-permute-start.45 = (bf16[128,768]{1,0:T(8,128)(2,1)S(1)}, bf16[128,768]{1,0:T(8,128)(2,1)S(1)}, u32[]{:S(2)}, u32[]{:S(2)}) collective-permute-start(bf16[128,768]{1,0:T(8,128)(2,1)S(1)} %get-tuple-element.163), channel_id=1, source_target_pairs={{0,16},{4,20},{8,24},{12,28},{16,0},{20,4},{24,8},{28,12},{1,17},{... | collective-permute-start | bytes 589832 | tf_op jit(solution)/shard_map/ppermute | solution.py:49
  142.0 14.2 %collective-permute-start.46 = (bf16[128,768]{1,0:T(8,128)(2,1)S(1)}, bf16[128,768]{1,0:T(8,128)(2,1)S(1)}, u32[]{:S(2)}, u32[]{:S(2)}) collective-permute-start(bf16[128,768]{1,0:T(8,128)(2,1)S(1)} %get-tuple-element.164), channel_id=1, source_target_pairs={{0,24},{4,28},{8,16},{12,20},{16,8},{20,12},{24,0},{28,4},{1,25},{... | collective-permute-start | bytes 589832 | tf_op jit(solution)/shard_map/ppermute | solution.py:49
  143.4 13.8 %collective-permute-start.47 = (bf16[128,768]{1,0:T(8,128)(2,1)S(1)}, bf16[128,768]{1,0:T(8,128)(2,1)S(1)}, u32[]{:S(2)}, u32[]{:S(2)}) collective-permute-start(bf16[128,768]{1,0:T(8,128)(2,1)S(1)} %get-tuple-element.165), channel_id=1, source_target_pairs={{0,8},{4,12},{8,0},{12,4},{16,24},{20,28},{24,16},{28,20},{1,9},{5... | collective-permute-start | bytes 589832 | tf_op jit(solution)/shard_map/ppermute | solution.py:49
  157.2 6.2 %collective-permute-start.50 = (bf16[4,24,896]{2,1,0:T(8,128)(2,1)S(1)}, bf16[4,24,896]{2,1,0:T(8,128)(2,1)S(1)}, u32[]{:S(2)}, u32[]{:S(2)}) collective-permute-start(bf16[4,24,896]{2,1,0:T(8,128)(2,1)S(1)} %shard_map.260), channel_id=1, source_target_pairs={{0,4},{4,0},{8,12},{12,8},{16,20},{20,16},{24,28},{28,24},{1,5},{5... | collective-permute-start | bytes 516104 | tf_op jit(solution)/shard_map/ppermute | solution.py:49
  158.8 33.2 %collective-permute-start.48 = (bf16[2,128,768]{2,1,0:T(8,128)(2,1)S(1)}, bf16[2,128,768]{2,1,0:T(8,128)(2,1)S(1)}, u32[]{:S(2)}, u32[]{:S(2)}) collective-permute-start(bf16[2,128,768]{2,1,0:T(8,128)(2,1)S(1)} %get-tuple-element.168), channel_id=1, source_target_pairs={{0,1},{1,0},{2,3},{3,2},{4,5},{5,4},{6,7},{7,6},{8,9},{9,8},{10,11... | collective-permute-start | bytes 1179656 | tf_op jit(solution)/shard_map/ppermute | solution.py:49
  158.8 10.8 %collective-permute-start.53 = (bf16[4,24,896]{2,1,0:T(8,128)(2,1)S(1)}, bf16[4,24,896]{2,1,0:T(8,128)(2,1)S(1)}, u32[]{:S(2)}, u32[]{:S(2)}) collective-permute-start(bf16[4,24,896]{2,1,0:T(8,128)(2,1)S(1)} %get-tuple-element.162.refs_0_), channel_id=1, source_target_pairs={{0,4},{4,0},{8,12},{12,8},{16,20},{20,16},{24,28},{28,24},{1,5},{5... | collective-permute-start | bytes 516104 | tf_op jit(solution)/shard_map/ppermute | solution.py:49
  159.3 12.8 %collective-permute-start.55 = (bf16[4,24,896]{2,1,0:T(8,128)(2,1)S(1)}, bf16[4,24,896]{2,1,0:T(8,128)(2,1)S(1)}, u32[]{:S(2)}, u32[]{:S(2)}) collective-permute-start(bf16[4,24,896]{2,1,0:T(8,128)(2,1)S(1)} %get-tuple-element.176), channel_id=1, source_target_pairs={{0,4},{4,0},{8,12},{12,8},{16,20},{20,16},{24,28},{28,24},{1,5},{5... | collective-permute-start | bytes 516104 | tf_op jit(solution)/shard_map/ppermute | solution.py:49
  163.5 12.0 %collective-permute-start.51 = (bf16[4,24,896]{2,1,0:T(8,128)(2,1)S(1)}, bf16[4,24,896]{2,1,0:T(8,128)(2,1)S(1)}, u32[]{:S(2)}, u32[]{:S(2)}) collective-permute-start(bf16[4,24,896]{2,1,0:T(8,128)(2,1)S(1)} %shard_map.261), channel_id=1, source_target_pairs={{0,4},{4,0},{8,12},{12,8},{16,20},{20,16},{24,28},{28,24},{1,5},{5... | collective-permute-start | bytes 516104 | tf_op jit(solution)/shard_map/ppermute | solution.py:49
  166.0 14.9 %collective-permute-start.52 = (bf16[4,24,896]{2,1,0:T(8,128)(2,1)S(1)}, bf16[4,24,896]{2,1,0:T(8,128)(2,1)S(1)}, u32[]{:S(2)}, u32[]{:S(2)}) collective-permute-start(bf16[4,24,896]{2,1,0:T(8,128)(2,1)S(1)} %add_convert_fusion.7), channel_id=1, source_target_pairs={{0,16},{4,20},{8,24},{12,28},{16,0},{20,4},{24,8},{28,12},{1,17},{... | collective-permute-start | bytes 516104 | tf_op jit(solution)/shard_map/ppermute | solution.py:49
  169.6 11.4 %collective-permute-start.54 = (bf16[4,24,896]{2,1,0:T(8,128)(2,1)S(1)}, bf16[4,24,896]{2,1,0:T(8,128)(2,1)S(1)}, u32[]{:S(2)}, u32[]{:S(2)}) collective-permute-start(bf16[4,24,896]{2,1,0:T(8,128)(2,1)S(1)} %add_convert_fusion.6), channel_id=1, source_target_pairs={{0,24},{4,28},{8,16},{12,20},{16,8},{20,12},{24,0},{28,4},{1,25},{... | collective-permute-start | bytes 516104 | tf_op jit(solution)/shard_map/ppermute | solution.py:49
  172.1 9.4 %collective-permute-start.56 = (bf16[4,24,896]{2,1,0:T(8,128)(2,1)S(1)}, bf16[4,24,896]{2,1,0:T(8,128)(2,1)S(1)}, u32[]{:S(2)}, u32[]{:S(2)}) collective-permute-start(bf16[4,24,896]{2,1,0:T(8,128)(2,1)S(1)} %add_convert_fusion.5), channel_id=1, source_target_pairs={{0,8},{4,12},{8,0},{12,4},{16,24},{20,28},{24,16},{28,20},{1,9},{5... | collective-permute-start | bytes 516104 | tf_op jit(solution)/shard_map/ppermute | solution.py:49
  182.2 1.9 collective-permute-start.57
  182.3 4.0 %collective-permute-start.58 = (bf16[24,704]{1,0:T(8,128)(2,1)S(1)}, bf16[24,704]{1,0:T(8,128)(2,1)S(1)}, u32[]{:S(2)}, u32[]{:S(2)}) collective-permute-start(bf16[24,704]{1,0:T(8,128)(2,1)S(1)} %get-tuple-element.179), channel_id=1, source_target_pairs={{0,2},{1,3},{2,0},{3,1},{4,6},{5,7},{6,4},{7,5},{8,10},{9,11},{10,... | collective-permute-start | bytes 101384 | tf_op jit(solution)/shard_map/ppermute | solution.py:49
  183.4 3.4 %collective-permute-start.59 = (bf16[24,704]{1,0:T(8,128)(2,1)S(1)}, bf16[24,704]{1,0:T(8,128)(2,1)S(1)}, u32[]{:S(2)}, u32[]{:S(2)}) collective-permute-start(bf16[24,704]{1,0:T(8,128)(2,1)S(1)} %get-tuple-element.180), channel_id=1, source_target_pairs={{0,3},{1,2},{2,1},{3,0},{4,7},{5,6},{6,5},{7,4},{8,11},{9,10},{10,... | collective-permute-start | bytes 101384 | tf_op jit(solution)/shard_map/ppermute | solution.py:49
  187.5 8.7 %collective-permute-start.61 = (bf16[24,3200]{1,0:T(8,128)(2,1)S(1)}, bf16[24,3200]{1,0:T(8,128)(2,1)S(1)}, u32[]{:S(2)}, u32[]{:S(2)}) collective-permute-start(bf16[24,3200]{1,0:T(8,128)(2,1)S(1)} %shard_map.263.refs_1_), channel_id=1, source_target_pairs={{0,8},{4,12},{8,0},{12,4},{16,24},{20,28},{24,16},{28,20},{1,9},{5... | collective-permute-start | bytes 460808 | tf_op jit(solution)/shard_map/ppermute | solution.py:49
  189.5 14.3 %collective-permute-start.63 = (bf16[24,3200]{1,0:T(8,128)(2,1)S(1)}, bf16[24,3200]{1,0:T(8,128)(2,1)S(1)}, u32[]{:S(2)}, u32[]{:S(2)}) collective-permute-start(bf16[24,3200]{1,0:T(8,128)(2,1)S(1)} %shard_map.263.refs_1_), channel_id=1, source_target_pairs={{0,16},{4,20},{8,24},{12,28},{16,0},{20,4},{24,8},{28,12},{1,17},{... | collective-permute-start | bytes 460808 | tf_op jit(solution)/shard_map/ppermute | solution.py:49
  190.3 14.1 %collective-permute-start.65 = (bf16[24,3200]{1,0:T(8,128)(2,1)S(1)}, bf16[24,3200]{1,0:T(8,128)(2,1)S(1)}, u32[]{:S(2)}, u32[]{:S(2)}) collective-permute-start(bf16[24,3200]{1,0:T(8,128)(2,1)S(1)} %shard_map.263.refs_1_), channel_id=1, source_target_pairs={{0,24},{4,28},{8,16},{12,20},{16,8},{20,12},{24,0},{28,4},{1,25},{... | collective-permute-start | bytes 460808 | tf_op jit(solution)/shard_map/ppermute | solution.py:49
  192.0 15.1 %collective-permute-start.49 = (bf16[128,768]{1,0:T(8,128)(2,1)S(1)}, bf16[128,768]{1,0:T(8,128)(2,1)S(1)}, u32[]{:S(2)}, u32[]{:S(2)}) collective-permute-start(bf16[128,768]{1,0:T(8,128)(2,1)S(1)} %fusion), channel_id=1, source_target_pairs={{0,2},{1,3},{2,0},{3,1},{4,6},{5,7},{6,4},{7,5},{8,10},{9,11},{10,... | collective-permute-start | bytes 589832 | tf_op jit(solution)/shard_map/ppermute | solution.py:49
  193.1 15.6 %collective-permute-start.60 = (bf16[24,3200]{1,0:T(8,128)(2,1)S(1)}, bf16[24,3200]{1,0:T(8,128)(2,1)S(1)}, u32[]{:S(2)}, u32[]{:S(2)}) collective-permute-start(bf16[24,3200]{1,0:T(8,128)(2,1)S(1)} %shard_map.263.refs_1_), channel_id=1, source_target_pairs={{0,4},{4,0},{8,12},{12,8},{16,20},{20,16},{24,28},{28,24},{1,5},{5... | collective-permute-start | bytes 460808 | tf_op jit(solution)/shard_map/ppermute | solution.py:49
  196.2 12.5 %collective-permute-start.62 = (bf16[24,3200]{1,0:T(8,128)(2,1)S(1)}, bf16[24,3200]{1,0:T(8,128)(2,1)S(1)}, u32[]{:S(2)}, u32[]{:S(2)}) collective-permute-start(bf16[24,3200]{1,0:T(8,128)(2,1)S(1)} %collective-permute-done.61.refs_3_), channel_id=1, source_target_pairs={{0,4},{4,0},{8,12},{12,8},{16,20},{20,16},{24,28},{28,24},{1,5},{5... | collective-permute-start | bytes 460808 | tf_op jit(solution)/shard_map/ppermute | solution.py:49
  203.8 5.2 %collective-permute-start.64 = (bf16[24,3200]{1,0:T(8,128)(2,1)S(1)}, bf16[24,3200]{1,0:T(8,128)(2,1)S(1)}, u32[]{:S(2)}, u32[]{:S(2)}) collective-permute-start(bf16[24,3200]{1,0:T(8,128)(2,1)S(1)} %collective-permute-done.63.refs_5_), channel_id=1, source_target_pairs={{0,4},{4,0},{8,12},{12,8},{16,20},{20,16},{24,28},{28,24},{1,5},{5... | collective-permute-start | bytes 460808 | tf_op jit(solution)/shard_map/ppermute | solution.py:49
  204.3 6.3 %collective-permute-start.66 = (bf16[24,3200]{1,0:T(8,128)(2,1)S(1)}, bf16[24,3200]{1,0:T(8,128)(2,1)S(1)}, u32[]{:S(2)}, u32[]{:S(2)}) collective-permute-start(bf16[24,3200]{1,0:T(8,128)(2,1)S(1)} %collective-permute-done.65.refs_7_), channel_id=1, source_target_pairs={{0,4},{4,0},{8,12},{12,8},{16,20},{20,16},{24,28},{28,24},{1,5},{5... | collective-permute-start | bytes 460808 | tf_op jit(solution)/shard_map/ppermute | solution.py:49
  (14 other events, 88.2 us)

commit v4 on v3

--- a/solution.py
+++ b/solution.py
@@ -88,7 +88,7 @@
     return [out[s] for s in range(8)]
 
 
-def sum_e(parts):
+def sum_e(parts, early=False):
     count = lax.axis_size(E)
     if count > 8:
         me = lax.axis_index(E)
@@ -99,6 +99,11 @@
     for s in (4, 6, 2):
         part = (parts[s].astype(wide) + got[s].astype(wide)).astype(low)
         terms.append(swap(part, E, s))
+    if early:
+        (first,) = call(
+            partial_kernel, [(parts[0].shape, wide)], [], jnp.zeros((1,), jnp.int32), parts[0], terms[2], cover=20
+        )
+        terms = [first, terms[1], *terms[3:]]
     return terms
 
 
@@ -112,6 +117,10 @@
     for ref in refs[1:]:
         out = out + (ref[...] if len(ref.shape) == rank else ref[1]).astype(wide)
     return out
+
+
+def partial_kernel(me_ref, *refs):
+    refs[-1][...] = total_of(refs[:-1])
 
 
 def store_w(outs, held, me):
@@ -519,7 +528,7 @@
 
 
 def join_kernel(me_ref, *refs):
-    terms, outs, output_ref, held = refs[:5], refs[5 : 5 + SHARDS], refs[5 + SHARDS], refs[6 + SHARDS]
+    terms, outs, (output_ref, held) = refs[: -SHARDS - 2], refs[-SHARDS - 2 : -2], refs[-2:]
     total = total_of(terms)
     columns = outs[0].shape[1]
     held[...] = total[:, :, :columns]
@@ -831,7 +840,7 @@
     grads = list(outs[3:])
     (layer_out,) = call(layer_kernel, [(row, low)], [], me, resid, *mixed_terms, after=(grads[-1],))
     if quick:
-        grads[5] = tie(grads[5], *mixed_terms[1:])
+        grads[3] = tie(grads[3], *mixed_terms[1:])
     back_terms, _ = sum_w(*outs[:3])
     (tokens_grad,) = call(
         tokens_back_kernel,
@@ -845,7 +854,7 @@
     )
 
     if quick:
-        terms = sum_e(grads)
+        terms = sum_e(grads, early=True)
         *grads, output_grad = call(
             join_kernel,
             [((piece, columns), low)] * SHARDS + [((piece, width), low)],

time: 213 us -> 210 us (0.986)
    pallas_call x23 -> x24, Pallas kernels: 51.1 us -> 51.1 us  [call(): pl.pallas_call(lambda *refs: kernel(*refs[skip:]), out_shape=tuple((jax.S...]
where the time goes in v4:
time: 210 us
  starting transfers between devices  82.5 us (39%)
  waiting for transfers between devices  70 us (33%)
  Pallas kernels  51.1 us (24%)
  local copies, waits for them, and re-layouts  3.26 us (2%)
    ppermute x67, starting transfers between devices, swap(): return lax.ppermute(value, axis, [(i, i ^ step) for i in range(count)])  82.5 us
    ppermute x67, waiting for transfers between devices, swap(): return lax.ppermute(value, axis, [(i, i ^ step) for i in range(count)])  70 us
    pallas_call x24, Pallas kernels, call(): pl.pallas_call(lambda *refs: kernel(*refs[skip:]), out_shape=tuple((jax.S...  51.1 us
  transfers between devices with their start and end apart: 67, of which 32 were waited for; matrix products, arithmetic and copies ran while one was open for 1% of the time, Pallas kernels for 21%

profile of v4, /device:TPU:0, one launch (start us, length us, event | category | flops | bytes accessed | tf_op | source)
XLA Modules:
  0.0 209.7 jit_solution(14792095817245162538)
XLA Ops:
  0.6 3.0 %collective-permute-start.1 = (bf16[128,768]{1,0:T(8,128)(2,1)}, bf16[128,768]{1,0:T(8,128)(2,1)S(1)}, u32[]{:S(2)}, u32[]{:S(2)}) collective-permute-start(bf16[128,768]{1,0:T(8,128)(2,1)} %refs_1_.11), channel_id=1, source_target_pairs={{0,2},{1,3},{2,0},{3,1},{4,6},{5,7},{6,4},{7,5},{8,10},{9,11},{10,... | collective-permute-start | bytes 589832 | tf_op jit(solution)/shard_map/ppermute | solution.py:49
  4.9 2.4 %shard_map.238 = (bf16[224,576]{1,0:T(8,128)(2,1)}, bf16[224,576]{1,0:T(8,128)(2,1)}, bf16[224,576]{1,0:T(8,128)(2,1)}, bf16[224,576]{1,0:T(8,128)(2,1)}) custom-call(s32[3]{0:T(128)} %pad_add_fusion.refs_0_.refs_1_.refs_2_, bf16[192,768]{1,0:T(8,128)(2,1)} %refs_1_.6, bf16[192,768]{1,0:T(8,128)(2,1)} %refs_2_.2, bf16[192,768]{1,0:T(8,128)(2,1)} %refs_3_.1, ...), custom_call_target="tpu_custom_call" | custom-call | flops 1 | bytes 1 | tf_op jit(solution)/shard_map/pallas_call | solution.py:141
  7.3 1.8 collective-permute-start.5
  9.7 1.6 shard_map.240.refs_3_.refs_2_
  11.4 1.6 collective-permute-start.6
  12.9 2.6 %collective-permute-start.7 = (bf16[144,768]{1,0:T(8,128)(2,1)}, bf16[144,768]{1,0:T(8,128)(2,1)S(1)}, u32[]{:S(2)}, u32[]{:S(2)}) collective-permute-start(bf16[144,768]{1,0:T(8,128)(2,1)} %shard_map.240.refs_3_.refs_2_), channel_id=1, source_target_pairs={{0,16},{4,20},{8,24},{12,28},{16,0},{20,4},{24,8},{28,12},{1,17},{... | collective-permute-start | bytes 663560 | tf_op jit(solution)/shard_map/ppermute | solution.py:49
  15.5 1.7 collective-permute-done.4.refs_7_
  17.2 3.6 %collective-permute-start.8 = (bf16[144,768]{1,0:T(8,128)(2,1)}, bf16[144,768]{1,0:T(8,128)(2,1)S(1)}, u32[]{:S(2)}, u32[]{:S(2)}) collective-permute-start(bf16[144,768]{1,0:T(8,128)(2,1)} %shard_map.240.refs_3_.refs_2_), channel_id=1, source_target_pairs={{0,24},{4,28},{8,16},{12,20},{16,8},{20,12},{24,0},{28,4},{1,25},{... | collective-permute-start | bytes 663560 | tf_op jit(solution)/shard_map/ppermute | solution.py:49
  20.8 1.8 collective-permute-done.5.refs_8_
  25.8 5.3 %shard_map.239 = (bf16[4,128,768]{2,1,0:T(8,128)(2,1)S(1)}, bf16[512,768]{1,0:T(8,128)(2,1)S(1)}, bf16[512,576]{1,0:T(8,128)(2,1)S(1)}, bf16[3,512,512]{2,1,0:T(...) custom-call(s32[3]{0:T(128)S(1)} %copy-done.7, ...), custom_call_target="tpu_custom_call" | custom-call | flops 20000000000 | bytes 1 | tf_op jit(solution)/shard_map/pallas_call | solution.py:141
  32.9 1.6 collective-permute-start.11
  35.6 6.2 %collective-permute-done.10.refs_5_ = bf16[128,768]{1,0:T(8,128)(2,1)S(1)} collective-permute-done((bf16[128,768]{1,0:T(8,128)(2,1)S(1)}, bf16[128,768]{1,0:T(8,128)(2,1)S(1)}, u32[]{:S(2)}, u32[]{:S(2)}) %collective-permute-start.10) | collective-permute-done | bytes 196640 | tf_op jit(solution)/shard_map/ppermute | solution.py:49
  42.5 4.4 %collective-permute-start.19 = (bf16[128,768]{1,0:T(8,128)(2,1)S(1)}, bf16[128,768]{1,0:T(8,128)(2,1)S(1)}, u32[]{:S(2)}, u32[]{:S(2)}) collective-permute-start(bf16[128,768]{1,0:T(8,128)(2,1)S(1)} %get-tuple-element.116.refs_0_.refs_4_), channel_id=1, source_target_pairs={{0,8},{4,12},{8,0},{12,4},{16,24},{20,28},{24,16},{28,20},{1,9},{5... | collective-permute-start | bytes 589832 | tf_op jit(solution)/shard_map/ppermute | solution.py:49
  48.0 1.4 collective-permute-start.23
  49.4 1.5 collective-permute-start.18
  50.9 4.6 %collective-permute-done.11.refs_6_ = bf16[4,144,768]{2,1,0:T(8,128)(2,1)S(1)} collective-permute-done((bf16[4,144,768]{2,1,0:T(8,128)(2,1)S(1)}, bf16[4,144,768]{2,1,0:T(8,128)(2,1)S(1)}, u32[]{:S(2)}, u32[]{:S(2)}) %collective-permute-start.11) | collective-permute-done | bytes 884768 | tf_op jit(solution)/shard_map/ppermute | solution.py:49
  55.5 1.8 shard_map.243
  58.2 1.5 collective-permute-start.20
  59.7 4.4 %collective-permute-done.21.refs_8_ = bf16[128,768]{1,0:T(8,128)(2,1)S(1)} collective-permute-done((bf16[128,768]{1,0:T(8,128)(2,1)S(1)}, bf16[128,768]{1,0:T(8,128)(2,1)S(1)}, u32[]{:S(2)}, u32[]{:S(2)}) %collective-permute-start.21) | collective-permute-done | bytes 196640 | tf_op jit(solution)/shard_map/ppermute | solution.py:49
  64.1 1.5 collective-permute-start.22
  67.1 3.1 %collective-permute-done.22.refs_9_ = bf16[128,768]{1,0:T(8,128)(2,1)S(1)} collective-permute-done((bf16[128,768]{1,0:T(8,128)(2,1)S(1)}, bf16[128,768]{1,0:T(8,128)(2,1)S(1)}, u32[]{:S(2)}, u32[]{:S(2)}) %collective-permute-start.22) | collective-permute-done | bytes 196640 | tf_op jit(solution)/shard_map/ppermute | solution.py:49
  70.2 2.1 %collective-permute-done.24.refs_11_ = bf16[128,768]{1,0:T(8,128)(2,1)S(1)} collective-permute-done((bf16[128,768]{1,0:T(8,128)(2,1)S(1)}, bf16[128,768]{1,0:T(8,128)(2,1)S(1)}, u32[]{:S(2)}, u32[]{:S(2)}) %collective-permute-start.24) | collective-permute-done | bytes 196640 | tf_op jit(solution)/shard_map/ppermute | solution.py:49
  72.3 1.5 shard_map.245.refs_7_.refs_9_.refs_8_
  77.3 3.7 %shard_map.244 = (f32[256,768]{1,0:T(8,128)S(1)}, f32[256,768]{1,0:T(8,128)S(1)}, f32[256,768]{1,0:T(8,128)S(1)}, f32[256,768]{1,0:T(8,128)S(1)}, f32[256,128]{1...) custom-call(s32[3]{0:T(128)S(1)} %copy-done.7, ...), custom_call_target="tpu_custom_call" | custom-call | flops 1 | bytes 1 | tf_op jit(solution)/shard_map/pallas_call | solution.py:141
  81.0 4.1 %shard_map.246 = (bf16[256,768]{1,0:T(8,128)(2,1)S(1)}, bf16[256,768]{1,0:T(8,128)(2,1)S(1)}, bf16[512,768]{1,0:T(8,128)(2,1)S(1)}, bf16[512,768]{1,0:T(8,128)(2,1)S(1)}, bf16[512,128]{1,0:T(8,128)(2,1)S(1)}) custom-call(s32[3]{0:T(128)S(1)} %copy-done.7, bf16[768,768]{1,0:T(8,128)(2,1)S(1)} %bitcast.17, ...), custom_call_target="tpu_custom_call" | custom-call | flops 1 | bytes 1 | tf_op jit(solution)/shard_map/pallas_call | solution.py:141
  85.5 2.3 %shard_map.248 = (bf16[256,768]{1,0:T(8,128)(2,1)S(1)}, bf16[256,768]{1,0:T(8,128)(2,1)S(1)}, bf16[256,768]{1,0:T(8,128)(2,1)S(1)}, bf16[256,128]{1,0:T(8,128)(2,1)S(1)}) custom-call(s32[3]{0:T(128)S(1)} %copy-done.7, bf16[768,768]{1,0:T(8,128)(2,1)S(1)} %bitcast.18, bf16[128,768]{1,0:T(8,128)(2,1)S(1)} %get-tuple-element.120.refs_2_.refs_3_, ...), custom_call_target="tpu_custom_call" | custom-call | flops 1 | bytes 1 | tf_op jit(solution)/shard_map/pallas_call | solution.py:141
  87.8 2.3 %shard_map.249 = (bf16[256,768]{1,0:T(8,128)(2,1)S(1)}, bf16[256,768]{1,0:T(8,128)(2,1)S(1)}, bf16[256,768]{1,0:T(8,128)(2,1)S(1)}, bf16[256,128]{1,0:T(8,128)(2,1)S(1)}) custom-call(bf16[256,128]{1,0:T(8,128)(2,1)S(1)} %get-tuple-element.131.refs_0_.refs_7_, s32[3]{0:T(128)S(1)} %copy-done.8, bf16[768,768]{1,0:T(8,128)(2,1)S(1)} %bitcast.19, ...), custom_call_target="tpu_custom_call" | custom-call | flops 1 | bytes 1 | tf_op jit(solution)/shard_map/pallas_call | solution.py:141
  92.2 1.3 collective-permute-start.34
  93.5 2.4 %shard_map.250 = (bf16[256,768]{1,0:T(8,128)(2,1)S(1)}, bf16[256,768]{1,0:T(8,128)(2,1)S(1)}, bf16[256,768]{1,0:T(8,128)(2,1)S(1)}, bf16[256,768]{1,0:T(8,128)(2,1)S(1)}, f32[768,128]{1,0:T(8,128)S(1)}) custom-call(bf16[256,768]{1,0:T(8,128)(2,1)S(1)} %add_convert_fusion.1.refs_0_, s32[3]{0:T(128)S(1)} %copy-done.8, bf16[768,768]{1,0:T(8,128)(2,1)S(1)} %bitcast.21, ...), custom_call_target="tpu_custom_call" | custom-call | flops 1 | bytes 1 | tf_op jit(solution)/shard_map/pallas_call | solution.py:141
  96.4 4.9 %shard_map.253 = (f32[1,768,768]{2,1,0:T(8,128)}, f32[1,768,768]{2,1,0:T(8,128)}, f32[8,128]{1,0:T(8,128)S(1)}) custom-call(bf16[256,768]{1,0:T(8,128)(2,1)S(1)} %get-tuple-element.140.refs_1_.refs_0_, s32[3]{0:T(128)S(1)} %copy-done.8, bf16[512,768]{1,0:T(8,128)(2,1)S(1)} %get-tuple-element.135.refs_3_.refs_2_, ...), custom_call_target="tpu_custom_call" | custom-call | flops 1 | bytes 1 | tf_op jit(solution)/shard_map/pallas_call | solution.py:141
  101.3 2.3 %collective-permute-done.34.refs_6_ = bf16[256,768]{1,0:T(8,128)(2,1)S(1)} collective-permute-done((bf16[256,768]{1,0:T(8,128)(2,1)S(1)}, bf16[256,768]{1,0:T(8,128)(2,1)S(1)}, u32[]{:S(2)}, u32[]{:S(2)}) %collective-permute-start.34) | collective-permute-done | bytes 393248 | tf_op jit(solution)/shard_map/ppermute | solution.py:49
  104.9 1.6 collective-permute-start.35
  108.4 1.5 collective-permute-start.40
  109.9 2.9 %collective-permute-done.35.refs_1_ = bf16[128,768]{1,0:T(8,128)(2,1)S(1)} collective-permute-done((bf16[128,768]{1,0:T(8,128)(2,1)S(1)}, bf16[128,768]{1,0:T(8,128)(2,1)S(1)}, u32[]{:S(2)}, u32[]{:S(2)}) %collective-permute-start.35) | collective-permute-done | bytes 196640 | tf_op jit(solution)/shard_map/ppermute | solution.py:49
  112.8 1.5 collective-permute-start.36
  114.3 2.6 %collective-permute-done.38 = bf16[128,768]{1,0:T(8,128)(2,1)S(1)} collective-permute-done((bf16[128,768]{1,0:T(8,128)(2,1)S(1)}, bf16[128,768]{1,0:T(8,128)(2,1)S(1)}, u32[]{:S(2)}, u32[]{:S(2)}) %collective-permute-start.38) | collective-permute-done | bytes 196640 | tf_op jit(solution)/shard_map/ppermute | solution.py:49
  117.0 5.6 %collective-permute-start.37 = (bf16[128,768]{1,0:T(8,128)(2,1)S(1)}, bf16[128,768]{1,0:T(8,128)(2,1)S(1)}, u32[]{:S(2)}, u32[]{:S(2)}) collective-permute-start(bf16[128,768]{1,0:T(8,128)(2,1)S(1)} %add_convert_fusion.4), channel_id=1, source_target_pairs={{0,16},{4,20},{8,24},{12,28},{16,0},{20,4},{24,8},{28,12},{1,17},{... | collective-permute-start | bytes 589832 | tf_op jit(solution)/shard_map/ppermute | solution.py:49
  122.7 1.4 collective-permute-start.39
  124.8 1.6 collective-permute-start.32
  126.5 6.1 %collective-permute-done.32.refs_4_ = bf16[256,768]{1,0:T(8,128)(2,1)S(1)} collective-permute-done((bf16[256,768]{1,0:T(8,128)(2,1)S(1)}, bf16[256,768]{1,0:T(8,128)(2,1)S(1)}, u32[]{:S(2)}, u32[]{:S(2)}) %collective-permute-start.32) | collective-permute-done | bytes 393248 | tf_op jit(solution)/shard_map/ppermute | solution.py:49
  138.3 3.8 %collective-permute-start.45 = (bf16[128,768]{1,0:T(8,128)(2,1)S(1)}, bf16[128,768]{1,0:T(8,128)(2,1)S(1)}, u32[]{:S(2)}, u32[]{:S(2)}) collective-permute-start(bf16[128,768]{1,0:T(8,128)(2,1)S(1)} %get-tuple-element.163), channel_id=1, source_target_pairs={{0,16},{4,20},{8,24},{12,28},{16,0},{20,4},{24,8},{28,12},{1,17},{... | collective-permute-start | bytes 589832 | tf_op jit(solution)/shard_map/ppermute | solution.py:49
  142.0 1.4 collective-permute-start.46
  144.2 3.3 %collective-permute-done.44.refs_13_ = bf16[128,768]{1,0:T(8,128)(2,1)S(1)} collective-permute-done((bf16[128,768]{1,0:T(8,128)(2,1)S(1)}, bf16[128,768]{1,0:T(8,128)(2,1)S(1)}, u32[]{:S(2)}, u32[]{:S(2)}) %collective-permute-start.44) | collective-permute-done | bytes 196640 | tf_op jit(solution)/shard_map/ppermute | solution.py:49
  147.5 6.6 %shard_map.257 = (bf16[128,768]{1,0:T(8,128)(2,1)S(1)}, bf16[128,768]{1,0:T(8,128)(2,1)S(1)}, bf16[2,128,768]{2,1,0:T(8,128)(2,1)S(1)}, bf16[4,24,896]{2,1,0:T(8...) custom-call(s32[3]{0:T(128)S(1)} %copy-done.8, ...), custom_call_target="tpu_custom_call" | custom-call | flops 20000000000 | bytes 1 | tf_op jit(solution)/shard_map/pallas_call | solution.py:141
  154.0 1.5 collective-permute-start.50
  156.3 1.5 collective-permute-start.53
  158.8 2.5 %collective-permute-done.50.refs_1_ = bf16[4,24,896]{2,1,0:T(8,128)(2,1)S(1)} collective-permute-done((bf16[4,24,896]{2,1,0:T(8,128)(2,1)S(1)}, bf16[4,24,896]{2,1,0:T(8,128)(2,1)S(1)}, u32[]{:S(2)}, u32[]{:S(2)}) %collective-permute-start.50) | collective-permute-done | bytes 172064 | tf_op jit(solution)/shard_map/ppermute | solution.py:49
  161.3 3.9 %collective-permute-start.51 = (bf16[4,24,896]{2,1,0:T(8,128)(2,1)S(1)}, bf16[4,24,896]{2,1,0:T(8,128)(2,1)S(1)}, u32[]{:S(2)}, u32[]{:S(2)}) collective-permute-start(bf16[4,24,896]{2,1,0:T(8,128)(2,1)S(1)} %add_convert_fusion.7), channel_id=1, source_target_pairs={{0,16},{4,20},{8,24},{12,28},{16,0},{20,4},{24,8},{28,12},{1,17},{... | collective-permute-start | bytes 516104 | tf_op jit(solution)/shard_map/ppermute | solution.py:49
  165.2 1.5 collective-permute-start.52
  166.8 1.4 collective-permute-start.54
  168.7 2.9 %collective-permute-start.56 = (bf16[4,24,896]{2,1,0:T(8,128)(2,1)S(1)}, bf16[4,24,896]{2,1,0:T(8,128)(2,1)S(1)}, u32[]{:S(2)}, u32[]{:S(2)}) collective-permute-start(bf16[4,24,896]{2,1,0:T(8,128)(2,1)S(1)} %add_convert_fusion.5), channel_id=1, source_target_pairs={{0,8},{4,12},{8,0},{12,4},{16,24},{20,28},{24,16},{28,20},{1,9},{5... | collective-permute-start | bytes 516104 | tf_op jit(solution)/shard_map/ppermute | solution.py:49
  171.6 5.6 %collective-permute-done.51.refs_2_ = bf16[4,24,896]{2,1,0:T(8,128)(2,1)S(1)} collective-permute-done((bf16[4,24,896]{2,1,0:T(8,128)(2,1)S(1)}, bf16[4,24,896]{2,1,0:T(8,128)(2,1)S(1)}, u32[]{:S(2)}, u32[]{:S(2)}) %collective-permute-start.51) | collective-permute-done | bytes 172064 | tf_op jit(solution)/shard_map/ppermute | solution.py:49
  177.3 2.3 %collective-permute-done.56.refs_4_ = bf16[4,24,896]{2,1,0:T(8,128)(2,1)S(1)} collective-permute-done((bf16[4,24,896]{2,1,0:T(8,128)(2,1)S(1)}, bf16[4,24,896]{2,1,0:T(8,128)(2,1)S(1)}, u32[]{:S(2)}, u32[]{:S(2)}) %collective-permute-start.56) | collective-permute-done | bytes 172064 | tf_op jit(solution)/shard_map/ppermute | solution.py:49
  182.2 2.2 %collective-permute-done.58.refs_3_ = bf16[24,704]{1,0:T(8,128)(2,1)S(1)} collective-permute-done((bf16[24,704]{1,0:T(8,128)(2,1)S(1)}, bf16[24,704]{1,0:T(8,128)(2,1)S(1)}, u32[]{:S(2)}, u32[]{:S(2)}) %collective-permute-start.58) | collective-permute-done | bytes 33824 | tf_op jit(solution)/shard_map/ppermute | solution.py:49
  186.2 1.9 collective-permute-start.63
  188.1 1.9 collective-permute-start.65
  191.2 1.5 collective-permute-start.60
  192.7 1.4 collective-permute-done.61.refs_3_
  195.3 5.3 %collective-permute-done.63.refs_5_ = bf16[24,3200]{1,0:T(8,128)(2,1)S(1)} collective-permute-done((bf16[24,3200]{1,0:T(8,128)(2,1)S(1)}, bf16[24,3200]{1,0:T(8,128)(2,1)S(1)}, u32[]{:S(2)}, u32[]{:S(2)}) %collective-permute-start.63) | collective-permute-done | bytes 153632 | tf_op jit(solution)/shard_map/ppermute | solution.py:49
  200.6 1.5 collective-permute-start.64
  202.6 1.3 shard_map.258
  204.0 1.5 shard_map.259
  205.9 1.6 collective-permute-done.66.refs_8_
  207.6 2.1 %shard_map.265 = (f32[192,768]{1,0:T(8,128)}, f32[192,768]{1,0:T(8,128)}, f32[192,768]{1,0:T(8,128)}, f32[192,768]{1,0:T(8,128)}, f32[192]{0:T(256)}, /*index=5*...) custom-call(s32[3]{0:T(128)S(1)} %copy-done.8, bf16[24,3200]{1,0:T(8,128)(2,1)S(1)} %shard_map.264.refs_1_, ...), custom_call_target="tpu_custom_call" | custom-call | flops 1 | bytes 1 | tf_op jit(solution)/shard_map/pallas_call | solution.py:141
  (131 shorter events, 38.2 us)
Async XLA Ops:
  0.6 8.8 %collective-permute-start.1 = (bf16[128,768]{1,0:T(8,128)(2,1)}, bf16[128,768]{1,0:T(8,128)(2,1)S(1)}, u32[]{:S(2)}, u32[]{:S(2)}) collective-permute-start(bf16[128,768]{1,0:T(8,128)(2,1)} %refs_1_.11), channel_id=1, source_target_pairs={{0,2},{1,3},{2,0},{3,1},{4,6},{5,7},{6,4},{7,5},{8,10},{9,11},{10,... | collective-permute-start | bytes 589832 | tf_op jit(solution)/shard_map/ppermute | solution.py:49
  7.3 5.6 %collective-permute-start.3 = (bf16[224,576]{1,0:T(8,128)(2,1)}, bf16[224,576]{1,0:T(8,128)(2,1)S(1)}, u32[]{:S(2)}, u32[]{:S(2)}) collective-permute-start(bf16[224,576]{1,0:T(8,128)(2,1)} %get-tuple-element.103), channel_id=1, source_target_pairs={{0,1},{1,0},{2,3},{3,2},{4,5},{5,4},{6,7},{7,6},{8,9},{9,8},{10,11... | collective-permute-start | bytes 774152 | tf_op jit(solution)/shard_map/ppermute | solution.py:49
  7.3 9.9 %collective-permute-start.4 = (bf16[224,576]{1,0:T(8,128)(2,1)}, bf16[224,576]{1,0:T(8,128)(2,1)S(1)}, u32[]{:S(2)}, u32[]{:S(2)}) collective-permute-start(bf16[224,576]{1,0:T(8,128)(2,1)} %get-tuple-element.104), channel_id=1, source_target_pairs={{0,2},{1,3},{2,0},{3,1},{4,6},{5,7},{6,4},{7,5},{8,10},{9,11},{10,... | collective-permute-start | bytes 774152 | tf_op jit(solution)/shard_map/ppermute | solution.py:49
  7.3 15.2 %collective-permute-start.5 = (bf16[224,576]{1,0:T(8,128)(2,1)}, bf16[224,576]{1,0:T(8,128)(2,1)S(1)}, u32[]{:S(2)}, u32[]{:S(2)}) collective-permute-start(bf16[224,576]{1,0:T(8,128)(2,1)} %get-tuple-element.105), channel_id=1, source_target_pairs={{0,3},{1,2},{2,1},{3,0},{4,7},{5,6},{6,5},{7,4},{8,11},{9,10},{10,... | collective-permute-start | bytes 774152 | tf_op jit(solution)/shard_map/ppermute | solution.py:49
  9.2 2.2 %collective-permute-start = (bf16[128,768]{1,0:T(8,128)(2,1)}, bf16[128,768]{1,0:T(8,128)(2,1)S(1)}, u32[]{:S(2)}, u32[]{:S(2)}) collective-permute-start(bf16[128,768]{1,0:T(8,128)(2,1)} %refs_1_.11), channel_id=1, source_target_pairs={{0,1},{1,0},{2,3},{3,2},{4,5},{5,4},{6,7},{7,6},{8,9},{9,8},{10,11... | collective-permute-start | bytes 589832 | tf_op jit(solution)/shard_map/ppermute | solution.py:49
  9.5 13.1 %collective-permute-start.2 = (bf16[128,768]{1,0:T(8,128)(2,1)S(1)}, bf16[128,768]{1,0:T(8,128)(2,1)S(1)}, u32[]{:S(2)}, u32[]{:S(2)}) collective-permute-start(bf16[128,768]{1,0:T(8,128)(2,1)S(1)} %collective-permute-done.1.refs_3_), channel_id=1, source_target_pairs={{0,1},{1,0},{2,3},{3,2},{4,5},{5,4},{6,7},{7,6},{8,9},{9,8},{10,11... | collective-permute-start | bytes 589832 | tf_op jit(solution)/shard_map/ppermute | solution.py:49
  11.4 19.8 %collective-permute-start.6 = (bf16[144,768]{1,0:T(8,128)(2,1)}, bf16[144,768]{1,0:T(8,128)(2,1)S(1)}, u32[]{:S(2)}, u32[]{:S(2)}) collective-permute-start(bf16[144,768]{1,0:T(8,128)(2,1)} %shard_map.240.refs_3_.refs_2_), channel_id=1, source_target_pairs={{0,8},{4,12},{8,0},{12,4},{16,24},{20,28},{24,16},{28,20},{1,9},{5... | collective-permute-start | bytes 663560 | tf_op jit(solution)/shard_map/ppermute | solution.py:49
  12.9 18.9 %collective-permute-start.7 = (bf16[144,768]{1,0:T(8,128)(2,1)}, bf16[144,768]{1,0:T(8,128)(2,1)S(1)}, u32[]{:S(2)}, u32[]{:S(2)}) collective-permute-start(bf16[144,768]{1,0:T(8,128)(2,1)} %shard_map.240.refs_3_.refs_2_), channel_id=1, source_target_pairs={{0,16},{4,20},{8,24},{12,28},{16,0},{20,4},{24,8},{28,12},{1,17},{... | collective-permute-start | bytes 663560 | tf_op jit(solution)/shard_map/ppermute | solution.py:49
  17.2 14.7 %collective-permute-start.8 = (bf16[144,768]{1,0:T(8,128)(2,1)}, bf16[144,768]{1,0:T(8,128)(2,1)S(1)}, u32[]{:S(2)}, u32[]{:S(2)}) collective-permute-start(bf16[144,768]{1,0:T(8,128)(2,1)} %shard_map.240.refs_3_.refs_2_), channel_id=1, source_target_pairs={{0,24},{4,28},{8,16},{12,20},{16,8},{20,12},{24,0},{28,4},{1,25},{... | collective-permute-start | bytes 663560 | tf_op jit(solution)/shard_map/ppermute | solution.py:49
  32.9 22.5 %collective-permute-start.11 = (bf16[4,144,768]{2,1,0:T(8,128)(2,1)S(1)}, bf16[4,144,768]{2,1,0:T(8,128)(2,1)S(1)}, u32[]{:S(2)}, u32[]{:S(2)}) collective-permute-start(bf16[4,144,768]{2,1,0:T(8,128)(2,1)S(1)} %get-tuple-element.117), channel_id=1, source_target_pairs={{0,4},{4,0},{8,12},{12,8},{16,20},{20,16},{24,28},{28,24},{1,5},{5... | collective-permute-start | bytes 2654216 | tf_op jit(solution)/shard_map/ppermute | solution.py:49
  34.7 7.0 %collective-permute-start.10 = (bf16[128,768]{1,0:T(8,128)(2,1)S(1)}, bf16[128,768]{1,0:T(8,128)(2,1)S(1)}, u32[]{:S(2)}, u32[]{:S(2)}) collective-permute-start(bf16[128,768]{1,0:T(8,128)(2,1)S(1)} %fusion.1), channel_id=1, source_target_pairs={{0,2},{1,3},{2,0},{3,1},{4,6},{5,7},{6,4},{7,5},{8,10},{9,11},{10,... | collective-permute-start | bytes 589832 | tf_op jit(solution)/shard_map/ppermute | solution.py:49
  42.5 15.7 %collective-permute-start.19 = (bf16[128,768]{1,0:T(8,128)(2,1)S(1)}, bf16[128,768]{1,0:T(8,128)(2,1)S(1)}, u32[]{:S(2)}, u32[]{:S(2)}) collective-permute-start(bf16[128,768]{1,0:T(8,128)(2,1)S(1)} %get-tuple-element.116.refs_0_.refs_4_), channel_id=1, source_target_pairs={{0,8},{4,12},{8,0},{12,4},{16,24},{20,28},{24,16},{28,20},{1,9},{5... | collective-permute-start | bytes 589832 | tf_op jit(solution)/shard_map/ppermute | solution.py:49
  46.9 17.2 %collective-permute-start.21 = (bf16[128,768]{1,0:T(8,128)(2,1)S(1)}, bf16[128,768]{1,0:T(8,128)(2,1)S(1)}, u32[]{:S(2)}, u32[]{:S(2)}) collective-permute-start(bf16[128,768]{1,0:T(8,128)(2,1)S(1)} %get-tuple-element.116.refs_0_.refs_4_), channel_id=1, source_target_pairs={{0,16},{4,20},{8,24},{12,28},{16,0},{20,4},{24,8},{28,12},{1,17},{... | collective-permute-start | bytes 589832 | tf_op jit(solution)/shard_map/ppermute | solution.py:49
  48.0 17.6 %collective-permute-start.23 = (bf16[128,768]{1,0:T(8,128)(2,1)S(1)}, bf16[128,768]{1,0:T(8,128)(2,1)S(1)}, u32[]{:S(2)}, u32[]{:S(2)}) collective-permute-start(bf16[128,768]{1,0:T(8,128)(2,1)S(1)} %get-tuple-element.116.refs_0_.refs_4_), channel_id=1, source_target_pairs={{0,24},{4,28},{8,16},{12,20},{16,8},{20,12},{24,0},{28,4},{1,25},{... | collective-permute-start | bytes 589832 | tf_op jit(solution)/shard_map/ppermute | solution.py:49
  49.4 16.7 %collective-permute-start.18 = (bf16[128,768]{1,0:T(8,128)(2,1)S(1)}, bf16[128,768]{1,0:T(8,128)(2,1)S(1)}, u32[]{:S(2)}, u32[]{:S(2)}) collective-permute-start(bf16[128,768]{1,0:T(8,128)(2,1)S(1)} %get-tuple-element.116.refs_0_.refs_4_), channel_id=1, source_target_pairs={{0,4},{4,0},{8,12},{12,8},{16,20},{20,16},{24,28},{28,24},{1,5},{5... | collective-permute-start | bytes 589832 | tf_op jit(solution)/shard_map/ppermute | solution.py:49
  57.3 15.0 %collective-permute-start.15 = (bf16[144,768]{1,0:T(8,128)(2,1)S(1)}, bf16[144,768]{1,0:T(8,128)(2,1)S(1)}, u32[]{:S(2)}, u32[]{:S(2)}) collective-permute-start(bf16[144,768]{1,0:T(8,128)(2,1)S(1)} %get-tuple-element.122.refs_3_.refs_13_), channel_id=1, source_target_pairs={{0,2},{1,3},{2,0},{3,1},{4,6},{5,7},{6,4},{7,5},{8,10},{9,11},{10,... | collective-permute-start | bytes 663560 | tf_op jit(solution)/shard_map/ppermute | solution.py:49
  58.2 9.0 %collective-permute-start.20 = (bf16[128,768]{1,0:T(8,128)(2,1)S(1)}, bf16[128,768]{1,0:T(8,128)(2,1)S(1)}, u32[]{:S(2)}, u32[]{:S(2)}) collective-permute-start(bf16[128,768]{1,0:T(8,128)(2,1)S(1)} %collective-permute-done.19.refs_6_), channel_id=1, source_target_pairs={{0,4},{4,0},{8,12},{12,8},{16,20},{20,16},{24,28},{28,24},{1,5},{5... | collective-permute-start | bytes 589832 | tf_op jit(solution)/shard_map/ppermute | solution.py:49
  64.1 6.1 %collective-permute-start.22 = (bf16[128,768]{1,0:T(8,128)(2,1)S(1)}, bf16[128,768]{1,0:T(8,128)(2,1)S(1)}, u32[]{:S(2)}, u32[]{:S(2)}) collective-permute-start(bf16[128,768]{1,0:T(8,128)(2,1)S(1)} %collective-permute-done.21.refs_8_), channel_id=1, source_target_pairs={{0,4},{4,0},{8,12},{12,8},{16,20},{20,16},{24,28},{28,24},{1,5},{5... | collective-permute-start | bytes 589832 | tf_op jit(solution)/shard_map/ppermute | solution.py:49
  65.6 6.7 %collective-permute-start.24 = (bf16[128,768]{1,0:T(8,128)(2,1)S(1)}, bf16[128,768]{1,0:T(8,128)(2,1)S(1)}, u32[]{:S(2)}, u32[]{:S(2)}) collective-permute-start(bf16[128,768]{1,0:T(8,128)(2,1)S(1)} %collective-permute-done.23.refs_10_), channel_id=1, source_target_pairs={{0,4},{4,0},{8,12},{12,8},{16,20},{20,16},{24,28},{28,24},{1,5},{5... | collective-permute-start | bytes 589832 | tf_op jit(solution)/shard_map/ppermute | solution.py:49
  66.1 6.2 %collective-permute-start.14 = (bf16[128,768]{1,0:T(8,128)(2,1)S(1)}, bf16[128,768]{1,0:T(8,128)(2,1)S(1)}, u32[]{:S(2)}, u32[]{:S(2)}) collective-permute-start(bf16[128,768]{1,0:T(8,128)(2,1)S(1)} %get-tuple-element.121.refs_2_.refs_12_), channel_id=1, source_target_pairs={{0,2},{1,3},{2,0},{3,1},{4,6},{5,7},{6,4},{7,5},{8,10},{9,11},{10,... | collective-permute-start | bytes 589832 | tf_op jit(solution)/shard_map/ppermute | solution.py:49
  67.1 8.6 %collective-permute-start.12 = (bf16[128,768]{1,0:T(8,128)(2,1)S(1)}, bf16[128,768]{1,0:T(8,128)(2,1)S(1)}, u32[]{:S(2)}, u32[]{:S(2)}) collective-permute-start(bf16[128,768]{1,0:T(8,128)(2,1)S(1)} %get-tuple-element.121.refs_2_.refs_12_), channel_id=1, source_target_pairs={{0,1},{1,0},{2,3},{3,2},{4,5},{5,4},{6,7},{7,6},{8,9},{9,8},{10,11... | collective-permute-start | bytes 589832 | tf_op jit(solution)/shard_map/ppermute | solution.py:49
  73.8 7.2 %collective-permute-start.26 = (bf16[256,768]{1,0:T(8,128)(2,1)S(1)}, bf16[256,768]{1,0:T(8,128)(2,1)S(1)}, u32[]{:S(2)}, u32[]{:S(2)}) collective-permute-start(bf16[256,768]{1,0:T(8,128)(2,1)S(1)} %shard_map.245.refs_7_.refs_9_.refs_8_), channel_id=1, source_target_pairs={{0,1},{1,0},{2,3},{3,2},{4,5},{5,4},{6,7},{7,6},{8,9},{9,8},{10,11... | collective-permute-start | bytes 1179656 | tf_op jit(solution)/shard_map/ppermute | solution.py:49
  73.9 11.5 %collective-permute-start.25 = (bf16[256,768]{1,0:T(8,128)(2,1)S(1)}, bf16[256,768]{1,0:T(8,128)(2,1)S(1)}, u32[]{:S(2)}, u32[]{:S(2)}) collective-permute-start(bf16[256,768]{1,0:T(8,128)(2,1)S(1)} %shard_map.245.refs_7_.refs_9_.refs_8_), channel_id=1, source_target_pairs={{0,2},{1,3},{2,0},{3,1},{4,6},{5,7},{6,4},{7,5},{8,10},{9,11},{10,... | collective-permute-start | bytes 1179656 | tf_op jit(solution)/shard_map/ppermute | solution.py:49
  75.4 1.9 collective-permute-start.17
  85.5 2.4 %collective-permute-start.27 = (bf16[256,768]{1,0:T(8,128)(2,1)S(1)}, bf16[256,768]{1,0:T(8,128)(2,1)S(1)}, u32[]{:S(2)}, u32[]{:S(2)}) collective-permute-start(bf16[256,768]{1,0:T(8,128)(2,1)S(1)} %shard_map.247.refs_5_.refs_11_.refs_10_), channel_id=1, source_target_pairs={{0,1},{1,0},{2,3},{3,2},{4,5},{5,4},{6,7},{7,6},{8,9},{9,8},{10,11... | collective-permute-start | bytes 1179656 | tf_op jit(solution)/shard_map/ppermute | solution.py:49
  90.2 1.9 collective-permute-start.28
  90.7 10.6 %collective-permute-start.33 = (bf16[256,768]{1,0:T(8,128)(2,1)S(1)}, bf16[256,768]{1,0:T(8,128)(2,1)S(1)}, u32[]{:S(2)}, u32[]{:S(2)}) collective-permute-start(bf16[256,768]{1,0:T(8,128)(2,1)S(1)} %get-tuple-element.150), channel_id=1, source_target_pairs={{0,1},{1,0},{2,3},{3,2},{4,5},{5,4},{6,7},{7,6},{8,9},{9,8},{10,11... | collective-permute-start | bytes 1179656 | tf_op jit(solution)/shard_map/ppermute | solution.py:49
  92.2 11.5 %collective-permute-start.34 = (bf16[256,768]{1,0:T(8,128)(2,1)S(1)}, bf16[256,768]{1,0:T(8,128)(2,1)S(1)}, u32[]{:S(2)}, u32[]{:S(2)}) collective-permute-start(bf16[256,768]{1,0:T(8,128)(2,1)S(1)} %add_convert_fusion.1.refs_0_), channel_id=1, source_target_pairs={{0,2},{1,3},{2,0},{3,1},{4,6},{5,7},{6,4},{7,5},{8,10},{9,11},{10,... | collective-permute-start | bytes 1179656 | tf_op jit(solution)/shard_map/ppermute | solution.py:49
  95.9 10.6 %collective-permute-start.30 = (bf16[256,768]{1,0:T(8,128)(2,1)S(1)}, bf16[256,768]{1,0:T(8,128)(2,1)S(1)}, u32[]{:S(2)}, u32[]{:S(2)}) collective-permute-start(bf16[256,768]{1,0:T(8,128)(2,1)S(1)} %get-tuple-element.143), channel_id=1, source_target_pairs={{0,1},{1,0},{2,3},{3,2},{4,5},{5,4},{6,7},{7,6},{8,9},{9,8},{10,11... | collective-permute-start | bytes 1179656 | tf_op jit(solution)/shard_map/ppermute | solution.py:49
  96.0 26.6 %collective-permute-start.29 = (bf16[256,768]{1,0:T(8,128)(2,1)S(1)}, bf16[256,768]{1,0:T(8,128)(2,1)S(1)}, u32[]{:S(2)}, u32[]{:S(2)}) collective-permute-start(bf16[256,768]{1,0:T(8,128)(2,1)S(1)} %get-tuple-element.141), channel_id=1, source_target_pairs={{0,1},{1,0},{2,3},{3,2},{4,5},{5,4},{6,7},{7,6},{8,9},{9,8},{10,11... | collective-permute-start | bytes 1179656 | tf_op jit(solution)/shard_map/ppermute | solution.py:49
  104.9 7.9 %collective-permute-start.35 = (bf16[128,768]{1,0:T(8,128)(2,1)S(1)}, bf16[128,768]{1,0:T(8,128)(2,1)S(1)}, u32[]{:S(2)}, u32[]{:S(2)}) collective-permute-start(bf16[128,768]{1,0:T(8,128)(2,1)S(1)} %get-tuple-element.153), channel_id=1, source_target_pairs={{0,4},{4,0},{8,12},{12,8},{16,20},{20,16},{24,28},{28,24},{1,5},{5... | collective-permute-start | bytes 589832 | tf_op jit(solution)/shard_map/ppermute | solution.py:49
  106.6 17.5 %collective-permute-start.31 = (bf16[256,768]{1,0:T(8,128)(2,1)S(1)}, bf16[256,768]{1,0:T(8,128)(2,1)S(1)}, u32[]{:S(2)}, u32[]{:S(2)}) collective-permute-start(bf16[256,768]{1,0:T(8,128)(2,1)S(1)} %add_convert_fusion), channel_id=1, source_target_pairs={{0,2},{1,3},{2,0},{3,1},{4,6},{5,7},{6,4},{7,5},{8,10},{9,11},{10,... | collective-permute-start | bytes 1179656 | tf_op jit(solution)/shard_map/ppermute | solution.py:49
  107.9 9.1 %collective-permute-start.38 = (bf16[128,768]{1,0:T(8,128)(2,1)S(1)}, bf16[128,768]{1,0:T(8,128)(2,1)S(1)}, u32[]{:S(2)}, u32[]{:S(2)}) collective-permute-start(bf16[128,768]{1,0:T(8,128)(2,1)S(1)} %get-tuple-element.156), channel_id=1, source_target_pairs={{0,4},{4,0},{8,12},{12,8},{16,20},{20,16},{24,28},{28,24},{1,5},{5... | collective-permute-start | bytes 589832 | tf_op jit(solution)/shard_map/ppermute | solution.py:49
  108.4 18.0 %collective-permute-start.40 = (bf16[128,768]{1,0:T(8,128)(2,1)S(1)}, bf16[128,768]{1,0:T(8,128)(2,1)S(1)}, u32[]{:S(2)}, u32[]{:S(2)}) collective-permute-start(bf16[128,768]{1,0:T(8,128)(2,1)S(1)} %get-tuple-element.158), channel_id=1, source_target_pairs={{0,4},{4,0},{8,12},{12,8},{16,20},{20,16},{24,28},{28,24},{1,5},{5... | collective-permute-start | bytes 589832 | tf_op jit(solution)/shard_map/ppermute | solution.py:49
  112.8 21.0 %collective-permute-start.36 = (bf16[128,768]{1,0:T(8,128)(2,1)S(1)}, bf16[128,768]{1,0:T(8,128)(2,1)S(1)}, u32[]{:S(2)}, u32[]{:S(2)}) collective-permute-start(bf16[128,768]{1,0:T(8,128)(2,1)S(1)} %shard_map.255), channel_id=1, source_target_pairs={{0,4},{4,0},{8,12},{12,8},{16,20},{20,16},{24,28},{28,24},{1,5},{5... | collective-permute-start | bytes 589832 | tf_op jit(solution)/shard_map/ppermute | solution.py:49
  117.0 17.6 %collective-permute-start.37 = (bf16[128,768]{1,0:T(8,128)(2,1)S(1)}, bf16[128,768]{1,0:T(8,128)(2,1)S(1)}, u32[]{:S(2)}, u32[]{:S(2)}) collective-permute-start(bf16[128,768]{1,0:T(8,128)(2,1)S(1)} %add_convert_fusion.4), channel_id=1, source_target_pairs={{0,16},{4,20},{8,24},{12,28},{16,0},{20,4},{24,8},{28,12},{1,17},{... | collective-permute-start | bytes 589832 | tf_op jit(solution)/shard_map/ppermute | solution.py:49
  122.7 12.0 %collective-permute-start.39 = (bf16[128,768]{1,0:T(8,128)(2,1)S(1)}, bf16[128,768]{1,0:T(8,128)(2,1)S(1)}, u32[]{:S(2)}, u32[]{:S(2)}) collective-permute-start(bf16[128,768]{1,0:T(8,128)(2,1)S(1)} %add_convert_fusion.3), channel_id=1, source_target_pairs={{0,24},{4,28},{8,16},{12,20},{16,8},{20,12},{24,0},{28,4},{1,25},{... | collective-permute-start | bytes 589832 | tf_op jit(solution)/shard_map/ppermute | solution.py:49
  124.8 7.8 %collective-permute-start.32 = (bf16[256,768]{1,0:T(8,128)(2,1)S(1)}, bf16[256,768]{1,0:T(8,128)(2,1)S(1)}, u32[]{:S(2)}, u32[]{:S(2)}) collective-permute-start(bf16[256,768]{1,0:T(8,128)(2,1)S(1)} %shard_map.251.refs_3_), channel_id=1, source_target_pairs={{0,4},{4,0},{8,12},{12,8},{16,20},{20,16},{24,28},{28,24},{1,5},{5... | collective-permute-start | bytes 1179656 | tf_op jit(solution)/shard_map/ppermute | solution.py:49
  126.4 9.0 %collective-permute-start.41 = (bf16[128,768]{1,0:T(8,128)(2,1)S(1)}, bf16[128,768]{1,0:T(8,128)(2,1)S(1)}, u32[]{:S(2)}, u32[]{:S(2)}) collective-permute-start(bf16[128,768]{1,0:T(8,128)(2,1)S(1)} %add_convert_fusion.2), channel_id=1, source_target_pairs={{0,8},{4,12},{8,0},{12,4},{16,24},{20,28},{24,16},{28,20},{1,9},{5... | collective-permute-start | bytes 589832 | tf_op jit(solution)/shard_map/ppermute | solution.py:49
  136.3 7.1 %collective-permute-start.42 = (bf16[128,768]{1,0:T(8,128)(2,1)S(1)}, bf16[128,768]{1,0:T(8,128)(2,1)S(1)}, u32[]{:S(2)}, u32[]{:S(2)}) collective-permute-start(bf16[128,768]{1,0:T(8,128)(2,1)S(1)} %get-tuple-element.161.refs_10_), channel_id=1, source_target_pairs={{0,1},{1,0},{2,3},{3,2},{4,5},{5,4},{6,7},{7,6},{8,9},{9,8},{10,11... | collective-permute-start | bytes 589832 | tf_op jit(solution)/shard_map/ppermute | solution.py:49
  136.4 7.8 %collective-permute-start.43 = (bf16[128,768]{1,0:T(8,128)(2,1)S(1)}, bf16[128,768]{1,0:T(8,128)(2,1)S(1)}, u32[]{:S(2)}, u32[]{:S(2)}) collective-permute-start(bf16[128,768]{1,0:T(8,128)(2,1)S(1)} %get-tuple-element.161.refs_10_), channel_id=1, source_target_pairs={{0,2},{1,3},{2,0},{3,1},{4,6},{5,7},{6,4},{7,5},{8,10},{9,11},{10,... | collective-permute-start | bytes 589832 | tf_op jit(solution)/shard_map/ppermute | solution.py:49
  137.5 10.0 %collective-permute-start.44 = (bf16[128,768]{1,0:T(8,128)(2,1)S(1)}, bf16[128,768]{1,0:T(8,128)(2,1)S(1)}, u32[]{:S(2)}, u32[]{:S(2)}) collective-permute-start(bf16[128,768]{1,0:T(8,128)(2,1)S(1)} %get-tuple-element.161.refs_10_), channel_id=1, source_target_pairs={{0,3},{1,2},{2,1},{3,0},{4,7},{5,6},{6,5},{7,4},{8,11},{9,10},{10,... | collective-permute-start | bytes 589832 | tf_op jit(solution)/shard_map/ppermute | solution.py:49
  138.3 18.0 %collective-permute-start.45 = (bf16[128,768]{1,0:T(8,128)(2,1)S(1)}, bf16[128,768]{1,0:T(8,128)(2,1)S(1)}, u32[]{:S(2)}, u32[]{:S(2)}) collective-permute-start(bf16[128,768]{1,0:T(8,128)(2,1)S(1)} %get-tuple-element.163), channel_id=1, source_target_pairs={{0,16},{4,20},{8,24},{12,28},{16,0},{20,4},{24,8},{28,12},{1,17},{... | collective-permute-start | bytes 589832 | tf_op jit(solution)/shard_map/ppermute | solution.py:49
  142.0 15.7 %collective-permute-start.46 = (bf16[128,768]{1,0:T(8,128)(2,1)S(1)}, bf16[128,768]{1,0:T(8,128)(2,1)S(1)}, u32[]{:S(2)}, u32[]{:S(2)}) collective-permute-start(bf16[128,768]{1,0:T(8,128)(2,1)S(1)} %get-tuple-element.164), channel_id=1, source_target_pairs={{0,24},{4,28},{8,16},{12,20},{16,8},{20,12},{24,0},{28,4},{1,25},{... | collective-permute-start | bytes 589832 | tf_op jit(solution)/shard_map/ppermute | solution.py:49
  143.4 14.4 %collective-permute-start.47 = (bf16[128,768]{1,0:T(8,128)(2,1)S(1)}, bf16[128,768]{1,0:T(8,128)(2,1)S(1)}, u32[]{:S(2)}, u32[]{:S(2)}) collective-permute-start(bf16[128,768]{1,0:T(8,128)(2,1)S(1)} %get-tuple-element.165), channel_id=1, source_target_pairs={{0,8},{4,12},{8,0},{12,4},{16,24},{20,28},{24,16},{28,20},{1,9},{5... | collective-permute-start | bytes 589832 | tf_op jit(solution)/shard_map/ppermute | solution.py:49
  154.0 7.2 %collective-permute-start.50 = (bf16[4,24,896]{2,1,0:T(8,128)(2,1)S(1)}, bf16[4,24,896]{2,1,0:T(8,128)(2,1)S(1)}, u32[]{:S(2)}, u32[]{:S(2)}) collective-permute-start(bf16[4,24,896]{2,1,0:T(8,128)(2,1)S(1)} %get-tuple-element.172), channel_id=1, source_target_pairs={{0,4},{4,0},{8,12},{12,8},{16,20},{20,16},{24,28},{28,24},{1,5},{5... | collective-permute-start | bytes 516104 | tf_op jit(solution)/shard_map/ppermute | solution.py:49
  155.6 34.5 %collective-permute-start.48 = (bf16[2,128,768]{2,1,0:T(8,128)(2,1)S(1)}, bf16[2,128,768]{2,1,0:T(8,128)(2,1)S(1)}, u32[]{:S(2)}, u32[]{:S(2)}) collective-permute-start(bf16[2,128,768]{2,1,0:T(8,128)(2,1)S(1)} %get-tuple-element.168), channel_id=1, source_target_pairs={{0,1},{1,0},{2,3},{3,2},{4,5},{5,4},{6,7},{7,6},{8,9},{9,8},{10,11... | collective-permute-start | bytes 1179656 | tf_op jit(solution)/shard_map/ppermute | solution.py:49
  156.3 10.5 %collective-permute-start.53 = (bf16[4,24,896]{2,1,0:T(8,128)(2,1)S(1)}, bf16[4,24,896]{2,1,0:T(8,128)(2,1)S(1)}, u32[]{:S(2)}, u32[]{:S(2)}) collective-permute-start(bf16[4,24,896]{2,1,0:T(8,128)(2,1)S(1)} %get-tuple-element.162.refs_0_), channel_id=1, source_target_pairs={{0,4},{4,0},{8,12},{12,8},{16,20},{20,16},{24,28},{28,24},{1,5},{5... | collective-permute-start | bytes 516104 | tf_op jit(solution)/shard_map/ppermute | solution.py:49
  157.8 10.9 %collective-permute-start.55 = (bf16[4,24,896]{2,1,0:T(8,128)(2,1)S(1)}, bf16[4,24,896]{2,1,0:T(8,128)(2,1)S(1)}, u32[]{:S(2)}, u32[]{:S(2)}) collective-permute-start(bf16[4,24,896]{2,1,0:T(8,128)(2,1)S(1)} %shard_map.262), channel_id=1, source_target_pairs={{0,4},{4,0},{8,12},{12,8},{16,20},{20,16},{24,28},{28,24},{1,5},{5... | collective-permute-start | bytes 516104 | tf_op jit(solution)/shard_map/ppermute | solution.py:49
  161.3 15.9 %collective-permute-start.51 = (bf16[4,24,896]{2,1,0:T(8,128)(2,1)S(1)}, bf16[4,24,896]{2,1,0:T(8,128)(2,1)S(1)}, u32[]{:S(2)}, u32[]{:S(2)}) collective-permute-start(bf16[4,24,896]{2,1,0:T(8,128)(2,1)S(1)} %add_convert_fusion.7), channel_id=1, source_target_pairs={{0,16},{4,20},{8,24},{12,28},{16,0},{20,4},{24,8},{28,12},{1,17},{... | collective-permute-start | bytes 516104 | tf_op jit(solution)/shard_map/ppermute | solution.py:49
  165.2 12.1 %collective-permute-start.52 = (bf16[4,24,896]{2,1,0:T(8,128)(2,1)S(1)}, bf16[4,24,896]{2,1,0:T(8,128)(2,1)S(1)}, u32[]{:S(2)}, u32[]{:S(2)}) collective-permute-start(bf16[4,24,896]{2,1,0:T(8,128)(2,1)S(1)} %shard_map.261), channel_id=1, source_target_pairs={{0,4},{4,0},{8,12},{12,8},{16,20},{20,16},{24,28},{28,24},{1,5},{5... | collective-permute-start | bytes 516104 | tf_op jit(solution)/shard_map/ppermute | solution.py:49
  166.8 10.5 %collective-permute-start.54 = (bf16[4,24,896]{2,1,0:T(8,128)(2,1)S(1)}, bf16[4,24,896]{2,1,0:T(8,128)(2,1)S(1)}, u32[]{:S(2)}, u32[]{:S(2)}) collective-permute-start(bf16[4,24,896]{2,1,0:T(8,128)(2,1)S(1)} %add_convert_fusion.6), channel_id=1, source_target_pairs={{0,24},{4,28},{8,16},{12,20},{16,8},{20,12},{24,0},{28,4},{1,25},{... | collective-permute-start | bytes 516104 | tf_op jit(solution)/shard_map/ppermute | solution.py:49
  168.7 10.9 %collective-permute-start.56 = (bf16[4,24,896]{2,1,0:T(8,128)(2,1)S(1)}, bf16[4,24,896]{2,1,0:T(8,128)(2,1)S(1)}, u32[]{:S(2)}, u32[]{:S(2)}) collective-permute-start(bf16[4,24,896]{2,1,0:T(8,128)(2,1)S(1)} %add_convert_fusion.5), channel_id=1, source_target_pairs={{0,8},{4,12},{8,0},{12,4},{16,24},{20,28},{24,16},{28,20},{1,9},{5... | collective-permute-start | bytes 516104 | tf_op jit(solution)/shard_map/ppermute | solution.py:49
  180.3 1.9 collective-permute-start.57
  180.3 4.0 %collective-permute-start.58 = (bf16[24,704]{1,0:T(8,128)(2,1)S(1)}, bf16[24,704]{1,0:T(8,128)(2,1)S(1)}, u32[]{:S(2)}, u32[]{:S(2)}) collective-permute-start(bf16[24,704]{1,0:T(8,128)(2,1)S(1)} %get-tuple-element.179), channel_id=1, source_target_pairs={{0,2},{1,3},{2,0},{3,1},{4,6},{5,7},{6,4},{7,5},{8,10},{9,11},{10,... | collective-permute-start | bytes 101384 | tf_op jit(solution)/shard_map/ppermute | solution.py:49
  181.4 3.4 %collective-permute-start.59 = (bf16[24,704]{1,0:T(8,128)(2,1)S(1)}, bf16[24,704]{1,0:T(8,128)(2,1)S(1)}, u32[]{:S(2)}, u32[]{:S(2)}) collective-permute-start(bf16[24,704]{1,0:T(8,128)(2,1)S(1)} %get-tuple-element.180), channel_id=1, source_target_pairs={{0,3},{1,2},{2,1},{3,0},{4,7},{5,6},{6,5},{7,4},{8,11},{9,10},{10,... | collective-permute-start | bytes 101384 | tf_op jit(solution)/shard_map/ppermute | solution.py:49
  185.6 8.5 %collective-permute-start.61 = (bf16[24,3200]{1,0:T(8,128)(2,1)S(1)}, bf16[24,3200]{1,0:T(8,128)(2,1)S(1)}, u32[]{:S(2)}, u32[]{:S(2)}) collective-permute-start(bf16[24,3200]{1,0:T(8,128)(2,1)S(1)} %shard_map.264.refs_1_), channel_id=1, source_target_pairs={{0,8},{4,12},{8,0},{12,4},{16,24},{20,28},{24,16},{28,20},{1,9},{5... | collective-permute-start | bytes 460808 | tf_op jit(solution)/shard_map/ppermute | solution.py:49
  186.2 14.3 %collective-permute-start.63 = (bf16[24,3200]{1,0:T(8,128)(2,1)S(1)}, bf16[24,3200]{1,0:T(8,128)(2,1)S(1)}, u32[]{:S(2)}, u32[]{:S(2)}) collective-permute-start(bf16[24,3200]{1,0:T(8,128)(2,1)S(1)} %shard_map.264.refs_1_), channel_id=1, source_target_pairs={{0,16},{4,20},{8,24},{12,28},{16,0},{20,4},{24,8},{28,12},{1,17},{... | collective-permute-start | bytes 460808 | tf_op jit(solution)/shard_map/ppermute | solution.py:49
  188.1 14.0 %collective-permute-start.65 = (bf16[24,3200]{1,0:T(8,128)(2,1)S(1)}, bf16[24,3200]{1,0:T(8,128)(2,1)S(1)}, u32[]{:S(2)}, u32[]{:S(2)}) collective-permute-start(bf16[24,3200]{1,0:T(8,128)(2,1)S(1)} %shard_map.264.refs_1_), channel_id=1, source_target_pairs={{0,24},{4,28},{8,16},{12,20},{16,8},{20,12},{24,0},{28,4},{1,25},{... | collective-permute-start | bytes 460808 | tf_op jit(solution)/shard_map/ppermute | solution.py:49
  190.1 13.9 %collective-permute-start.49 = (bf16[128,768]{1,0:T(8,128)(2,1)S(1)}, bf16[128,768]{1,0:T(8,128)(2,1)S(1)}, u32[]{:S(2)}, u32[]{:S(2)}) collective-permute-start(bf16[128,768]{1,0:T(8,128)(2,1)S(1)} %fusion), channel_id=1, source_target_pairs={{0,2},{1,3},{2,0},{3,1},{4,6},{5,7},{6,4},{7,5},{8,10},{9,11},{10,... | collective-permute-start | bytes 589832 | tf_op jit(solution)/shard_map/ppermute | solution.py:49
  191.2 14.3 %collective-permute-start.60 = (bf16[24,3200]{1,0:T(8,128)(2,1)S(1)}, bf16[24,3200]{1,0:T(8,128)(2,1)S(1)}, u32[]{:S(2)}, u32[]{:S(2)}) collective-permute-start(bf16[24,3200]{1,0:T(8,128)(2,1)S(1)} %shard_map.264.refs_1_), channel_id=1, source_target_pairs={{0,4},{4,0},{8,12},{12,8},{16,20},{20,16},{24,28},{28,24},{1,5},{5... | collective-permute-start | bytes 460808 | tf_op jit(solution)/shard_map/ppermute | solution.py:49
  194.1 11.4 %collective-permute-start.62 = (bf16[24,3200]{1,0:T(8,128)(2,1)S(1)}, bf16[24,3200]{1,0:T(8,128)(2,1)S(1)}, u32[]{:S(2)}, u32[]{:S(2)}) collective-permute-start(bf16[24,3200]{1,0:T(8,128)(2,1)S(1)} %collective-permute-done.61.refs_3_), channel_id=1, source_target_pairs={{0,4},{4,0},{8,12},{12,8},{16,20},{20,16},{24,28},{28,24},{1,5},{5... | collective-permute-start | bytes 460808 | tf_op jit(solution)/shard_map/ppermute | solution.py:49
  200.6 5.3 %collective-permute-start.64 = (bf16[24,3200]{1,0:T(8,128)(2,1)S(1)}, bf16[24,3200]{1,0:T(8,128)(2,1)S(1)}, u32[]{:S(2)}, u32[]{:S(2)}) collective-permute-start(bf16[24,3200]{1,0:T(8,128)(2,1)S(1)} %collective-permute-done.63.refs_5_), channel_id=1, source_target_pairs={{0,4},{4,0},{8,12},{12,8},{16,20},{20,16},{24,28},{28,24},{1,5},{5... | collective-permute-start | bytes 460808 | tf_op jit(solution)/shard_map/ppermute | solution.py:49
  202.1 5.5 %collective-permute-start.66 = (bf16[24,3200]{1,0:T(8,128)(2,1)S(1)}, bf16[24,3200]{1,0:T(8,128)(2,1)S(1)}, u32[]{:S(2)}, u32[]{:S(2)}) collective-permute-start(bf16[24,3200]{1,0:T(8,128)(2,1)S(1)} %collective-permute-done.65.refs_7_), channel_id=1, source_target_pairs={{0,4},{4,0},{8,12},{12,8},{16,20},{20,16},{24,28},{28,24},{1,5},{5... | collective-permute-start | bytes 460808 | tf_op jit(solution)/shard_map/ppermute | solution.py:49
  (14 other events, 89.3 us)
